TPU v7x, 512 devices: a whole 4x8x8 slice. The times are simulated.
512 devices in a mesh: wide: 64 (over y, z_hi, x), narrow: 8 (over z_lo, core).
Axes of the slice: x: 4, y: 8, z: 8 (z_hi: 2, z_lo: 4; z = z_hi * 4 + z_lo), core: 2. Of those that a mesh axis runs over, the one named last changes fastest.
Arguments:
- eta_modes: float32 [2, 2048, 2048], P(None, 'wide', 'narrow'), may hold values from -6 to 6
- phi_modes: float32 [2, 2048, 2048], P(None, 'wide', 'narrow'), may hold values from -6 to 6
- zone_field: float32 [4096, 128], P('wide'), may hold values from -6 to 6
- offsets: int32 [64, 2], replicated, may hold values from 0 to 2047
Outputs:
- eta_next: float32 [2, 2048, 2048], P(None, 'wide', 'narrow')
- phi_next: float32 [2, 2048, 2048], P(None, 'wide', 'narrow')
Inputs may be any that keep to these rules, and one draw needn't show every extreme that they name: Row t of offsets gives the HOS grid cell (x, y) of zone tile t's first cell; tiles may intersect and wrap around the periodic grid.
All inputs are finite; a program needn't handle non-finite values.
Results may differ from a plain program's by a relative error of at most 0.00005.
Values sent between devices are 32-bit elements; how exact they have to be, the bound alone decides.
No kernel may reach another device: no remote copies, remote signals or barrier semaphores. Data moves between devices by JAX's collectives and lax.ppermute only.
A program may use at most 128 MiB of HBM per device.

v0:
```python
import functools
import math

import jax
import jax.numpy as jnp
import ml_dtypes
import numpy as np
from jax import lax
from jax.experimental import pallas as pl
from jax.experimental.pallas import tpu as pltpu
from jax.sharding import PartitionSpec as P

NX = 2048
NY = 2048
FINE = 4096
BOTH = ("wide", "narrow")
TURN_X = 2.0 * math.pi / NX
TURN_Y = 2.0 * math.pi / NY
time_step = 0.04
gravity = 9.81
spread = 1.0 / math.sqrt(NX * NY)
zone_scale = 1.0 / math.sqrt(4096 * 128)
f32 = jnp.float32
bf16 = jnp.bfloat16
VMEM_LIMIT = 56 * 1024 * 1024


def part(value, which):
    return np.where(which == 0, np.real(value), np.imag(value))


def angles(ints, period):
    return 2.0 * np.pi * (np.asarray(ints) % period) / period


def pair(matrix):
    high = matrix.astype(np.float32).astype(ml_dtypes.bfloat16)
    low = (matrix - high.astype(np.float64)).astype(np.float32).astype(ml_dtypes.bfloat16)
    return high, low


@functools.cache
def tables():
    out = {}
    row = np.arange(512)
    h, a, jj, slot = row // 256, row // 128 % 2, row // 32 % 4, row % 32
    f, i = slot // 4, slot % 4
    col = np.arange(320)
    cn, cf, ca, cj = col // 40, col // 8 % 5, col // 4 % 2, col % 4
    x0 = 4 * h + i
    turn = np.exp(1j * angles(x0[:, None] * cn[None, :], 8))
    turn = turn * np.where(cf < 4, 1j, 1.0)[None, :] * (1j ** ca)[None, :]
    same = (f[:, None] == cf[None, :]) & (jj[:, None] == cj[None, :])
    first = np.where(same, part(turn, a[:, None]), 0.0)
    second = np.where(same, part(1j * turn, a[:, None]), 0.0)
    out["rows"] = pair(np.concatenate([first, second], 0))
    k256 = np.arange(256)
    lanes_x0 = 4 * np.arange(2)[:, None] + np.arange(8)[None, :] % 4
    phase = angles(lanes_x0[:, :, None] * k256, NX)
    out["rows_turn"] = (np.cos(phase).astype(np.float32), np.sin(phase).astype(np.float32))
    phase = angles(k256[:, None] * k256[None, :], 256)
    out["x"] = pair(np.concatenate([np.cos(phase), np.sin(phase)], 1))
    k512 = np.arange(512)
    phase = angles(k512[:, None] * k512[None, :], 512)
    out["y"] = pair(np.concatenate([np.cos(phase), np.sin(phase)], 1))
    lane = np.arange(128)
    phase = angles(k512[:, None] * (lane // 32)[None, :], NY)
    out["y_turn"] = (np.cos(phase).astype(np.float32), np.sin(phase).astype(np.float32))
    phase = angles(k512[:, None] * (lane % 32 // 8)[None, :], NY)
    out["y_back"] = (np.cos(phase).astype(np.float32), np.sin(phase).astype(np.float32))
    ljj, lf, li = lane // 32, lane % 32 // 4, lane % 4
    gather = np.zeros((2, 128, 5, 128))
    for y0 in range(4):
        for k in range(128):
            if lf[k] < 5:
                value = np.round(np.exp(1j * angles(ljj[k] * y0, 4)) * 2) / 2
                gather[0, k, lf[k], y0 * 4 + li[k]] = value.real * spread
                gather[1, k, lf[k], y0 * 4 + li[k]] = -value.imag * spread
    out["gather"] = gather.reshape(256, 640).astype(ml_dtypes.bfloat16)
    deal = np.zeros((2, 128, 2, 128))
    for k in range(64):
        ka, kj, kf, ki = k // 32, k // 8 % 4, k // 4 % 2, k % 4
        for y0 in range(4):
            value = np.round(np.exp(-1j * angles(kj * y0, 4)) * 2) / 2
            deal[kf, y0 * 4 + ki, 0, k] = part(value, ka)
            deal[kf, y0 * 4 + ki, 1, k] = part(-1j * value, ka)
    out["deal"] = deal.reshape(256, 256).astype(ml_dtypes.bfloat16)
    row = np.arange(128)
    h, a, jj, f, i = row // 64, row // 32 % 2, row // 8 % 4, row // 4 % 2, row % 4
    x0 = 4 * h + i
    z0, za, zj = row // 8, row // 4 % 2, row % 4
    phase = np.concatenate([angles(x0[:, None] * k256, NX), angles(z0[:, None] * k256, FINE)], 0)
    out["back_turn"] = (np.cos(phase).astype(np.float32), np.sin(phase).astype(np.float32))
    on, of, oa, oj = row // 16, row // 8 % 2, row // 4 % 2, row % 4
    turn = np.exp(-1j * angles(on[:, None] * x0[None, :], 8)) * (1j ** a)[None, :]
    same = (of[:, None] == f[None, :]) & (oj[:, None] == jj[None, :])
    main = [np.where(same, part(turn * s, oa[:, None]), 0.0) for s in (1, -1j)]
    signed = np.where(on < 4, on, on - 8)
    turn = np.exp(-1j * angles(signed[:, None] * z0[None, :], 16)) * (1j ** za)[None, :]
    same = (of[:, None] == 0) & (oj[:, None] == zj[None, :])
    zone = [np.where(same, part(turn * s, oa[:, None]), 0.0) for s in (1, -1j)]
    out["back"] = pair(np.concatenate([main[0], zone[0], main[1], zone[1]], 1))
    return out


def split(value):
    high = value.astype(bf16)
    return high, (value - high.astype(f32)).astype(bf16)


def dot(left, right, dims=((1,), (0,))):
    return lax.dot_general(left, right, (dims, ((), ())), preferred_element_type=f32)


def dot3(left, right, dims=((1,), (0,))):
    return dot(left[0], right[0], dims) + (dot(left[0], right[1], dims) + dot(left[1], right[0], dims))


def iota(shape, dim):
    return lax.broadcasted_iota(jnp.int32, shape, dim)


def cos_of(phase):
    moved = phase + 512
    quarter = (moved >> 10) & 3
    angle = ((moved & 1023) - 512).astype(f32) * (2.0 * math.pi / FINE)
    square = angle * angle
    cosine = 1.0 + square * (-0.5 + square * (1.0 / 24 + square * (-1.0 / 720 + square * (1.0 / 40320))))
    sine = angle * (
        1.0 + square * (-1.0 / 6 + square * (1.0 / 120 + square * (-1.0 / 5040 + square * (1.0 / 362880))))
    )
    size = jnp.where((quarter & 1) == 0, cosine, sine)
    return jnp.where((quarter == 1) | (quarter == 2), -size, size)


def wave_of(index):
    return jnp.where(index < 1024, index, index - 2048).astype(f32)


def deal_kernel(eta, phi, out):
    for n in range(8):
        for source, base in ((eta, 0), (phi, 8)):
            for a in range(2):
                out[n, base + 4 * a : base + 4 * a + 4, :] = source[a, 4 * n : 4 * n + 4, :]


def source_kernel(place, offsets, zone, out):
    tile = place[0]
    own = place[1]
    ox = offsets[tile, 0]
    oy = offsets[tile, 1]
    lane = iota((128, 128), 1)
    wanted = (16 * own + (lane >> 3) - 2 * (ox & 7)) & 127
    pick = jnp.where(iota((128, 128), 0) == wanted, 1.0, 0.0).astype(bf16)
    high, low = split(zone[...] * zone_scale)
    cells = dot(high, pick) + dot(low, pick)
    lane = iota((64, 128), 1)
    phase = (lane & 3) * (2 * oy + iota((64, 128), 0)) + 1024 * ((lane >> 2) & 1)
    right = jnp.concatenate([cells * cos_of(phase), cells * cos_of(phase + 3072)], 0)
    lane = iota((512, 128), 1)
    m = iota((512, 128), 0)
    m = jnp.where(m < 256, m, m - 512)
    left = cos_of(4 * m * (2 * oy + (lane & 63)) + jnp.where(lane < 64, 0, 1024))
    out[...] = dot3(split(left), split(right))


def rows_kernel(place, modes, mix_high, mix_low, cos_turn, sin_turn, x_high, x_low, out):
    first_ky = 32 * place[0] + 4 * place[1]
    wave_y = wave_of(first_ky + (iota((8, 256), 0) & 3)) * TURN_Y
    tiles = []
    for n in range(8):
        wave_x = wave_of(256 * n + iota((8, 256), 1)) * TURN_X
        kappa = jnp.sqrt(wave_x * wave_x + wave_y * wave_y)
        eta = modes[n, 0:8, :]
        phi = modes[n, 8:16, :]
        tiles += [wave_x * eta, wave_y * eta, wave_x * phi, wave_y * phi, kappa * phi]
    rows = split(jnp.concatenate(tiles, 0))
    both = dot3((mix_high[...], mix_low[...]), rows)
    first = both[:512].reshape(2, 32, 8, 256)
    second = both[512:].reshape(2, 32, 8, 256)
    cosine = cos_turn[...][:, None]
    sine = sin_turn[...][:, None]
    turned = (first * cosine + second * sine).reshape(512, 256)
    quarter = (second * cosine - first * sine).reshape(512, 256)
    result = dot3(
        (x_high[...], x_low[...]), split(jnp.concatenate([turned, quarter], 1)), ((1,), (1,))
    )
    for g in range(4):
        out[pl.ds(g, 256, stride=4), :] = result[:, 128 * g : 128 * g + 128]


def columns_kernel(
    terms, source, y_high, y_low, cos_turn, sin_turn, gather, cos_back, sin_back, deal, out
):
    words = jnp.concatenate([terms[pl.ds(0, 512, stride=2), :], terms[pl.ds(1, 512, stride=2), :]], 1)
    high, low = split(words)
    with_cos = dot3((y_high[:, :512], y_low[:, :512]), (high, low))
    with_sin = dot3((y_high[:, 512:], y_low[:, 512:]), (high, low))
    real = with_cos[:, :128] - with_sin[:, 128:]
    imag = with_sin[:, :128] + with_cos[:, 128:]
    cosine = cos_turn[...]
    sine = sin_turn[...]
    high, low = split(
        jnp.concatenate([real * cosine - imag * sine, real * sine + imag * cosine], 1)
    )
    fields = dot(high, gather[...]) + dot(low, gather[...])
    slope_ex, slope_ey, slope_px, slope_py, lift = (
        fields[:, 128 * k : 128 * k + 128] for k in range(5)
    )
    first_order = lift * (slope_ex * slope_ex + slope_ey * slope_ey) - (
        slope_px * slope_ex + slope_py * slope_ey
    )
    second_term = 0.5 * (lift * lift - slope_px * slope_px - slope_py * slope_py)
    high, low = split(
        jnp.concatenate([first_order, second_term], 1) * (time_step * spread)
    )
    both = dot(high, deal[...]) + dot(low, deal[...])
    first = both[:, :128]
    second = both[:, 128:]
    cosine = cos_back[...]
    sine = sin_back[...]
    turned = jnp.concatenate([first * cosine + second * sine, second * cosine - first * sine], 0)
    out[pl.ds(0, 512, stride=2), :] = dot3((y_high[...], y_low[...]), split(turned))
    out[pl.ds(1, 512, stride=2), :] = source[...]


def rows_back_kernel(
    offsets, terms, x_high, x_low, cos_turn, sin_turn, mix_high, mix_low, out, cells, ends
):
    lane = iota((256, 128), 1)
    left = terms[pl.ds(0, 256, stride=4), :]
    right = terms[pl.ds(2, 256, stride=4), :]
    main = jnp.where(lane < 64, left, pltpu.roll(right, 64, 1))
    lane = iota((8, 128), 1)
    block = iota((8, 128), 0)
    spot = iota((8, 256), 1)
    depth = iota((8, 256), 0)
    places = []
    last_places = []
    base_rows = []
    for t in range(64):
        ox = offsets[t, 0]
        tile = terms[pl.ds(16 * t + 1, 8, stride=2), :]
        beyond = (block == 0) & (lane < 16 * (ox & 7))
        cells[8 * t : 8 * t + 8, :] = jnp.where(beyond, 0.0, tile)
        ends[t : t + 1, :] = jnp.where(beyond, tile, 0.0)[0:1, :]
        base = ox >> 3
        places.append(jnp.where(spot == ((base + depth) & 255), 1.0, 0.0))
        base_rows.append(base)
    for t in range(0, 64, 8):
        base = jnp.zeros((8, 256), jnp.int32)
        for k in range(8):
            base = jnp.where(depth == k, base_rows[t + k], base)
        last_places.append(jnp.where(spot == ((base + 8) & 255), 1.0, 0.0))
    where_to = jnp.concatenate(places + last_places, 0).astype(bf16)
    high, low = split(jnp.concatenate([cells[...].T, ends[...].T[:, :64]], 1))
    grid = dot(high, where_to) + dot(low, where_to)
    both = dot3(split(jnp.concatenate([main.T, grid], 0)), (x_high[...], x_low[...]))
    with_cos = both[:, :256]
    with_sin = both[:, 256:]
    cosine = cos_turn[...]
    sine = sin_turn[...]
    turned = jnp.concatenate(
        [with_cos * cosine - with_sin * sine, with_cos * sine + with_sin * cosine], 0
    )
    result = dot3((mix_high[...], mix_low[...]), split(turned))
    out[...] = result.reshape(8, 16, 256)


def finish_kernel(place, terms, eta, phi, eta_next, phi_next):
    first_ky = 32 * place[0]
    wave_x = wave_of(256 * place[1] + iota((32, 256), 1)) * TURN_X
    wave_y = wave_of(first_ky + iota((32, 256), 0)) * TURN_Y
    kappa = time_step * jnp.sqrt(wave_x * wave_x + wave_y * wave_y)
    for a in range(2):
        surface = eta[a]
        potential = phi[a]
        eta_next[a] = surface + kappa * potential
        phi_next[a] = potential - (time_step * gravity) * surface
        for n in range(8):
            rows = slice(4 * n, 4 * n + 4)
            eta_next[a, rows, :] += terms[n, 4 * a : 4 * a + 4, :]
            phi_next[a, rows, :] += terms[n, 8 + 4 * a : 12 + 4 * a, :]


def call(kernel, shapes, scalars, arrays, scratch=(), flops=0):
    single = isinstance(shapes, tuple)
    shapes = [shapes] if single else shapes
    vmem = pl.BlockSpec(memory_space=pltpu.VMEM)
    smem = pl.BlockSpec(memory_space=pltpu.SMEM)
    moved = sum(4 * math.prod(s) for s in shapes) + sum(x.size * x.dtype.itemsize for x in arrays)
    result = pl.pallas_call(
        kernel,
        out_shape=[jax.ShapeDtypeStruct(s, f32) for s in shapes],
        in_specs=[smem] * len(scalars) + [vmem] * len(arrays),
        out_specs=[vmem] * len(shapes),
        scratch_shapes=list(scratch),
        compiler_params=pltpu.CompilerParams(vmem_limit_bytes=VMEM_LIMIT),
        cost_estimate=pl.CostEstimate(flops=flops, bytes_accessed=moved, transcendentals=0),
        name=kernel.__name__,
    )(*scalars, *arrays)
    return result[0] if single else result


def stage_deal(eta, phi):
    return call(deal_kernel, (8, 16, 256), [], [eta, phi])


def stage_source(place, offsets, zone):
    return call(source_kernel, (512, 128), [place, offsets], [zone], flops=2**26)


def stage_rows(place, modes):
    t = tables()
    constants = [*t["rows"], *t["rows_turn"], *t["x"]]
    return call(rows_kernel, (1024, 128), [place], [modes, *constants], flops=2**30)


def stage_columns(terms, source):
    t = tables()
    constants = [*t["y"], *t["y_turn"], t["gather"], *t["y_back"], t["deal"]]
    return call(columns_kernel, (1024, 128), [], [terms, source, *constants], flops=2**30)


def stage_rows_back(offsets, terms):
    t = tables()
    constants = [*t["x"], *t["back_turn"], *t["back"]]
    scratch = [pltpu.VMEM((512, 128), f32), pltpu.VMEM((64, 128), f32)]
    return call(rows_back_kernel, (8, 16, 256), [offsets], [terms, *constants], scratch, flops=2**29)


def stage_finish(place, terms, eta, phi):
    return call(finish_kernel, [(2, 32, 256)] * 2, [place], [terms, eta, phi])


def local(eta_modes, phi_modes, zone_field, offsets):
    place = jnp.stack([lax.axis_index("wide"), lax.axis_index("narrow")]).astype(jnp.int32)
    swap = functools.partial(lax.all_to_all, split_axis=0, concat_axis=0, tiled=True)
    modes = swap(stage_deal(eta_modes, phi_modes), "narrow")
    source = stage_source(place, offsets, zone_field)
    columns = swap(stage_rows(place, modes), BOTH)
    rows = swap(stage_columns(columns, source), BOTH)
    terms = swap(stage_rows_back(offsets, rows), "narrow")
    return tuple(stage_finish(place, terms, eta_modes, phi_modes))


def solution(mesh):
    in_specs = (P(None, "wide", "narrow"), P(None, "wide", "narrow"), P("wide", None), P())
    out_specs = (P(None, "wide", "narrow"), P(None, "wide", "narrow"))
    return jax.shard_map(local, mesh=mesh, in_specs=in_specs, out_specs=out_specs, check_vma=False)
```

profile of v0, /device:TPU:1, one launch (start us, length us, event | category | flops | bytes accessed | tf_op | source)
XLA Modules:
  0.0 121.7 jit_solution(5960033403784895151)
XLA Ops:
  0.6 1.5 %deal_kernel.1 = f32[8,16,256]{2,1,0:T(8,128)} custom-call(f32[2,32,256]{2,1,0:T(8,128)} %eta.3, f32[2,32,256]{2,1,0:T(8,128)} %phi.3), custom_call_target="tpu_custom_call" | custom-call | bytes 262144 | tf_op jit(solution)/shard_map/deal_kernel/pallas_call | solution.py:292
  2.2 10.1 %all-to-all-start = ((f32[8,16,256]{2,1,0:T(8,128)}), f32[8,16,256]{2,1,0:T(8,128)S(1)}, u32[]{:S(2)}, u32[]{:S(2)}) async-start(f32[8,16,256]{2,1,0:T(8,128)} %deal_kernel.1), calls=%async_computation | async-start | bytes 262144 | tf_op jit(solution)/shard_map/all_to_all | solution.py:339
  12.3 0.6 pad_add_fusion.place
  13.0 5.2 %all-to-all-done.modes = f32[8,16,256]{2,1,0:T(8,128)S(1)} async-done(((f32[8,16,256]{2,1,0:T(8,128)}), f32[8,16,256]{2,1,0:T(8,128)S(1)}, u32[]{:S(2)}, u32[]{:S(2)}) %all-to-all-start) | async-done | bytes 131104 | tf_op jit(solution)/shard_map/all_to_all | solution.py:339
  18.2 0.0 copy-start.1
  18.2 0.6 copy-done.1
  18.8 4.6 %rows_kernel.1 = f32[1024,128]{1,0:T(8,128)} custom-call(s32[2]{0:T(128)} %pad_add_fusion.place, f32[8,16,256]{2,1,0:T(8,128)} %copy-done.1, bf16[1024,320]{1,0:T(8,128)(2,1)} %constant.45.clone.mix_high, bf16[1024,320]{1,0:T(8,128)(2,1)} %constant.46.clone.mix_low, f32[2,8,256]{2,1,0:T(8,128)} %constant.47.clone.cos_turn, ...), custom_call_target="tpu_custom_call" | custom-call | flops 1073741824 | bytes 2523136 | tf_op jit(solution)/shard_map/rows_kernel/pallas_call | solution.py:292
  23.4 0.0 copy-start.2
  23.4 17.5 %all-to-all-start.1 = ((f32[512,2,128]{2,1,0:T(2,128)}), f32[512,2,128]{2,1,0:T(2,128)S(1)}, u32[]{:S(2)}, u32[]{:S(2)}) async-start(f32[512,2,128]{2,1,0:T(2,128)} %bitcast.9), calls=%async_computation.1 | async-start | bytes 1048576 | tf_op jit(solution)/shard_map/all_to_all | solution.py:341
  40.9 0.0 copy-done.2
  40.9 0.7 copy.25.offsets
  41.7 2.6 %source_kernel.1.source = f32[512,128]{1,0:T(8,128)} custom-call(s32[2]{0:T(128)} %pad_add_fusion.place, s32[64,2]{1,0:T(8,128)} %copy.25.offsets, f32[64,128]{1,0:T(8,128)} %zone.1), custom_call_target="tpu_custom_call" | custom-call | flops 67108864 | bytes 294912 | tf_op jit(solution)/shard_map/source_kernel/pallas_call | solution.py:292
  44.2 19.4 %all-to-all-done.1 = f32[512,2,128]{2,1,0:T(2,128)S(1)} async-done(((f32[512,2,128]{2,1,0:T(2,128)}), f32[512,2,128]{2,1,0:T(2,128)S(1)}, u32[]{:S(2)}, u32[]{:S(2)}) %all-to-all-start.1) | async-done | bytes 524320 | tf_op jit(solution)/shard_map/all_to_all | solution.py:341
  63.7 0.0 copy-start
  63.7 0.8 copy-done
  64.5 7.2 %columns_kernel.1 = f32[1024,128]{1,0:T(8,128)} custom-call(f32[1024,128]{1,0:T(8,128)} %bitcast.6, f32[512,128]{1,0:T(8,128)} %source_kernel.1.source, bf16[512,1024]{1,0:T(8,128)(2,1)} %constant.51.clone.y_high, bf16[512,1024]{1,0:T(8,128)(2,1)} %constant.52.clone.y_low, f32[512,128]{1,0:T(8,128)} %constant.53.clone.cos_turn, ...), custom_call_target="tpu_custom_call" | custom-call | flops 1073741824 | bytes 4915200 | tf_op jit(solution)/shard_map/columns_kernel/pallas_call | solution.py:292
  71.7 34.1 %all_to_all.32 = f32[512,2,128]{2,1,0:T(2,128)} all-to-all(f32[512,2,128]{2,1,0:T(2,128)} %bitcast.7), channel_id=1, replica_groups=mesh['wide'=64,'narrow'=8] {'wide','narrow'}, dimensions={0} | all-to-all | bytes 1048576 | tf_op jit(solution)/shard_map/all_to_all | solution.py:342
  105.8 3.3 %rows_back_kernel.1 = f32[8,16,256]{2,1,0:T(8,128)} custom-call(s32[64,2]{1,0:T(8,128)} %copy.25.offsets, f32[1024,128]{1,0:T(8,128)} %bitcast.8, bf16[256,512]{1,0:T(8,128)(2,1)} %constant.49.clone.x_high, bf16[256,512]{1,0:T(8,128)(2,1)} %constant.50.clone.x_low, f32[256,256]{1,0:T(8,128)} %constant.59.clone.cos_turn, f32[256,256]{1,0:T(8,128)} %constant.60.clone.sin_turn, ...), custom_call_target="tpu_custom_call" | custom-call | flops 536870912 | bytes 1966080 | tf_op jit(solution)/shard_map/rows_back_kernel/pallas_call | solution.py:292
  109.2 10.9 %all_to_all.33.terms = f32[8,16,256]{2,1,0:T(8,128)} all-to-all(f32[8,16,256]{2,1,0:T(8,128)} %rows_back_kernel.1), channel_id=1, replica_groups=mesh['wide'=64,'narrow'=8] {'narrow'}, dimensions={0} | all-to-all | bytes 262144 | tf_op jit(solution)/shard_map/all_to_all | solution.py:343
  120.1 1.7 %finish_kernel.1 = (f32[2,32,256]{2,1,0:T(8,128)}, f32[2,32,256]{2,1,0:T(8,128)}) custom-call(s32[2]{0:T(128)} %pad_add_fusion.place, f32[8,16,256]{2,1,0:T(8,128)} %all_to_all.33.terms, f32[2,32,256]{2,1,0:T(8,128)} %eta.3, f32[2,32,256]{2,1,0:T(8,128)} %phi.3), custom_call_target="tpu_custom_call" | custom-call | bytes 393216 | tf_op jit(solution)/shard_map/finish_kernel/pallas_call | solution.py:292
Async XLA Ops:
  2.2 16.0 %all-to-all-start = ((f32[8,16,256]{2,1,0:T(8,128)}), f32[8,16,256]{2,1,0:T(8,128)S(1)}, u32[]{:S(2)}, u32[]{:S(2)}) async-start(f32[8,16,256]{2,1,0:T(8,128)} %deal_kernel.1), calls=%async_computation | async-start | bytes 262144 | tf_op jit(solution)/shard_map/all_to_all | solution.py:339
  18.2 0.6 copy-start.1
  23.4 17.5 %copy-start.2 = (s32[64,2]{0,1:T(2,128)S(1)}, s32[64,2]{0,1:T(2,128)}, u32[]{:S(2)}) copy-start(s32[64,2]{0,1:T(2,128)} %param.25) | copy-start | bytes 1540
  23.4 40.2 %all-to-all-start.1 = ((f32[512,2,128]{2,1,0:T(2,128)}), f32[512,2,128]{2,1,0:T(2,128)S(1)}, u32[]{:S(2)}, u32[]{:S(2)}) async-start(f32[512,2,128]{2,1,0:T(2,128)} %bitcast.9), calls=%async_computation.1 | async-start | bytes 1048576 | tf_op jit(solution)/shard_map/all_to_all | solution.py:341
  63.7 0.8 copy-start
where the time goes:
time: 122 us
  blocking collectives  45.1 us (37%)
  starting transfers between devices  27.6 us (23%)
  waiting for transfers between devices  24.6 us (20%)
  Pallas kernels  21 us (17%)
  local copies, waits for them, and re-layouts  2.15 us (2%)
    all_to_all x1, blocking collectives, local(): rows = swap(stage_columns(columns, source), BOTH)  34.1 us
    pallas_call x6, Pallas kernels, call(): pl.pallas_call(kernel, out_shape=[jax.ShapeDtypeStruct(s, f32) for s in s...  21 us
    all_to_all x1, waiting for transfers between devices, local(): columns = swap(stage_rows(place, modes), BOTH)  19.4 us
    all_to_all x1, starting transfers between devices, local(): columns = swap(stage_rows(place, modes), BOTH)  17.5 us
    all_to_all x1, blocking collectives, local(): terms = swap(stage_rows_back(offsets, rows), 'narrow')  10.9 us
    all_to_all x1, starting transfers between devices, local(): modes = swap(stage_deal(eta_modes, phi_modes), 'narrow')  10.1 us
    all_to_all x1, waiting for transfers between devices, local(): modes = swap(stage_deal(eta_modes, phi_modes), 'narrow')  5.19 us
  transfers between devices with their start and end apart: 2, of which 2 were waited for; matrix products, arithmetic and copies ran while one was open for 1% of the time, Pallas kernels for 2%

commit v1 on v0

v1 whole, which is shorter than its diff:
```python
import functools
import math

import jax
import jax.numpy as jnp
import ml_dtypes
import numpy as np
from jax import lax
from jax.experimental import pallas as pl
from jax.experimental.pallas import tpu as pltpu
from jax.sharding import Mesh
from jax.sharding import PartitionSpec as P

NX = 2048
NY = 2048
FINE = 4096
TURN_X = 2.0 * math.pi / NX
TURN_Y = 2.0 * math.pi / NY
time_step = 0.04
gravity = 9.81
spread = 1.0 / math.sqrt(NX * NY)
zone_scale = 1.0 / math.sqrt(4096 * 128)
f32 = jnp.float32
bf16 = jnp.bfloat16
VMEM_LIMIT = 24 * 1024 * 1024


def part(value, which):
    return np.where(which == 0, np.real(value), np.imag(value))


def angles(ints, period):
    return 2.0 * np.pi * (np.asarray(ints) % period) / period


def pair(matrix):
    high = matrix.astype(np.float32).astype(ml_dtypes.bfloat16)
    low = (matrix - high.astype(np.float64)).astype(np.float32).astype(ml_dtypes.bfloat16)
    return high, low


def circle(phase):
    return np.cos(phase).astype(np.float32), np.sin(phase).astype(np.float32)


@functools.cache
def tables():
    out = {}
    k256 = np.arange(256)
    phase = angles(k256[:, None] * k256[None, :], 256)
    out["turn"] = pair(np.concatenate([np.cos(phase), np.sin(phase)], 1))
    row = np.arange(64)
    i, a, jj = row // 16, row // 8 % 2, row % 8
    col = np.arange(128)
    n, ca, cj = col // 16, col // 8 % 2, col % 8
    base = np.exp(1j * angles(i[:, None] * n[None, :], 8)) * (1j ** ca)[None, :]
    same = jj[:, None] == cj[None, :]
    for name, factor in (("slope", 1j), ("lift", 1.0)):
        halves = [np.where(same, part(base * factor * s, a[:, None]), 0.0) for s in (1, 1j)]
        out[name] = pair(np.concatenate(halves, 0))
    x0 = 4 * np.arange(2)[:, None] + np.arange(64)[None, :] // 16
    out["rows_turn"] = circle(angles(x0[:, :, None] * k256, NX))
    lane = np.arange(128)
    out["y_turn"] = circle(angles(k256[:, None] * (lane % 8)[None, :], NY))
    y0 = np.arange(8)
    turn = np.exp(1j * angles((lane % 8)[:, None] * y0[None, :], 8)) * spread
    gather = np.zeros((2, 128, 4, 128))
    gather_lift = np.zeros((128, 128))
    for k in range(128):
        f, i = k // 32, k // 8 % 4
        gather[0, k, f, y0 * 4 + i] = turn[k].real
        gather[1, k, f, y0 * 4 + i] = -turn[k].imag
        if k < 64:
            gather_lift[k, y0 * 4 + i] = turn[k].real if k < 32 else -turn[k].imag
    out["gather"] = pair(gather.reshape(256, 512))
    out["gather_lift"] = pair(gather_lift)
    deal = np.zeros((2, 128, 2, 128))
    for k in range(128):
        f, a, i, jj = k // 64, k // 32 % 2, k // 8 % 4, k % 8
        turn = np.exp(-1j * angles(jj * y0, 8))
        deal[f, y0 * 4 + i, 0, k] = part(turn, a)
        deal[f, y0 * 4 + i, 1, k] = part(-1j * turn, a)
    out["deal"] = pair(deal.reshape(256, 256))
    x0 = 4 * np.arange(2)[:, None] + np.arange(32)[None, :] // 8
    out["main_turn"] = circle(angles(x0[:, :, None] * k256, NX))
    cell = np.arange(128) // 8
    out["zone_turn"] = circle(angles(cell[:, None] * k256, FINE))
    row = np.arange(256)
    n, of, oa, oj = row // 32, row // 16 % 2, row // 8 % 2, row % 8
    col = np.arange(128)
    f, a, i, jj = col // 64, col // 32 % 2, col // 8 % 4, col % 8
    turn = np.exp(-1j * angles(n[:, None] * i[None, :], 8)) * (1j ** a)[None, :]
    same = (of[:, None] == f[None, :]) & (oj[:, None] == jj[None, :])
    halves = [np.where(same, part(turn * s, oa[:, None]), 0.0) for s in (1, -1j)]
    out["main_mix"] = pair(np.concatenate(halves, 1))
    row = np.arange(128)
    n, oa, oj = row // 16, row // 8 % 2, row % 8
    a, p, jj = np.arange(256) // 128, np.arange(256) // 8 % 16, np.arange(256) % 8
    signed = np.where(n < 4, n, n - 8)
    turn = np.exp(-1j * angles(signed[:, None] * p[None, :], 16)) * (1j ** a)[None, :]
    same = oj[:, None] == jj[None, :]
    halves = [np.where(same, part(turn * s, oa[:, None]), 0.0) for s in (1, -1j)]
    out["zone_mix"] = pair(np.concatenate(halves, 1))
    return out


def split(value):
    high = value.astype(bf16)
    return high, (value - high.astype(f32)).astype(bf16)


def dot(left, right, dims=((1,), (0,))):
    return lax.dot_general(left, right, (dims, ((), ())), preferred_element_type=f32)


def dot3(left, right, dims=((1,), (0,))):
    return dot(left[0], right[0], dims) + (dot(left[0], right[1], dims) + dot(left[1], right[0], dims))


def iota(shape, dim):
    return lax.broadcasted_iota(jnp.int32, shape, dim)


def cos_of(phase):
    moved = phase + 512
    quarter = (moved >> 10) & 3
    angle = ((moved & 1023) - 512).astype(f32) * (2.0 * math.pi / FINE)
    square = angle * angle
    cosine = 1.0 + square * (-0.5 + square * (1.0 / 24 + square * (-1.0 / 720 + square * (1.0 / 40320))))
    sine = angle * (
        1.0 + square * (-1.0 / 6 + square * (1.0 / 120 + square * (-1.0 / 5040 + square * (1.0 / 362880))))
    )
    size = jnp.where((quarter & 1) == 0, cosine, sine)
    return jnp.where((quarter == 1) | (quarter == 2), -size, size)


def wave_of(index):
    return jnp.where(index < 1024, index, index - 2048).astype(f32)


def deal_kernel(eta, phi, out):
    for z in range(4):
        for source, base in ((eta, 0), (phi, 16)):
            for a in range(2):
                rows = source[a, 8 * z : 8 * z + 8, :]
                for c in range(2):
                    out[2 * z + c, base + 8 * a : base + 8 * a + 8, :] = rows


def source_kernel(place, offsets, zone, out):
    tile = place[0]
    own = 4 * place[2] + place[1]
    ox = offsets[tile, 0]
    oy = offsets[tile, 1]
    lane = iota((128, 128), 1)
    wanted = (16 * own + (lane >> 3) - 2 * (ox & 7)) & 127
    pick = jnp.where(iota((128, 128), 0) == wanted, 1.0, 0.0).astype(bf16)
    high, low = split(zone[...] * zone_scale)
    cells = dot(high, pick) + dot(low, pick)
    phase = (iota((64, 128), 1) & 7) * (2 * oy + iota((64, 128), 0))
    real = cells * cos_of(phase)
    imag = cells * cos_of(phase + 1024)
    right = jnp.concatenate(
        [jnp.concatenate([real, imag], 1), jnp.concatenate([-imag, real], 1)], 0
    )
    lane = iota((256, 128), 1)
    g = iota((256, 128), 0)
    g = jnp.where(g < 128, g, g - 256)
    left = cos_of(8 * g * (2 * oy + (lane & 63)) + jnp.where(lane < 64, 0, 1024))
    out[...] = dot3(split(left), split(right))


def rows_kernel(
    place, modes, slope_high, slope_low, lift_high, lift_low, cos_turn, sin_turn, high, low, out
):
    first_ky = 32 * place[0] + 8 * place[1]
    core = place[2]
    odd = 1.0 - 2.0 * core.astype(f32)
    wave_y = wave_of(first_ky + (iota((16, 256), 0) & 7)) * TURN_Y
    tiles = [[], [], [], [], []]
    for n in range(8):
        wave_x = wave_of(256 * n + iota((16, 256), 1)) * TURN_X
        kappa = jnp.sqrt(wave_x * wave_x + wave_y * wave_y)
        eta = modes[n, 0:16, :]
        phi = modes[n, 16:32, :]
        if n % 2:
            eta = eta * odd
            phi = phi * odd
        terms = (wave_x * eta, wave_y * eta, wave_x * phi, wave_y * phi, kappa * phi)
        for f in range(5):
            tiles[f].append(terms[f])
    cosine = cos_turn[core]
    sine = sin_turn[core]
    slope_mix = (slope_high[...], slope_low[...])
    lift_mix = (lift_high[...], lift_low[...])
    parts = [[], []]
    for f in range(5):
        rows = split(jnp.concatenate(tiles[f], 0))
        both = dot3(slope_mix if f < 4 else lift_mix, rows)
        first = both[:64]
        second = both[64:]
        turned = (first * cosine + second * sine).reshape(4, 2, 8, 256)
        quarter = (second * cosine - first * sine).reshape(4, 2, 8, 256)
        for a in range(2):
            parts[a].append(
                jnp.concatenate(
                    [turned[:, a].reshape(32, 256), quarter[:, a].reshape(32, 256)], 1
                )
            )
    real, imag = parts
    words = real[:4] + imag[:4] + [real[4], imag[4], -imag[4], real[4]]
    result = dot3((high[...], low[...]), split(jnp.concatenate(words, 0)), ((1,), (1,)))
    for q in range(3):
        out[pl.ds(q, 256, stride=4), :] = result[:, 128 * q : 128 * q + 128]
    out[pl.ds(3, 256, stride=4), :] = jnp.zeros((256, 128), f32)


def columns_kernel(
    terms,
    source,
    high,
    low,
    cos_turn,
    sin_turn,
    gather_high,
    gather_low,
    gather_lift_high,
    gather_lift_low,
    deal_high,
    deal_low,
    out,
):
    words = split(
        jnp.concatenate([terms[pl.ds(q, 256, stride=4), :] for q in range(3)], 1)
    )
    with_cos = dot3((high[:, :256], low[:, :256]), words)
    with_sin = dot3((high[:, 256:], low[:, 256:]), words)
    real = with_cos[:, :128] - with_sin[:, 128:256]
    imag = with_sin[:, :128] + with_cos[:, 128:256]
    lane = iota((256, 128), 1)
    rolled = pltpu.roll(with_sin[:, 256:], 64, 1)
    lift = with_cos[:, 256:] + jnp.where(lane < 64, rolled, -rolled)
    cosine = cos_turn[...]
    sine = sin_turn[...]
    slopes = split(
        jnp.concatenate([real * cosine - imag * sine, real * sine + imag * cosine], 1)
    )
    lift = split(lift * cosine + pltpu.roll(lift, 64, 1) * sine)
    fields = dot3(slopes, (gather_high[...], gather_low[...]))
    lift = dot3(lift, (gather_lift_high[...], gather_lift_low[...]))
    slope_ex, slope_ey, slope_px, slope_py = (
        fields[:, 128 * k : 128 * k + 128] for k in range(4)
    )
    first_order = lift * (slope_ex * slope_ex + slope_ey * slope_ey) - (
        slope_px * slope_ex + slope_py * slope_ey
    )
    second_term = 0.5 * (lift * lift - slope_px * slope_px - slope_py * slope_py)
    products = jnp.concatenate([first_order, second_term], 1) * (time_step * spread)
    both = dot3(split(products), (deal_high[...], deal_low[...]))
    first = both[:, :128]
    second = both[:, 128:]
    turned = jnp.concatenate([first * cosine + second * sine, second * cosine - first * sine], 0)
    out[pl.ds(0, 256, stride=4), :] = dot3((high[...], low[...]), split(turned))
    out[pl.ds(1, 256, stride=4), :] = source[:, :128]
    out[pl.ds(2, 256, stride=4), :] = source[:, 128:]
    out[pl.ds(3, 256, stride=4), :] = jnp.zeros((256, 128), f32)


def rows_back_kernel(
    place,
    offsets,
    terms,
    high,
    low,
    cos_main,
    sin_main,
    cos_zone,
    sin_zone,
    main_high,
    main_low,
    zone_high,
    zone_low,
    out,
    ends,
):
    core = place[2]
    depth = iota((8, 256), 0)
    spot = iota((8, 256), 1)
    lane = iota((8, 128), 1)
    row = iota((8, 128), 0)
    cells = [[], []]
    places = []
    last_places = []
    bases = []
    for t in range(0, 64, 2):
        ox = offsets[t, 0], offsets[t + 1, 0]
        base = ox[0] >> 3, ox[1] >> 3
        bases += base
        edge = jnp.where(row < 4, 8 * (2 * (ox[0] & 7)), 8 * (2 * (ox[1] & 7)))
        edge = jnp.where(((row & 3) == 0) & (core == 0), edge, 0)
        beyond = lane < edge
        for a in range(2):
            tile = terms[pl.ds(16 * t + 1 + a, 8, stride=4), :]
            cells[a].append(jnp.where(beyond, 0.0, tile))
            moved = jnp.where(beyond, tile, 0.0)
            ends[t : t + 1, 128 * a : 128 * a + 128] = moved[0:1, :]
            ends[t + 1 : t + 2, 128 * a : 128 * a + 128] = moved[4:5, :]
        target = jnp.where(depth < 4, base[0], base[1]) + (depth & 3) + 4 * core
        places.append(jnp.where(spot == (target & 255), 1.0, 0.0))
    for t in range(0, 64, 8):
        target = jnp.zeros((8, 256), jnp.int32)
        for k in range(8):
            target = jnp.where(depth == k, bases[t + k], target)
        last_places.append(jnp.where(spot == ((target + 8) & 255), 1.0, 0.0))
    where_to = jnp.concatenate(places, 0).astype(bf16)
    last_to = jnp.concatenate(last_places, 0).astype(bf16)
    cells = jnp.concatenate([jnp.concatenate(half, 0) for half in cells], 1)
    near = split(cells.T)
    far = split(ends[...].T)
    grid = (dot(near[0], where_to) + dot(near[1], where_to)) + (
        dot(far[0], last_to) + dot(far[1], last_to)
    )
    main = terms[pl.ds(0, 256, stride=4), :].T
    both = dot3(split(jnp.concatenate([main, grid], 0)), (high[...], low[...]))

    def turned(lines, cosine, sine):
        with_cos = lines[:, :, :256]
        with_sin = lines[:, :, 256:]
        real = with_cos * cosine - with_sin * sine
        imag = with_cos * sine + with_sin * cosine
        count = lines.shape[0] * lines.shape[1]
        return split(
            jnp.concatenate([real.reshape(count, 256), imag.reshape(count, 256)], 0)
        )

    main = turned(both[:128].reshape(4, 32, 512), cos_main[core][None], sin_main[core][None])
    zone = turned(both[128:].reshape(2, 128, 512), cos_zone[...][None], sin_zone[...][None])
    main = dot3((main_high[...], main_low[...]), main)
    zone = dot3((zone_high[...], zone_low[...]), zone)
    odd = 1.0 - 2.0 * core.astype(f32)
    for n in range(8):
        block = main[32 * n : 32 * n + 32]
        if n % 2:
            block = block * odd
        out[n, 0:16, :] = block[:16] + zone[16 * n : 16 * n + 16]
        out[n, 16:32, :] = block[16:]


def finish_kernel(place, terms, eta, phi, eta_next, phi_next):
    for z in range(4):
        rows = slice(8 * z, 8 * z + 8)
        wave_x = wave_of(256 * (2 * place[1] + place[2]) + iota((8, 256), 1)) * TURN_X
        wave_y = wave_of(32 * place[0] + 8 * z + iota((8, 256), 0)) * TURN_Y
        kappa = time_step * jnp.sqrt(wave_x * wave_x + wave_y * wave_y)
        for a in range(2):
            surface = eta[a, rows, :]
            potential = phi[a, rows, :]
            part_of = slice(8 * a, 8 * a + 8)
            added = terms[2 * z, part_of, :] + terms[2 * z + 1, part_of, :]
            eta_next[a, rows, :] = surface + kappa * potential + added
            part_of = slice(16 + 8 * a, 24 + 8 * a)
            added = terms[2 * z, part_of, :] + terms[2 * z + 1, part_of, :]
            phi_next[a, rows, :] = potential - (time_step * gravity) * surface + added


def call(kernel, shapes, scalars, arrays, scratch=(), flops=0):
    single = isinstance(shapes, tuple)
    shapes = [shapes] if single else shapes
    vmem = pl.BlockSpec(memory_space=pltpu.VMEM)
    smem = pl.BlockSpec(memory_space=pltpu.SMEM)
    moved = sum(4 * math.prod(s) for s in shapes) + sum(x.size * x.dtype.itemsize for x in arrays)
    result = pl.pallas_call(
        kernel,
        out_shape=[jax.ShapeDtypeStruct(s, f32) for s in shapes],
        in_specs=[smem] * len(scalars) + [vmem] * len(arrays),
        out_specs=[vmem] * len(shapes),
        scratch_shapes=list(scratch),
        compiler_params=pltpu.CompilerParams(vmem_limit_bytes=VMEM_LIMIT),
        cost_estimate=pl.CostEstimate(flops=flops, bytes_accessed=moved, transcendentals=0),
        name=kernel.__name__,
    )(*scalars, *arrays)
    return result[0] if single else result


def stage_deal(eta, phi):
    return call(deal_kernel, (8, 32, 256), [], [eta, phi])


def stage_source(place, offsets, zone):
    return call(source_kernel, (256, 256), [place, offsets], [zone], flops=2**26)


def stage_rows(place, modes):
    t = tables()
    constants = [*t["slope"], *t["lift"], *t["rows_turn"], *t["turn"]]
    return call(rows_kernel, (1024, 128), [place], [modes, *constants], flops=2**30)


def stage_columns(terms, source):
    t = tables()
    constants = [*t["turn"], *t["y_turn"], *t["gather"], *t["gather_lift"], *t["deal"]]
    return call(columns_kernel, (1024, 128), [], [terms, source, *constants], flops=2**30)


def stage_rows_back(place, offsets, terms):
    t = tables()
    constants = [*t["turn"], *t["main_turn"], *t["zone_turn"], *t["main_mix"], *t["zone_mix"]]
    scratch = [pltpu.VMEM((64, 256), f32)]
    arrays = [terms, *constants]
    return call(rows_back_kernel, (8, 32, 256), [place, offsets], arrays, scratch, flops=2**29)


def stage_finish(place, terms, eta, phi):
    return call(finish_kernel, [(2, 32, 256)] * 2, [place], [terms, eta, phi])


def local(eta_modes, phi_modes, zone_field, offsets):
    place = jnp.stack([lax.axis_index(axis) for axis in ("wide", "lane", "core")]).astype(jnp.int32)
    swap = functools.partial(lax.all_to_all, split_axis=0, concat_axis=0, tiled=True)
    modes = swap(stage_deal(eta_modes, phi_modes), ("lane", "core"))
    source = stage_source(place, offsets, zone_field)
    columns = swap(stage_rows(place, modes), ("wide", "lane"))
    rows = swap(stage_columns(columns, source), ("wide", "lane"))
    terms = swap(stage_rows_back(place, offsets, rows), ("lane", "core"))
    return tuple(stage_finish(place, terms, eta_modes, phi_modes))


def solution(mesh):
    wide, narrow = mesh.devices.shape
    chips = Mesh(mesh.devices.reshape(wide, narrow // 2, 2), ("wide", "lane", "core"))
    modes = P(None, "wide", ("lane", "core"))
    in_specs = (modes, modes, P("wide", None), P())
    return jax.shard_map(
        local, mesh=chips, in_specs=in_specs, out_specs=(modes, modes), check_vma=False
    )
```

time: 122 us -> 110 us (0.902)
  Pallas kernels: 21 us -> 10.3 us
  blocking collectives: 45.1 us -> 43 us
    pallas_call x6, Pallas kernels: 21 us -> 10.3 us  [call(): pl.pallas_call(kernel, out_shape=[jax.ShapeDtypeStruct(s, f32) for s in s...]
    all_to_all x2, blocking collectives: 45.1 us -> 43 us  [the longest x1 27.2 us: local(): rows = swap(stage_columns(columns, source), ('wide', 'lane'))]
    unnamed x7 -> x61, local copies, waits for them, and re-layouts: 2.15 us -> 2.56 us
  transfers between devices with their start and end apart: 2 -> 2, of which waited for: 2 -> 2; matrix products, arithmetic and copies ran while one was open for 1% -> 0% of each run, Pallas kernels for 2% -> 1%
where the time goes in v1:
time: 110 us; the launch traced here: 109 us
  blocking collectives  43 us (39%)
  starting transfers between devices  28.7 us (26%)
  waiting for transfers between devices  23.6 us (21%)
  Pallas kernels  10.3 us (9%)
  local copies, waits for them, and re-layouts  2.56 us (2%)
    all_to_all x1, blocking collectives, local(): rows = swap(stage_columns(columns, source), ('wide', 'lane'))  27.2 us
    all_to_all x1, starting transfers between devices, local(): columns = swap(stage_rows(place, modes), ('wide', 'lane'))  18.3 us
    all_to_all x1, blocking collectives, local(): terms = swap(stage_rows_back(place, offsets, rows), ('lane', 'core'))  15.8 us
    all_to_all x1, waiting for transfers between devices, local(): columns = swap(stage_rows(place, modes), ('wide', 'lane'))  14.9 us
    all_to_all x1, starting transfers between devices, local(): modes = swap(stage_deal(eta_modes, phi_modes), ('lane', 'core'))  10.3 us
    pallas_call x6, Pallas kernels, call(): pl.pallas_call(kernel, out_shape=[jax.ShapeDtypeStruct(s, f32) for s in s...  10.3 us
    all_to_all x1, waiting for transfers between devices, local(): modes = swap(stage_deal(eta_modes, phi_modes), ('lane', 'core'))  8.65 us
    unnamed x61, local copies, waits for them, and re-layouts  2.56 us
  transfers between devices with their start and end apart: 2, of which 2 were waited for; matrix products, arithmetic and copies ran while one was open for 0% of the time, Pallas kernels for 1%

profile of v1, /device:TPU:1, one launch (start us, length us, event | category | flops | bytes accessed | tf_op | source)
XLA Modules:
  0.0 109.1 jit_solution(7014821036201524925)
XLA Ops:
  0.6 0.8 copy-done.2
  1.5 0.8 copy-done.4
  2.3 0.0 copy-start.27
  2.3 0.0 copy-start.28
  2.3 0.7 deal_kernel.1
  3.1 10.3 %all-to-all-start = ((f32[8,32,256]{2,1,0:T(8,128)}), f32[8,32,256]{2,1,0:T(8,128)S(1)}, u32[]{:S(2)}, u32[]{:S(2)}) async-start(f32[8,32,256]{2,1,0:T(8,128)} %deal_kernel.1), calls=%async_computation | async-start | bytes 524288 | tf_op jit(solution)/shard_map/all_to_all | solution.py:420
  13.4 0.1 pad_add_fusion.place
  13.5 8.7 %all-to-all-done.modes = f32[8,32,256]{2,1,0:T(8,128)S(1)} async-done(((f32[8,32,256]{2,1,0:T(8,128)}), f32[8,32,256]{2,1,0:T(8,128)S(1)}, u32[]{:S(2)}, u32[]{:S(2)}) %all-to-all-start) | async-done | bytes 262176 | tf_op jit(solution)/shard_map/all_to_all | solution.py:420
  22.2 2.3 %rows_kernel.1 = f32[1024,128]{1,0:T(8,128)} custom-call(s32[3]{0:T(128)S(1)} %pad_add_fusion.place, f32[8,32,256]{2,1,0:T(8,128)S(1)} %all-to-all-done.modes, bf16[128,128]{1,0:T(8,128)(2,1)S(1)} %copy-done.25, bf16[128,128]{1,0:T(8,128)(2,1)S(1)} %copy-done.26, bf16[128,128]{1,0:T(8,128)(2,1)S(1)} %copy-done.27, bf16[128,128]{1,0:T(8,128)(2,1)S(1)} %copy-done.28, ...), custom_call_target="tpu_custom_call" | custom-call | flops 1073741824 | bytes 1703936 | tf_op jit(solution)/shard_map/rows_kernel/pallas_call | solution.py:372
  24.5 0.0 copy-start.19
  24.5 0.0 copy-start.20
  24.5 18.3 %all-to-all-start.1 = ((f32[256,4,128]{2,1,0:T(4,128)}), f32[256,4,128]{2,1,0:T(4,128)S(1)}, u32[]{:S(2)}, u32[]{:S(2)}) async-start(f32[256,4,128]{2,1,0:T(4,128)} %bitcast.3), calls=%async_computation.1 | async-start | bytes 1048576 | tf_op jit(solution)/shard_map/all_to_all | solution.py:422
  42.9 0.0 copy-start.15
  42.9 0.1 copy.31.offsets
  43.0 0.6 copy-done.14
  43.7 1.6 %source_kernel.1.source = f32[256,256]{1,0:T(8,128)S(1)} custom-call(s32[3]{0:T(128)S(1)} %pad_add_fusion.place, s32[64,2]{1,0:T(8,128)S(1)} %copy.31.offsets, f32[64,128]{1,0:T(8,128)S(1)} %copy-done.14), custom_call_target="tpu_custom_call" | custom-call | flops 67108864 | bytes 294912 | tf_op jit(solution)/shard_map/source_kernel/pallas_call | solution.py:372
  45.3 14.9 %all-to-all-done.1 = f32[256,4,128]{2,1,0:T(4,128)S(1)} async-done(((f32[256,4,128]{2,1,0:T(4,128)}), f32[256,4,128]{2,1,0:T(4,128)S(1)}, u32[]{:S(2)}, u32[]{:S(2)}) %all-to-all-start.1) | async-done | bytes 524320 | tf_op jit(solution)/shard_map/all_to_all | solution.py:422
  60.2 1.7 %columns_kernel.1 = f32[1024,128]{1,0:T(8,128)S(1)} custom-call(f32[1024,128]{1,0:T(8,128)S(1)} %bitcast.8, f32[256,256]{1,0:T(8,128)S(1)} %source_kernel.1.source, bf16[256,512]{1,0:T(8,128)(2,1)S(1)} %copy-done, bf16[256,512]{1,0:T(8,128)(2,1)S(1)} %copy-done.1, f32[256,128]{1,0:T(8,128)S(1)} %copy-done.17, f32[256,128]{1,0:T(8,128)S(1)} %copy-done.18, ...), custom_call_target="tpu_custom_call" | custom-call | flops 1073741824 | bytes 2949120 | tf_op jit(solution)/shard_map/columns_kernel/pallas_call | solution.py:372
  61.9 0.0 copy-start.6
  61.9 0.0 copy-start.7
  62.0 27.2 %all_to_all.32 = f32[256,4,128]{2,1,0:T(4,128)S(1)} all-to-all(f32[256,4,128]{2,1,0:T(4,128)S(1)} %bitcast.9), channel_id=1, replica_groups=mesh['wide'=64,'lane'=4,'core'=2] {'wide','lane'}, dimensions={0} | all-to-all | bytes 1048576 | tf_op jit(solution)/shard_map/all_to_all | solution.py:423
  89.3 2.7 %rows_back_kernel.1 = f32[8,32,256]{2,1,0:T(8,128)S(1)} custom-call(s32[3]{0:T(128)S(1)} %pad_add_fusion.place, s32[64,2]{1,0:T(8,128)S(1)} %copy.31.offsets, f32[1024,128]{1,0:T(8,128)S(1)} %bitcast.7, bf16[256,512]{1,0:T(8,128)(2,1)S(1)} %copy-done, bf16[256,512]{1,0:T(8,128)(2,1)S(1)} %copy-done.1, f32[2,32,256]{2,1,0:T(8,128)S(1)} %copy-done.12, ...), custom_call_target="tpu_custom_call" | custom-call | flops 536870912 | bytes 2228224 | tf_op jit(solution)/shard_map/rows_back_kernel/pallas_call | solution.py:372
  92.1 15.8 %all_to_all.33.terms = f32[8,32,256]{2,1,0:T(8,128)S(1)} all-to-all(f32[8,32,256]{2,1,0:T(8,128)S(1)} %rows_back_kernel.1), channel_id=1, replica_groups=mesh['wide'=64,'lane'=4,'core'=2] {'lane','core'}, dimensions={0} | all-to-all | bytes 524288 | tf_op jit(solution)/shard_map/all_to_all | solution.py:424
  107.9 1.2 %finish_kernel.1 = (f32[2,32,256]{2,1,0:T(8,128)}, f32[2,32,256]{2,1,0:T(8,128)}) custom-call(s32[3]{0:T(128)S(1)} %pad_add_fusion.place, f32[8,32,256]{2,1,0:T(8,128)S(1)} %all_to_all.33.terms, f32[2,32,256]{2,1,0:T(8,128)S(1)} %copy-done.3, f32[2,32,256]{2,1,0:T(8,128)S(1)} %copy-done.5), custom_call_target="tpu_custom_call" | custom-call | bytes 524288 | tf_op jit(solution)/shard_map/finish_kernel/pallas_call | solution.py:372
  (50 shorter events, 0.1 us)
Async XLA Ops:
  2.3 19.8 %copy-start.21 = (f32[2,64,256]{2,1,0:T(8,128)S(1)}, f32[2,64,256]{2,1,0:T(8,128)}, u32[]{:S(2)}) copy-start(f32[2,64,256]{2,1,0:T(8,128)} %constant.65.clone.cos_turn) | copy-start | bytes 393220
  2.3 19.8 %copy-start.22 = (f32[2,64,256]{2,1,0:T(8,128)S(1)}, f32[2,64,256]{2,1,0:T(8,128)}, u32[]{:S(2)}) copy-start(f32[2,64,256]{2,1,0:T(8,128)} %constant.66.clone.sin_turn) | copy-start | bytes 393220
  2.3 19.8 %copy-start.25 = (bf16[128,128]{1,0:T(8,128)(2,1)S(1)}, bf16[128,128]{1,0:T(8,128)(2,1)}, u32[]{:S(2)}) copy-start(bf16[128,128]{1,0:T(8,128)(2,1)} %constant.61.clone.slope_high) | copy-start | bytes 98308
  2.3 19.8 %copy-start.26 = (bf16[128,128]{1,0:T(8,128)(2,1)S(1)}, bf16[128,128]{1,0:T(8,128)(2,1)}, u32[]{:S(2)}) copy-start(bf16[128,128]{1,0:T(8,128)(2,1)} %constant.62.clone.slope_low) | copy-start | bytes 98308
  2.3 19.8 %copy-start.27 = (bf16[128,128]{1,0:T(8,128)(2,1)S(1)}, bf16[128,128]{1,0:T(8,128)(2,1)}, u32[]{:S(2)}) copy-start(bf16[128,128]{1,0:T(8,128)(2,1)} %constant.63.clone.lift_high) | copy-start | bytes 98308
  2.3 19.8 %copy-start.28 = (bf16[128,128]{1,0:T(8,128)(2,1)S(1)}, bf16[128,128]{1,0:T(8,128)(2,1)}, u32[]{:S(2)}) copy-start(bf16[128,128]{1,0:T(8,128)(2,1)} %constant.64.clone.lift_low) | copy-start | bytes 98308
  3.1 19.1 %copy-start = (bf16[256,512]{1,0:T(8,128)(2,1)S(1)}, bf16[256,512]{1,0:T(8,128)(2,1)}, u32[]{:S(2)}) copy-start(bf16[256,512]{1,0:T(8,128)(2,1)} %constant.67.clone.high) | copy-start | bytes 786436
  3.1 19.1 %copy-start.1 = (bf16[256,512]{1,0:T(8,128)(2,1)S(1)}, bf16[256,512]{1,0:T(8,128)(2,1)}, u32[]{:S(2)}) copy-start(bf16[256,512]{1,0:T(8,128)(2,1)} %constant.68.clone.low) | copy-start | bytes 786436
  3.1 19.0 %all-to-all-start = ((f32[8,32,256]{2,1,0:T(8,128)}), f32[8,32,256]{2,1,0:T(8,128)S(1)}, u32[]{:S(2)}, u32[]{:S(2)}) async-start(f32[8,32,256]{2,1,0:T(8,128)} %deal_kernel.1), calls=%async_computation | async-start | bytes 524288 | tf_op jit(solution)/shard_map/all_to_all | solution.py:420
  24.5 18.4 %copy-start.29 = (s32[64,2]{0,1:T(2,128)S(1)}, s32[64,2]{0,1:T(2,128)}, u32[]{:S(2)}) copy-start(s32[64,2]{0,1:T(2,128)} %param.31) | copy-start | bytes 1540
  24.5 35.6 %copy-start.16 = (bf16[256,512]{1,0:T(8,128)(2,1)S(1)}, bf16[256,512]{1,0:T(8,128)(2,1)}, u32[]{:S(2)}) copy-start(bf16[256,512]{1,0:T(8,128)(2,1)} %constant.72.clone.gather_low) | copy-start | bytes 786436
  24.5 35.6 %copy-start.17 = (f32[256,128]{1,0:T(8,128)S(1)}, f32[256,128]{1,0:T(8,128)}, u32[]{:S(2)}) copy-start(f32[256,128]{1,0:T(8,128)} %constant.69.clone.cos_turn) | copy-start | bytes 393220
  24.5 35.6 %copy-start.18 = (f32[256,128]{1,0:T(8,128)S(1)}, f32[256,128]{1,0:T(8,128)}, u32[]{:S(2)}) copy-start(f32[256,128]{1,0:T(8,128)} %constant.70.clone.sin_turn) | copy-start | bytes 393220
  24.5 35.6 %copy-start.19 = (bf16[256,256]{1,0:T(8,128)(2,1)S(1)}, bf16[256,256]{1,0:T(8,128)(2,1)}, u32[]{:S(2)}) copy-start(bf16[256,256]{1,0:T(8,128)(2,1)} %constant.75.clone.deal_high) | copy-start | bytes 393220
  24.5 35.6 %copy-start.20 = (bf16[256,256]{1,0:T(8,128)(2,1)S(1)}, bf16[256,256]{1,0:T(8,128)(2,1)}, u32[]{:S(2)}) copy-start(bf16[256,256]{1,0:T(8,128)(2,1)} %constant.76.clone.deal_low) | copy-start | bytes 393220
  24.5 35.6 %all-to-all-start.1 = ((f32[256,4,128]{2,1,0:T(4,128)}), f32[256,4,128]{2,1,0:T(4,128)S(1)}, u32[]{:S(2)}, u32[]{:S(2)}) async-start(f32[256,4,128]{2,1,0:T(4,128)} %bitcast.3), calls=%async_computation.1 | async-start | bytes 1048576 | tf_op jit(solution)/shard_map/all_to_all | solution.py:422
  61.9 27.3 %copy-start.6 = (f32[128,256]{1,0:T(8,128)S(1)}, f32[128,256]{1,0:T(8,128)}, u32[]{:S(2)}) copy-start(f32[128,256]{1,0:T(8,128)} %constant.79.clone.cos_zone) | copy-start | bytes 393220
  61.9 27.3 %copy-start.7 = (f32[128,256]{1,0:T(8,128)S(1)}, f32[128,256]{1,0:T(8,128)}, u32[]{:S(2)}) copy-start(f32[128,256]{1,0:T(8,128)} %constant.80.clone.sin_zone) | copy-start | bytes 393220
  62.0 27.3 %copy-start.8 = (bf16[256,256]{1,0:T(8,128)(2,1)S(1)}, bf16[256,256]{1,0:T(8,128)(2,1)}, u32[]{:S(2)}) copy-start(bf16[256,256]{1,0:T(8,128)(2,1)} %constant.81.clone.main_high) | copy-start | bytes 393220
  62.0 27.3 %copy-start.9 = (bf16[256,256]{1,0:T(8,128)(2,1)S(1)}, bf16[256,256]{1,0:T(8,128)(2,1)}, u32[]{:S(2)}) copy-start(bf16[256,256]{1,0:T(8,128)(2,1)} %constant.82.clone.main_low) | copy-start | bytes 393220
  62.0 27.3 %copy-start.10 = (bf16[128,512]{1,0:T(8,128)(2,1)S(1)}, bf16[128,512]{1,0:T(8,128)(2,1)}, u32[]{:S(2)}) copy-start(bf16[128,512]{1,0:T(8,128)(2,1)} %constant.83.clone.zone_high) | copy-start | bytes 393220
  62.0 27.3 %copy-start.11 = (bf16[128,512]{1,0:T(8,128)(2,1)S(1)}, bf16[128,512]{1,0:T(8,128)(2,1)}, u32[]{:S(2)}) copy-start(bf16[128,512]{1,0:T(8,128)(2,1)} %constant.84.clone.zone_low) | copy-start | bytes 393220
  62.0 27.3 %copy-start.12 = (f32[2,32,256]{2,1,0:T(8,128)S(1)}, f32[2,32,256]{2,1,0:T(8,128)}, u32[]{:S(2)}) copy-start(f32[2,32,256]{2,1,0:T(8,128)} %constant.77.clone.cos_main) | copy-start | bytes 196612
  62.0 27.3 %copy-start.13 = (f32[2,32,256]{2,1,0:T(8,128)S(1)}, f32[2,32,256]{2,1,0:T(8,128)}, u32[]{:S(2)}) copy-start(f32[2,32,256]{2,1,0:T(8,128)} %constant.78.clone.sin_main) | copy-start | bytes 196612
  (8 other events, 84.5 us)

commit v2 on v1

--- a/solution.py
+++ b/solution.py
@@ -138,13 +138,20 @@
     return jnp.where(index < 1024, index, index - 2048).astype(f32)
 
 
-def deal_kernel(eta, phi, out):
+def deal_kernel(eta, phi, out, done):
+    copies = []
     for z in range(4):
-        for source, base in ((eta, 0), (phi, 16)):
-            for a in range(2):
-                rows = source[a, 8 * z : 8 * z + 8, :]
-                for c in range(2):
-                    out[2 * z + c, base + 8 * a : base + 8 * a + 8, :] = rows
+        for k, source in enumerate((eta, phi)):
+            for c in range(2):
+                copies.append(
+                    pltpu.make_async_copy(
+                        source.at[:, 8 * z : 8 * z + 8, :], out.at[2 * z + c, k], done.at[len(copies)]
+                    )
+                )
+    for copy in copies:
+        copy.start()
+    for copy in copies:
+        copy.wait()
 
 
 def source_kernel(place, offsets, zone, out):
@@ -211,8 +218,7 @@
     words = real[:4] + imag[:4] + [real[4], imag[4], -imag[4], real[4]]
     result = dot3((high[...], low[...]), split(jnp.concatenate(words, 0)), ((1,), (1,)))
     for q in range(3):
-        out[pl.ds(q, 256, stride=4), :] = result[:, 128 * q : 128 * q + 128]
-    out[pl.ds(3, 256, stride=4), :] = jnp.zeros((256, 128), f32)
+        out[pl.ds(q, 256, stride=3), :] = result[:, 128 * q : 128 * q + 128]
 
 
 def columns_kernel(
@@ -231,7 +237,7 @@
     out,
 ):
     words = split(
-        jnp.concatenate([terms[pl.ds(q, 256, stride=4), :] for q in range(3)], 1)
+        jnp.concatenate([terms[pl.ds(q, 256, stride=3), :] for q in range(3)], 1)
     )
     with_cos = dot3((high[:, :256], low[:, :256]), words)
     with_sin = dot3((high[:, 256:], low[:, 256:]), words)
@@ -260,10 +266,9 @@
     first = both[:, :128]
     second = both[:, 128:]
     turned = jnp.concatenate([first * cosine + second * sine, second * cosine - first * sine], 0)
-    out[pl.ds(0, 256, stride=4), :] = dot3((high[...], low[...]), split(turned))
-    out[pl.ds(1, 256, stride=4), :] = source[:, :128]
-    out[pl.ds(2, 256, stride=4), :] = source[:, 128:]
-    out[pl.ds(3, 256, stride=4), :] = jnp.zeros((256, 128), f32)
+    out[pl.ds(0, 256, stride=3), :] = dot3((high[...], low[...]), split(turned))
+    out[pl.ds(1, 256, stride=3), :] = source[:, :128]
+    out[pl.ds(2, 256, stride=3), :] = source[:, 128:]
 
 
 def rows_back_kernel(
@@ -300,7 +305,7 @@
         edge = jnp.where(((row & 3) == 0) & (core == 0), edge, 0)
         beyond = lane < edge
         for a in range(2):
-            tile = terms[pl.ds(16 * t + 1 + a, 8, stride=4), :]
+            tile = terms[pl.ds(12 * t + 1 + a, 8, stride=3), :]
             cells[a].append(jnp.where(beyond, 0.0, tile))
             moved = jnp.where(beyond, tile, 0.0)
             ends[t : t + 1, 128 * a : 128 * a + 128] = moved[0:1, :]
@@ -320,7 +325,7 @@
     grid = (dot(near[0], where_to) + dot(near[1], where_to)) + (
         dot(far[0], last_to) + dot(far[1], last_to)
     )
-    main = terms[pl.ds(0, 256, stride=4), :].T
+    main = terms[pl.ds(0, 256, stride=3), :].T
     both = dot3(split(jnp.concatenate([main, grid], 0)), (high[...], low[...]))
 
     def turned(lines, cosine, sine):
@@ -383,7 +388,18 @@
 
 
 def stage_deal(eta, phi):
-    return call(deal_kernel, (8, 32, 256), [], [eta, phi])
+    anywhere = pl.BlockSpec(memory_space=pl.ANY)
+    dealt = pl.pallas_call(
+        deal_kernel,
+        out_shape=jax.ShapeDtypeStruct((8, 2, 2, 8, 256), f32),
+        in_specs=[anywhere, anywhere],
+        out_specs=anywhere,
+        scratch_shapes=[pltpu.SemaphoreType.DMA((16,))],
+        compiler_params=pltpu.CompilerParams(vmem_limit_bytes=56 * 1024 * 1024),
+        cost_estimate=pl.CostEstimate(flops=0, bytes_accessed=3 * 2**17, transcendentals=0),
+        name="deal_kernel",
+    )(eta, phi)
+    return dealt.reshape(8, 32, 256)
 
 
 def stage_source(place, offsets, zone):
@@ -393,13 +409,13 @@
 def stage_rows(place, modes):
     t = tables()
     constants = [*t["slope"], *t["lift"], *t["rows_turn"], *t["turn"]]
-    return call(rows_kernel, (1024, 128), [place], [modes, *constants], flops=2**30)
+    return call(rows_kernel, (768, 128), [place], [modes, *constants], flops=2**30)
 
 
 def stage_columns(terms, source):
     t = tables()
     constants = [*t["turn"], *t["y_turn"], *t["gather"], *t["gather_lift"], *t["deal"]]
-    return call(columns_kernel, (1024, 128), [], [terms, source, *constants], flops=2**30)
+    return call(columns_kernel, (768, 128), [], [terms, source, *constants], flops=2**30)
 
 
 def stage_rows_back(place, offsets, terms):
@@ -417,10 +433,14 @@
 def local(eta_modes, phi_modes, zone_field, offsets):
     place = jnp.stack([lax.axis_index(axis) for axis in ("wide", "lane", "core")]).astype(jnp.int32)
     swap = functools.partial(lax.all_to_all, split_axis=0, concat_axis=0, tiled=True)
+
+    def turn(words):
+        return swap(words.reshape(256, 1, 384), ("wide", "lane")).reshape(768, 128)
+
     modes = swap(stage_deal(eta_modes, phi_modes), ("lane", "core"))
     source = stage_source(place, offsets, zone_field)
-    columns = swap(stage_rows(place, modes), ("wide", "lane"))
-    rows = swap(stage_columns(columns, source), ("wide", "lane"))
+    columns = turn(stage_rows(place, modes))
+    rows = turn(stage_columns(columns, source))
     terms = swap(stage_rows_back(place, offsets, rows), ("lane", "core"))
     return tuple(stage_finish(place, terms, eta_modes, phi_modes))
 

time: 110 us -> 111 us (level)
  Pallas kernels: 10.3 us -> 18.7 us
  blocking collectives: 43 us -> 40.3 us
  waiting for transfers between devices: 23.6 us -> 21.3 us
  local copies, waits for them, and re-layouts: 2.56 us -> 0.9 us
    pallas_call x0 -> x1, Pallas kernels: none -> 9.19 us  [stage_deal(): pl.pallas_call(deal_kernel, out_shape=jax.ShapeDtypeStruct((8, 2, 2, 8, 2...]
    all_to_all x1, blocking collectives: 27.2 us -> 23.8 us  [turn(): return swap(words.reshape(256, 1, 384), ('wide', 'lane')).reshape(768, 128)]
    all_to_all x1, waiting for transfers between devices: 14.9 us -> 12.6 us  [turn(): return swap(words.reshape(256, 1, 384), ('wide', 'lane')).reshape(768, 128)]
    unnamed x61 -> x57, local copies, waits for them, and re-layouts: 2.56 us -> 0.9 us
    pallas_call x6 -> x5, Pallas kernels: 10.3 us -> 9.48 us  [call(): pl.pallas_call(kernel, out_shape=[jax.ShapeDtypeStruct(s, f32) for s in s...]
where the time goes in v2:
time: 111 us
  blocking collectives  40.3 us (36%)
  starting transfers between devices  28.7 us (26%)
  waiting for transfers between devices  21.3 us (19%)
  Pallas kernels  18.7 us (17%)
    all_to_all x1, blocking collectives, turn(): return swap(words.reshape(256, 1, 384), ('wide', 'lane')).reshape(768, 128)  23.8 us
    all_to_all x1, starting transfers between devices, turn(): return swap(words.reshape(256, 1, 384), ('wide', 'lane')).reshape(768, 128)  18.3 us
    all_to_all x1, blocking collectives, local(): terms = swap(stage_rows_back(place, offsets, rows), ('lane', 'core'))  16.4 us
    all_to_all x1, waiting for transfers between devices, turn(): return swap(words.reshape(256, 1, 384), ('wide', 'lane')).reshape(768, 128)  12.6 us
    all_to_all x1, starting transfers between devices, local(): modes = swap(stage_deal(eta_modes, phi_modes), ('lane', 'core'))  10.3 us
    pallas_call x5, Pallas kernels, call(): pl.pallas_call(kernel, out_shape=[jax.ShapeDtypeStruct(s, f32) for s in s...  9.48 us
    pallas_call x1, Pallas kernels, stage_deal(): pl.pallas_call(deal_kernel, out_shape=jax.ShapeDtypeStruct((8, 2, 2, 8, 2...  9.19 us
    all_to_all x1, waiting for transfers between devices, local(): modes = swap(stage_deal(eta_modes, phi_modes), ('lane', 'core'))  8.65 us
  transfers between devices with their start and end apart: 2, of which 2 were waited for; matrix products, arithmetic and copies ran while one was open for 0% of the time, Pallas kernels for 1%

profile of v2, /device:TPU:1, one launch (start us, length us, event | category | flops | bytes accessed | tf_op | source)
XLA Modules:
  0.0 110.8 jit_solution(8511400396691195644)
XLA Ops:
  0.6 0.0 copy-start.19
  0.6 0.0 copy-start.20
  0.7 0.0 copy-start.23
  0.7 0.0 copy-start.24
  0.7 0.0 copy-start.26
  0.7 9.2 %deal_kernel.1 = f32[8,2,2,8,256]{4,3,2,1,0:T(8,128)} custom-call(f32[2,32,256]{2,1,0:T(8,128)} %eta.3, f32[2,32,256]{2,1,0:T(8,128)} %phi.3), custom_call_target="tpu_custom_call" | custom-call | bytes 393216 | tf_op jit(solution)/shard_map/deal_kernel/pallas_call | solution.py:392
  9.9 0.0 copy-start.1
  9.9 10.3 %all-to-all-start = ((f32[8,32,256]{2,1,0:T(8,128)}), f32[8,32,256]{2,1,0:T(8,128)S(1)}, u32[]{:S(2)}, u32[]{:S(2)}) async-start(f32[8,32,256]{2,1,0:T(8,128)} %bitcast.11), calls=%async_computation | async-start | bytes 524288 | tf_op jit(solution)/shard_map/all_to_all | solution.py:440
  20.3 0.1 pad_add_fusion.place
  20.3 8.7 %all-to-all-done.modes = f32[8,32,256]{2,1,0:T(8,128)S(1)} async-done(((f32[8,32,256]{2,1,0:T(8,128)}), f32[8,32,256]{2,1,0:T(8,128)S(1)}, u32[]{:S(2)}, u32[]{:S(2)}) %all-to-all-start) | async-done | bytes 262176 | tf_op jit(solution)/shard_map/all_to_all | solution.py:440
  29.1 2.3 %rows_kernel.1 = f32[768,128]{1,0:T(8,128)} custom-call(s32[3]{0:T(128)S(1)} %pad_add_fusion.place, f32[8,32,256]{2,1,0:T(8,128)S(1)} %all-to-all-done.modes, bf16[128,128]{1,0:T(8,128)(2,1)S(1)} %copy-done.23, bf16[128,128]{1,0:T(8,128)(2,1)S(1)} %copy-done.24, bf16[128,128]{1,0:T(8,128)(2,1)S(1)} %copy-done.25, bf16[128,128]{1,0:T(8,128)(2,1)S(1)} %copy-done.26, ...), custom_call_target="tpu_custom_call" | custom-call | flops 1073741824 | bytes 1572864 | tf_op jit(solution)/shard_map/rows_kernel/pallas_call | solution.py:377
  31.4 0.0 copy-start.18
  31.4 18.3 %all-to-all-start.1 = ((f32[256,1,384]{2,1,0:T(1,128)}), f32[256,1,384]{2,1,0:T(1,128)S(1)}, u32[]{:S(2)}, u32[]{:S(2)}) async-start(f32[256,1,384]{2,1,0:T(1,128)} %bitcast.4), calls=%async_computation.1 | async-start | bytes 786432 | tf_op jit(solution)/shard_map/all_to_all | solution.py:438
  49.8 0.0 copy-start.13
  49.8 0.1 copy.35.offsets
  49.9 0.6 copy-done.12
  50.5 1.6 %source_kernel.1.source = f32[256,256]{1,0:T(8,128)S(1)} custom-call(s32[3]{0:T(128)S(1)} %pad_add_fusion.place, s32[64,2]{1,0:T(8,128)S(1)} %copy.35.offsets, f32[64,128]{1,0:T(8,128)S(1)} %copy-done.12), custom_call_target="tpu_custom_call" | custom-call | flops 67108864 | bytes 294912 | tf_op jit(solution)/shard_map/source_kernel/pallas_call | solution.py:377
  52.1 12.6 %all-to-all-done.1 = f32[256,1,384]{2,1,0:T(1,128)S(1)} async-done(((f32[256,1,384]{2,1,0:T(1,128)}), f32[256,1,384]{2,1,0:T(1,128)S(1)}, u32[]{:S(2)}, u32[]{:S(2)}) %all-to-all-start.1) | async-done | bytes 393248 | tf_op jit(solution)/shard_map/all_to_all | solution.py:438
  64.8 0.0 copy-start.11
  64.8 1.7 %columns_kernel.1 = f32[768,128]{1,0:T(8,128)S(1)} custom-call(f32[768,128]{1,0:T(8,128)S(1)} %bitcast.9, f32[256,256]{1,0:T(8,128)S(1)} %source_kernel.1.source, bf16[256,512]{1,0:T(8,128)(2,1)S(1)} %copy-done, bf16[256,512]{1,0:T(8,128)(2,1)S(1)} %copy-done.1, f32[256,128]{1,0:T(8,128)S(1)} %copy-done.15, f32[256,128]{1,0:T(8,128)S(1)} %copy-done.16, ...), custom_call_target="tpu_custom_call" | custom-call | flops 1073741824 | bytes 2686976 | tf_op jit(solution)/shard_map/columns_kernel/pallas_call | solution.py:377
  66.5 23.8 %all_to_all.20 = f32[256,1,384]{2,1,0:T(1,128)S(1)} all-to-all(f32[256,1,384]{2,1,0:T(1,128)S(1)} %bitcast.10), channel_id=1, replica_groups=mesh['wide'=64,'lane'=4,'core'=2] {'wide','lane'}, dimensions={0} | all-to-all | bytes 786432 | tf_op jit(solution)/shard_map/all_to_all | solution.py:438
  90.4 2.7 %rows_back_kernel.1 = f32[8,32,256]{2,1,0:T(8,128)S(1)} custom-call(s32[3]{0:T(128)S(1)} %pad_add_fusion.place, s32[64,2]{1,0:T(8,128)S(1)} %copy.35.offsets, f32[768,128]{1,0:T(8,128)S(1)} %bitcast.8, bf16[256,512]{1,0:T(8,128)(2,1)S(1)} %copy-done, bf16[256,512]{1,0:T(8,128)(2,1)S(1)} %copy-done.1, f32[2,32,256]{2,1,0:T(8,128)S(1)} %copy-done.10, ...), custom_call_target="tpu_custom_call" | custom-call | flops 536870912 | bytes 2097152 | tf_op jit(solution)/shard_map/rows_back_kernel/pallas_call | solution.py:377
  93.2 16.4 %all_to_all.21.terms = f32[8,32,256]{2,1,0:T(8,128)S(1)} all-to-all(f32[8,32,256]{2,1,0:T(8,128)S(1)} %rows_back_kernel.1), channel_id=1, replica_groups=mesh['wide'=64,'lane'=4,'core'=2] {'lane','core'}, dimensions={0} | all-to-all | bytes 524288 | tf_op jit(solution)/shard_map/all_to_all | solution.py:444
  109.6 1.2 %finish_kernel.1 = (f32[2,32,256]{2,1,0:T(8,128)}, f32[2,32,256]{2,1,0:T(8,128)}) custom-call(s32[3]{0:T(128)S(1)} %pad_add_fusion.place, f32[8,32,256]{2,1,0:T(8,128)S(1)} %all_to_all.21.terms, f32[2,32,256]{2,1,0:T(8,128)S(1)} %copy-done.2, f32[2,32,256]{2,1,0:T(8,128)S(1)} %copy-done.3), custom_call_target="tpu_custom_call" | custom-call | bytes 524288 | tf_op jit(solution)/shard_map/finish_kernel/pallas_call | solution.py:377
  (46 shorter events, 0.1 us)
Async XLA Ops:
  0.6 28.4 %copy-start.19 = (f32[2,64,256]{2,1,0:T(8,128)S(1)}, f32[2,64,256]{2,1,0:T(8,128)}, u32[]{:S(2)}) copy-start(f32[2,64,256]{2,1,0:T(8,128)} %constant.65.clone.cos_turn) | copy-start | bytes 393220
  0.6 28.3 %copy-start.20 = (f32[2,64,256]{2,1,0:T(8,128)S(1)}, f32[2,64,256]{2,1,0:T(8,128)}, u32[]{:S(2)}) copy-start(f32[2,64,256]{2,1,0:T(8,128)} %constant.66.clone.sin_turn) | copy-start | bytes 393220
  0.7 28.3 %copy-start.23 = (bf16[128,128]{1,0:T(8,128)(2,1)S(1)}, bf16[128,128]{1,0:T(8,128)(2,1)}, u32[]{:S(2)}) copy-start(bf16[128,128]{1,0:T(8,128)(2,1)} %constant.61.clone.slope_high) | copy-start | bytes 98308
  0.7 28.3 %copy-start.24 = (bf16[128,128]{1,0:T(8,128)(2,1)S(1)}, bf16[128,128]{1,0:T(8,128)(2,1)}, u32[]{:S(2)}) copy-start(bf16[128,128]{1,0:T(8,128)(2,1)} %constant.62.clone.slope_low) | copy-start | bytes 98308
  0.7 28.3 %copy-start.25 = (bf16[128,128]{1,0:T(8,128)(2,1)S(1)}, bf16[128,128]{1,0:T(8,128)(2,1)}, u32[]{:S(2)}) copy-start(bf16[128,128]{1,0:T(8,128)(2,1)} %constant.63.clone.lift_high) | copy-start | bytes 98308
  0.7 28.3 %copy-start.26 = (bf16[128,128]{1,0:T(8,128)(2,1)S(1)}, bf16[128,128]{1,0:T(8,128)(2,1)}, u32[]{:S(2)}) copy-start(bf16[128,128]{1,0:T(8,128)(2,1)} %constant.64.clone.lift_low) | copy-start | bytes 98308
  9.9 19.1 %copy-start = (bf16[256,512]{1,0:T(8,128)(2,1)S(1)}, bf16[256,512]{1,0:T(8,128)(2,1)}, u32[]{:S(2)}) copy-start(bf16[256,512]{1,0:T(8,128)(2,1)} %constant.67.clone.high) | copy-start | bytes 786436
  9.9 19.1 %copy-start.1 = (bf16[256,512]{1,0:T(8,128)(2,1)S(1)}, bf16[256,512]{1,0:T(8,128)(2,1)}, u32[]{:S(2)}) copy-start(bf16[256,512]{1,0:T(8,128)(2,1)} %constant.68.clone.low) | copy-start | bytes 786436
  9.9 19.1 %all-to-all-start = ((f32[8,32,256]{2,1,0:T(8,128)}), f32[8,32,256]{2,1,0:T(8,128)S(1)}, u32[]{:S(2)}, u32[]{:S(2)}) async-start(f32[8,32,256]{2,1,0:T(8,128)} %bitcast.11), calls=%async_computation | async-start | bytes 524288 | tf_op jit(solution)/shard_map/all_to_all | solution.py:440
  29.0 20.7 %copy-start.27 = (s32[64,2]{0,1:T(2,128)S(1)}, s32[64,2]{0,1:T(2,128)}, u32[]{:S(2)}) copy-start(s32[64,2]{0,1:T(2,128)} %param.31) | copy-start | bytes 1540
  31.4 33.3 %copy-start.14 = (bf16[256,512]{1,0:T(8,128)(2,1)S(1)}, bf16[256,512]{1,0:T(8,128)(2,1)}, u32[]{:S(2)}) copy-start(bf16[256,512]{1,0:T(8,128)(2,1)} %constant.72.clone.gather_low) | copy-start | bytes 786436
  31.4 33.3 %copy-start.15 = (f32[256,128]{1,0:T(8,128)S(1)}, f32[256,128]{1,0:T(8,128)}, u32[]{:S(2)}) copy-start(f32[256,128]{1,0:T(8,128)} %constant.69.clone.cos_turn) | copy-start | bytes 393220
  31.4 33.3 %copy-start.16 = (f32[256,128]{1,0:T(8,128)S(1)}, f32[256,128]{1,0:T(8,128)}, u32[]{:S(2)}) copy-start(f32[256,128]{1,0:T(8,128)} %constant.70.clone.sin_turn) | copy-start | bytes 393220
  31.4 33.3 %copy-start.17 = (bf16[256,256]{1,0:T(8,128)(2,1)S(1)}, bf16[256,256]{1,0:T(8,128)(2,1)}, u32[]{:S(2)}) copy-start(bf16[256,256]{1,0:T(8,128)(2,1)} %constant.75.clone.deal_high) | copy-start | bytes 393220
  31.4 33.3 %copy-start.18 = (bf16[256,256]{1,0:T(8,128)(2,1)S(1)}, bf16[256,256]{1,0:T(8,128)(2,1)}, u32[]{:S(2)}) copy-start(bf16[256,256]{1,0:T(8,128)(2,1)} %constant.76.clone.deal_low) | copy-start | bytes 393220
  31.4 33.3 %all-to-all-start.1 = ((f32[256,1,384]{2,1,0:T(1,128)}), f32[256,1,384]{2,1,0:T(1,128)S(1)}, u32[]{:S(2)}, u32[]{:S(2)}) async-start(f32[256,1,384]{2,1,0:T(1,128)} %bitcast.4), calls=%async_computation.1 | async-start | bytes 786432 | tf_op jit(solution)/shard_map/all_to_all | solution.py:438
  64.8 25.6 %copy-start.10 = (f32[2,32,256]{2,1,0:T(8,128)S(1)}, f32[2,32,256]{2,1,0:T(8,128)}, u32[]{:S(2)}) copy-start(f32[2,32,256]{2,1,0:T(8,128)} %constant.77.clone.cos_main) | copy-start | bytes 196612
  64.8 25.6 %copy-start.11 = (f32[2,32,256]{2,1,0:T(8,128)S(1)}, f32[2,32,256]{2,1,0:T(8,128)}, u32[]{:S(2)}) copy-start(f32[2,32,256]{2,1,0:T(8,128)} %constant.78.clone.sin_main) | copy-start | bytes 196612
  66.5 23.9 %copy-start.4 = (f32[128,256]{1,0:T(8,128)S(1)}, f32[128,256]{1,0:T(8,128)}, u32[]{:S(2)}) copy-start(f32[128,256]{1,0:T(8,128)} %constant.79.clone.cos_zone) | copy-start | bytes 393220
  66.5 23.9 %copy-start.5 = (f32[128,256]{1,0:T(8,128)S(1)}, f32[128,256]{1,0:T(8,128)}, u32[]{:S(2)}) copy-start(f32[128,256]{1,0:T(8,128)} %constant.80.clone.sin_zone) | copy-start | bytes 393220
  66.5 23.9 %copy-start.6 = (bf16[256,256]{1,0:T(8,128)(2,1)S(1)}, bf16[256,256]{1,0:T(8,128)(2,1)}, u32[]{:S(2)}) copy-start(bf16[256,256]{1,0:T(8,128)(2,1)} %constant.81.clone.main_high) | copy-start | bytes 393220
  66.5 23.9 %copy-start.7 = (bf16[256,256]{1,0:T(8,128)(2,1)S(1)}, bf16[256,256]{1,0:T(8,128)(2,1)}, u32[]{:S(2)}) copy-start(bf16[256,256]{1,0:T(8,128)(2,1)} %constant.82.clone.main_low) | copy-start | bytes 393220
  66.5 23.9 %copy-start.8 = (bf16[128,512]{1,0:T(8,128)(2,1)S(1)}, bf16[128,512]{1,0:T(8,128)(2,1)}, u32[]{:S(2)}) copy-start(bf16[128,512]{1,0:T(8,128)(2,1)} %constant.83.clone.zone_high) | copy-start | bytes 393220
  66.5 23.9 %copy-start.9 = (bf16[128,512]{1,0:T(8,128)(2,1)S(1)}, bf16[128,512]{1,0:T(8,128)(2,1)}, u32[]{:S(2)}) copy-start(bf16[128,512]{1,0:T(8,128)(2,1)} %constant.84.clone.zone_low) | copy-start | bytes 393220
  (6 other events, 77.1 us)

commit v3 on v1

--- a/solution.py
+++ b/solution.py
@@ -22,7 +22,6 @@
 zone_scale = 1.0 / math.sqrt(4096 * 128)
 f32 = jnp.float32
 bf16 = jnp.bfloat16
-VMEM_LIMIT = 24 * 1024 * 1024
 
 
 def part(value, which):
@@ -143,8 +142,7 @@
         for source, base in ((eta, 0), (phi, 16)):
             for a in range(2):
                 rows = source[a, 8 * z : 8 * z + 8, :]
-                for c in range(2):
-                    out[2 * z + c, base + 8 * a : base + 8 * a + 8, :] = rows
+                out[z, base + 8 * a : base + 8 * a + 8, :] = rows
 
 
 def source_kernel(place, offsets, zone, out):
@@ -171,7 +169,7 @@
 
 
 def rows_kernel(
-    place, modes, slope_high, slope_low, lift_high, lift_low, cos_turn, sin_turn, high, low, out
+    place, own, other, slope_high, slope_low, lift_high, lift_low, cos_turn, sin_turn, high, low, out
 ):
     first_ky = 32 * place[0] + 8 * place[1]
     core = place[2]
@@ -181,8 +179,10 @@
     for n in range(8):
         wave_x = wave_of(256 * n + iota((16, 256), 1)) * TURN_X
         kappa = jnp.sqrt(wave_x * wave_x + wave_y * wave_y)
-        eta = modes[n, 0:16, :]
-        phi = modes[n, 16:32, :]
+        mine, theirs = (own, other) if n % 2 == 0 else (other, own)
+        z = n // 2
+        eta = jnp.where(core == 0, mine[z, 0:16, :], theirs[z, 0:16, :])
+        phi = jnp.where(core == 0, mine[z, 16:32, :], theirs[z, 16:32, :])
         if n % 2:
             eta = eta * odd
             phi = phi * odd
@@ -211,8 +211,7 @@
     words = real[:4] + imag[:4] + [real[4], imag[4], -imag[4], real[4]]
     result = dot3((high[...], low[...]), split(jnp.concatenate(words, 0)), ((1,), (1,)))
     for q in range(3):
-        out[pl.ds(q, 256, stride=4), :] = result[:, 128 * q : 128 * q + 128]
-    out[pl.ds(3, 256, stride=4), :] = jnp.zeros((256, 128), f32)
+        out[pl.ds(q, 256, stride=3), :] = result[:, 128 * q : 128 * q + 128]
 
 
 def columns_kernel(
@@ -231,7 +230,7 @@
     out,
 ):
     words = split(
-        jnp.concatenate([terms[pl.ds(q, 256, stride=4), :] for q in range(3)], 1)
+        jnp.concatenate([terms[pl.ds(q, 256, stride=3), :] for q in range(3)], 1)
     )
     with_cos = dot3((high[:, :256], low[:, :256]), words)
     with_sin = dot3((high[:, 256:], low[:, 256:]), words)
@@ -260,10 +259,9 @@
     first = both[:, :128]
     second = both[:, 128:]
     turned = jnp.concatenate([first * cosine + second * sine, second * cosine - first * sine], 0)
-    out[pl.ds(0, 256, stride=4), :] = dot3((high[...], low[...]), split(turned))
-    out[pl.ds(1, 256, stride=4), :] = source[:, :128]
-    out[pl.ds(2, 256, stride=4), :] = source[:, 128:]
-    out[pl.ds(3, 256, stride=4), :] = jnp.zeros((256, 128), f32)
+    out[pl.ds(0, 256, stride=3), :] = dot3((high[...], low[...]), split(turned))
+    out[pl.ds(1, 256, stride=3), :] = source[:, :128]
+    out[pl.ds(2, 256, stride=3), :] = source[:, 128:]
 
 
 def rows_back_kernel(
@@ -281,6 +279,7 @@
     zone_high,
     zone_low,
     out,
+    away,
     ends,
 ):
     core = place[2]
@@ -300,7 +299,7 @@
         edge = jnp.where(((row & 3) == 0) & (core == 0), edge, 0)
         beyond = lane < edge
         for a in range(2):
-            tile = terms[pl.ds(16 * t + 1 + a, 8, stride=4), :]
+            tile = terms[pl.ds(12 * t + 1 + a, 8, stride=3), :]
             cells[a].append(jnp.where(beyond, 0.0, tile))
             moved = jnp.where(beyond, tile, 0.0)
             ends[t : t + 1, 128 * a : 128 * a + 128] = moved[0:1, :]
@@ -320,7 +319,7 @@
     grid = (dot(near[0], where_to) + dot(near[1], where_to)) + (
         dot(far[0], last_to) + dot(far[1], last_to)
     )
-    main = terms[pl.ds(0, 256, stride=4), :].T
+    main = terms[pl.ds(0, 256, stride=3), :].T
     both = dot3(split(jnp.concatenate([main, grid], 0)), (high[...], low[...]))
 
     def turned(lines, cosine, sine):
@@ -338,12 +337,17 @@
     main = dot3((main_high[...], main_low[...]), main)
     zone = dot3((zone_high[...], zone_low[...]), zone)
     odd = 1.0 - 2.0 * core.astype(f32)
+    blocks = []
     for n in range(8):
         block = main[32 * n : 32 * n + 32]
         if n % 2:
             block = block * odd
-        out[n, 0:16, :] = block[:16] + zone[16 * n : 16 * n + 16]
-        out[n, 16:32, :] = block[16:]
+        blocks.append(
+            jnp.concatenate([block[:16] + zone[16 * n : 16 * n + 16], block[16:]], 0)
+        )
+    for z in range(4):
+        out[z] = jnp.where(core == 0, blocks[2 * z], blocks[2 * z + 1])
+        away[z] = jnp.where(core == 0, blocks[2 * z + 1], blocks[2 * z])
 
 
 def finish_kernel(place, terms, eta, phi, eta_next, phi_next):
@@ -356,14 +360,13 @@
             surface = eta[a, rows, :]
             potential = phi[a, rows, :]
             part_of = slice(8 * a, 8 * a + 8)
-            added = terms[2 * z, part_of, :] + terms[2 * z + 1, part_of, :]
-            eta_next[a, rows, :] = surface + kappa * potential + added
+            eta_next[a, rows, :] = surface + kappa * potential + terms[z, part_of, :]
             part_of = slice(16 + 8 * a, 24 + 8 * a)
-            added = terms[2 * z, part_of, :] + terms[2 * z + 1, part_of, :]
-            phi_next[a, rows, :] = potential - (time_step * gravity) * surface + added
-
-
-def call(kernel, shapes, scalars, arrays, scratch=(), flops=0):
+            linear = potential - (time_step * gravity) * surface
+            phi_next[a, rows, :] = linear + terms[z, part_of, :]
+
+
+def call(kernel, shapes, scalars, arrays, scratch=(), flops=0, limit=24):
     single = isinstance(shapes, tuple)
     shapes = [shapes] if single else shapes
     vmem = pl.BlockSpec(memory_space=pltpu.VMEM)
@@ -375,7 +378,7 @@
         in_specs=[smem] * len(scalars) + [vmem] * len(arrays),
         out_specs=[vmem] * len(shapes),
         scratch_shapes=list(scratch),
-        compiler_params=pltpu.CompilerParams(vmem_limit_bytes=VMEM_LIMIT),
+        compiler_params=pltpu.CompilerParams(vmem_limit_bytes=limit * 1024 * 1024),
         cost_estimate=pl.CostEstimate(flops=flops, bytes_accessed=moved, transcendentals=0),
         name=kernel.__name__,
     )(*scalars, *arrays)
@@ -383,23 +386,23 @@
 
 
 def stage_deal(eta, phi):
-    return call(deal_kernel, (8, 32, 256), [], [eta, phi])
+    return call(deal_kernel, (4, 32, 256), [], [eta, phi], limit=56)
 
 
 def stage_source(place, offsets, zone):
     return call(source_kernel, (256, 256), [place, offsets], [zone], flops=2**26)
 
 
-def stage_rows(place, modes):
+def stage_rows(place, own, other):
     t = tables()
     constants = [*t["slope"], *t["lift"], *t["rows_turn"], *t["turn"]]
-    return call(rows_kernel, (1024, 128), [place], [modes, *constants], flops=2**30)
+    return call(rows_kernel, (768, 128), [place], [own, other, *constants], flops=2**30)
 
 
 def stage_columns(terms, source):
     t = tables()
     constants = [*t["turn"], *t["y_turn"], *t["gather"], *t["gather_lift"], *t["deal"]]
-    return call(columns_kernel, (1024, 128), [], [terms, source, *constants], flops=2**30)
+    return call(columns_kernel, (768, 128), [], [terms, source, *constants], flops=2**30)
 
 
 def stage_rows_back(place, offsets, terms):
@@ -407,7 +410,7 @@
     constants = [*t["turn"], *t["main_turn"], *t["zone_turn"], *t["main_mix"], *t["zone_mix"]]
     scratch = [pltpu.VMEM((64, 256), f32)]
     arrays = [terms, *constants]
-    return call(rows_back_kernel, (8, 32, 256), [place, offsets], arrays, scratch, flops=2**29)
+    return call(rows_back_kernel, [(4, 32, 256)] * 2, [place, offsets], arrays, scratch, flops=2**29)
 
 
 def stage_finish(place, terms, eta, phi):
@@ -417,11 +420,20 @@
 def local(eta_modes, phi_modes, zone_field, offsets):
     place = jnp.stack([lax.axis_index(axis) for axis in ("wide", "lane", "core")]).astype(jnp.int32)
     swap = functools.partial(lax.all_to_all, split_axis=0, concat_axis=0, tiled=True)
-    modes = swap(stage_deal(eta_modes, phi_modes), ("lane", "core"))
+
+    def turn(words):
+        return swap(words.reshape(256, 1, 384), ("wide", "lane")).reshape(768, 128)
+
+    def across(rows):
+        return lax.ppermute(rows, "core", [(0, 1), (1, 0)])
+
+    own = swap(stage_deal(eta_modes, phi_modes), "lane")
     source = stage_source(place, offsets, zone_field)
-    columns = swap(stage_rows(place, modes), ("wide", "lane"))
-    rows = swap(stage_columns(columns, source), ("wide", "lane"))
-    terms = swap(stage_rows_back(place, offsets, rows), ("lane", "core"))
+    own, source = lax.optimization_barrier((own, source))
+    columns = turn(stage_rows(place, own, across(own)))
+    rows = turn(stage_columns(columns, source))
+    share, away = stage_rows_back(place, offsets, rows)
+    terms = swap(share + across(away), "lane")
     return tuple(stage_finish(place, terms, eta_modes, phi_modes))
 
 

time: 110 us -> 103 us (0.936)
  blocking collectives: 43 us -> 65.6 us
  waiting for transfers between devices: 23.6 us -> 4.36 us
  starting transfers between devices: 28.7 us -> 19.9 us
    all_to_all x2 -> x3, blocking collectives: 43 us -> 65.6 us  [the longest x2 58.2 us: turn(): return swap(words.reshape(256, 1, 384), ('wide', 'lane')).reshape(768, 128)]
    all_to_all x2 -> x1, waiting for transfers between devices: 23.6 us -> 2.43 us  [local(): own = swap(stage_deal(eta_modes, phi_modes), 'lane')]
    all_to_all x2 -> x1, starting transfers between devices: 28.7 us -> 7.94 us  [local(): own = swap(stage_deal(eta_modes, phi_modes), 'lane')]
    ppermute x0 -> x2, starting transfers between devices: none -> 11.9 us  [across(): return lax.ppermute(rows, 'core', [(0, 1), (1, 0)])]
    ppermute x0 -> x2, waiting for transfers between devices: none -> 1.93 us  [across(): return lax.ppermute(rows, 'core', [(0, 1), (1, 0)])]
    unnamed x61 -> x57, local copies, waits for them, and re-layouts: 2.56 us -> 1.58 us
  transfers between devices with their start and end apart: 2 -> 3, of which waited for: 2 -> 3; matrix products, arithmetic and copies ran while one was open for 0% -> 0% of each run, Pallas kernels for 1% -> 2%
where the time goes in v3:
time: 103 us
  blocking collectives  65.6 us (64%)
  starting transfers between devices  19.9 us (19%)
  Pallas kernels  10.3 us (10%)
  waiting for transfers between devices  4.36 us (4%)
  local copies, waits for them, and re-layouts  1.58 us (2%)
    all_to_all x2, blocking collectives, turn(): return swap(words.reshape(256, 1, 384), ('wide', 'lane')).reshape(768, 128)  58.2 us
    ppermute x2, starting transfers between devices, across(): return lax.ppermute(rows, 'core', [(0, 1), (1, 0)])  11.9 us
    pallas_call x6, Pallas kernels, call(): pl.pallas_call(kernel, out_shape=[jax.ShapeDtypeStruct(s, f32) for s in s...  10.3 us
    all_to_all x1, starting transfers between devices, local(): own = swap(stage_deal(eta_modes, phi_modes), 'lane')  7.94 us
    all_to_all x1, blocking collectives, local(): terms = swap(share + across(away), 'lane')  7.4 us
    all_to_all x1, waiting for transfers between devices, local(): own = swap(stage_deal(eta_modes, phi_modes), 'lane')  2.43 us
  transfers between devices with their start and end apart: 3, of which 3 were waited for; matrix products, arithmetic and copies ran while one was open for 0% of the time, Pallas kernels for 2%

profile of v3, /device:TPU:1, one launch (start us, length us, event | category | flops | bytes accessed | tf_op | source)
XLA Modules:
  0.0 102.8 jit_solution(6027320834390215864)
XLA Ops:
  0.7 0.0 copy-start.17
  0.7 0.0 copy-start.18
  0.7 1.6 %deal_kernel.1 = f32[4,32,256]{2,1,0:T(8,128)} custom-call(f32[2,32,256]{2,1,0:T(8,128)} %eta.3, f32[2,32,256]{2,1,0:T(8,128)} %phi.3), custom_call_target="tpu_custom_call" | custom-call | bytes 262144 | tf_op jit(solution)/shard_map/deal_kernel/pallas_call | solution.py:375
  2.3 7.9 %all-to-all-start = ((f32[4,32,256]{2,1,0:T(8,128)}), f32[4,32,256]{2,1,0:T(8,128)S(1)}, u32[]{:S(2)}, u32[]{:S(2)}) async-start(f32[4,32,256]{2,1,0:T(8,128)} %deal_kernel.1), calls=%async_computation | async-start | bytes 262144 | tf_op jit(solution)/shard_map/all_to_all | solution.py:430
  10.2 0.1 copy.35.offsets
  10.3 0.1 pad_add_fusion.place
  10.4 0.6 copy-done.2
  11.0 1.6 %source_kernel.1.source = f32[256,256]{1,0:T(8,128)S(1)} custom-call(s32[3]{0:T(128)S(1)} %pad_add_fusion.place, s32[64,2]{1,0:T(8,128)S(1)} %copy.35.offsets, f32[64,128]{1,0:T(8,128)S(1)} %copy-done.2), custom_call_target="tpu_custom_call" | custom-call | flops 67108864 | bytes 294912 | tf_op jit(solution)/shard_map/source_kernel/pallas_call | solution.py:375
  12.5 2.4 %all-to-all-done.own = f32[4,32,256]{2,1,0:T(8,128)S(1)} async-done(((f32[4,32,256]{2,1,0:T(8,128)}), f32[4,32,256]{2,1,0:T(8,128)S(1)}, u32[]{:S(2)}, u32[]{:S(2)}) %all-to-all-start) | async-done | bytes 131104 | tf_op jit(solution)/shard_map/all_to_all | solution.py:430
  15.0 5.4 %collective-permute-start = (f32[4,32,256]{2,1,0:T(8,128)S(1)}, f32[4,32,256]{2,1,0:T(8,128)S(1)}, u32[]{:S(2)}, u32[]{:S(2)}) collective-permute-start(f32[4,32,256]{2,1,0:T(8,128)S(1)} %all-to-all-done.own), channel_id=1, source_target_pairs={{0,1},{1,0},{2,3},{3,2},{4,5},{5,4},{6,7},{7,6},{8,9},{9,8},{10,11... | collective-permute-start | bytes 393224 | tf_op jit(solution)/shard_map/ppermute | solution.py:428
  20.4 1.0 collective-permute-done.other
  21.4 0.0 copy-start.26
  21.4 0.7 copy-done.26
  22.2 1.5 %rows_kernel.1 = f32[768,128]{1,0:T(8,128)S(1)} custom-call(s32[3]{0:T(128)S(1)} %pad_add_fusion.place, f32[4,32,256]{2,1,0:T(8,128)S(1)} %all-to-all-done.own, f32[4,32,256]{2,1,0:T(8,128)S(1)} %collective-permute-done.other, bf16[128,128]{1,0:T(8,128)(2,1)S(1)} %copy-done.26, bf16[128,128]{1,0:T(8,128)(2,1)S(1)} %copy-done.25, ...), custom_call_target="tpu_custom_call" | custom-call | flops 1073741824 | bytes 1572864 | tf_op jit(solution)/shard_map/rows_kernel/pallas_call | solution.py:375
  23.7 0.0 copy-start.5
  23.7 0.0 copy-start.6
  23.8 33.9 %all_to_all.20 = f32[256,1,384]{2,1,0:T(1,128)S(1)} all-to-all(f32[256,1,384]{2,1,0:T(1,128)S(1)} %bitcast.10), channel_id=1, replica_groups=mesh['wide'=64,'lane'=4,'core'=2] {'wide','lane'}, dimensions={0} | all-to-all | bytes 786432 | tf_op jit(solution)/shard_map/all_to_all | solution.py:425
  57.8 1.7 %columns_kernel.1 = f32[768,128]{1,0:T(8,128)S(1)} custom-call(f32[768,128]{1,0:T(8,128)S(1)} %bitcast.8, f32[256,256]{1,0:T(8,128)S(1)} %source_kernel.1.source, bf16[256,512]{1,0:T(8,128)(2,1)S(1)} %copy-done.4, bf16[256,512]{1,0:T(8,128)(2,1)S(1)} %copy-done.3, f32[256,128]{1,0:T(8,128)S(1)} %copy-done.16, f32[256,128]{1,0:T(8,128)S(1)} %copy-done.15, ...), custom_call_target="tpu_custom_call" | custom-call | flops 1073741824 | bytes 2686976 | tf_op jit(solution)/shard_map/columns_kernel/pallas_call | solution.py:375
  59.5 24.3 %all_to_all.21 = f32[256,1,384]{2,1,0:T(1,128)S(1)} all-to-all(f32[256,1,384]{2,1,0:T(1,128)S(1)} %bitcast.9), channel_id=1, replica_groups=mesh['wide'=64,'lane'=4,'core'=2] {'wide','lane'}, dimensions={0} | all-to-all | bytes 786432 | tf_op jit(solution)/shard_map/all_to_all | solution.py:425
  83.9 2.7 %rows_back_kernel.1 = (f32[4,32,256]{2,1,0:T(8,128)S(1)}, f32[4,32,256]{2,1,0:T(8,128)S(1)}) custom-call(s32[3]{0:T(128)S(1)} %pad_add_fusion.place, s32[64,2]{1,0:T(8,128)S(1)} %copy.35.offsets, f32[768,128]{1,0:T(8,128)S(1)} %bitcast.7, bf16[256,512]{1,0:T(8,128)(2,1)S(1)} %copy-done.4, bf16[256,512]{1,0:T(8,128)(2,1)S(1)} %copy-done.3, ...), custom_call_target="tpu_custom_call" | custom-call | flops 536870912 | bytes 2097152 | tf_op jit(solution)/shard_map/rows_back_kernel/pallas_call | solution.py:375
  86.6 6.5 %collective-permute-start.1 = (f32[4,32,256]{2,1,0:T(8,128)S(1)}, f32[4,32,256]{2,1,0:T(8,128)S(1)}, u32[]{:S(2)}, u32[]{:S(2)}) collective-permute-start(f32[4,32,256]{2,1,0:T(8,128)S(1)} %get-tuple-element.9), channel_id=1, source_target_pairs={{0,1},{1,0},{2,3},{3,2},{4,5},{5,4},{6,7},{7,6},{8,9},{9,8},{10,11... | collective-permute-start | bytes 393224 | tf_op jit(solution)/shard_map/ppermute | solution.py:428
  93.2 1.0 collective-permute-done.1
  94.2 7.4 %all_to_all.22.terms = f32[4,32,256]{2,1,0:T(8,128)S(1)} all-to-all(f32[4,32,256]{2,1,0:T(8,128)S(1)} %add.3), channel_id=1, replica_groups=mesh['wide'=64,'lane'=4,'core'=2] {'lane'}, dimensions={0} | all-to-all | bytes 262144 | tf_op jit(solution)/shard_map/all_to_all | solution.py:436
  101.6 1.2 %finish_kernel.1 = (f32[2,32,256]{2,1,0:T(8,128)}, f32[2,32,256]{2,1,0:T(8,128)}) custom-call(s32[3]{0:T(128)S(1)} %pad_add_fusion.place, f32[4,32,256]{2,1,0:T(8,128)S(1)} %all_to_all.22.terms, f32[2,32,256]{2,1,0:T(8,128)S(1)} %copy-done, f32[2,32,256]{2,1,0:T(8,128)S(1)} %copy-done.1), custom_call_target="tpu_custom_call" | custom-call | bytes 393216 | tf_op jit(solution)/shard_map/finish_kernel/pallas_call | solution.py:375
  (50 shorter events, 0.1 us)
Async XLA Ops:
  0.6 20.7 %copy-start.25 = (bf16[128,128]{1,0:T(8,128)(2,1)S(1)}, bf16[128,128]{1,0:T(8,128)(2,1)}, u32[]{:S(2)}) copy-start(bf16[128,128]{1,0:T(8,128)(2,1)} %constant.62.clone.slope_low) | copy-start | bytes 98308
  0.7 20.7 %copy-start.17 = (f32[2,64,256]{2,1,0:T(8,128)S(1)}, f32[2,64,256]{2,1,0:T(8,128)}, u32[]{:S(2)}) copy-start(f32[2,64,256]{2,1,0:T(8,128)} %constant.66.clone.sin_turn) | copy-start | bytes 393220
  0.7 20.7 %copy-start.18 = (f32[2,64,256]{2,1,0:T(8,128)S(1)}, f32[2,64,256]{2,1,0:T(8,128)}, u32[]{:S(2)}) copy-start(f32[2,64,256]{2,1,0:T(8,128)} %constant.65.clone.cos_turn) | copy-start | bytes 393220
  2.3 19.1 %copy-start.3 = (bf16[256,512]{1,0:T(8,128)(2,1)S(1)}, bf16[256,512]{1,0:T(8,128)(2,1)}, u32[]{:S(2)}) copy-start(bf16[256,512]{1,0:T(8,128)(2,1)} %constant.68.clone.low) | copy-start | bytes 786436
  2.3 12.7 %all-to-all-start = ((f32[4,32,256]{2,1,0:T(8,128)}), f32[4,32,256]{2,1,0:T(8,128)S(1)}, u32[]{:S(2)}, u32[]{:S(2)}) async-start(f32[4,32,256]{2,1,0:T(8,128)} %deal_kernel.1), calls=%async_computation | async-start | bytes 262144 | tf_op jit(solution)/shard_map/all_to_all | solution.py:430
  10.2 11.2 %copy-start.4 = (bf16[256,512]{1,0:T(8,128)(2,1)S(1)}, bf16[256,512]{1,0:T(8,128)(2,1)}, u32[]{:S(2)}) copy-start(bf16[256,512]{1,0:T(8,128)(2,1)} %constant.67.clone.high) | copy-start | bytes 786436
  15.0 6.4 %collective-permute-start = (f32[4,32,256]{2,1,0:T(8,128)S(1)}, f32[4,32,256]{2,1,0:T(8,128)S(1)}, u32[]{:S(2)}, u32[]{:S(2)}) collective-permute-start(f32[4,32,256]{2,1,0:T(8,128)S(1)} %all-to-all-done.own), channel_id=1, source_target_pairs={{0,1},{1,0},{2,3},{3,2},{4,5},{5,4},{6,7},{7,6},{8,9},{9,8},{10,11... | collective-permute-start | bytes 393224 | tf_op jit(solution)/shard_map/ppermute | solution.py:428
  22.2 35.5 %copy-start.15 = (f32[256,128]{1,0:T(8,128)S(1)}, f32[256,128]{1,0:T(8,128)}, u32[]{:S(2)}) copy-start(f32[256,128]{1,0:T(8,128)} %constant.70.clone.sin_turn) | copy-start | bytes 393220
  22.2 35.5 %copy-start.16 = (f32[256,128]{1,0:T(8,128)S(1)}, f32[256,128]{1,0:T(8,128)}, u32[]{:S(2)}) copy-start(f32[256,128]{1,0:T(8,128)} %constant.69.clone.cos_turn) | copy-start | bytes 393220
  22.2 35.5 %copy-start.21 = (bf16[128,128]{1,0:T(8,128)(2,1)S(1)}, bf16[128,128]{1,0:T(8,128)(2,1)}, u32[]{:S(2)}) copy-start(bf16[128,128]{1,0:T(8,128)(2,1)} %constant.74.clone.gather_lift_low) | copy-start | bytes 98308
  22.2 35.5 %copy-start.22 = (bf16[128,128]{1,0:T(8,128)(2,1)S(1)}, bf16[128,128]{1,0:T(8,128)(2,1)}, u32[]{:S(2)}) copy-start(bf16[128,128]{1,0:T(8,128)(2,1)} %constant.73.clone.gather_lift_high) | copy-start | bytes 98308
  23.7 34.0 %copy-start.5 = (bf16[256,512]{1,0:T(8,128)(2,1)S(1)}, bf16[256,512]{1,0:T(8,128)(2,1)}, u32[]{:S(2)}) copy-start(bf16[256,512]{1,0:T(8,128)(2,1)} %constant.72.clone.gather_low) | copy-start | bytes 786436
  23.7 34.0 %copy-start.6 = (bf16[256,512]{1,0:T(8,128)(2,1)S(1)}, bf16[256,512]{1,0:T(8,128)(2,1)}, u32[]{:S(2)}) copy-start(bf16[256,512]{1,0:T(8,128)(2,1)} %constant.71.clone.gather_high) | copy-start | bytes 786436
  23.7 34.0 %copy-start.13 = (bf16[256,256]{1,0:T(8,128)(2,1)S(1)}, bf16[256,256]{1,0:T(8,128)(2,1)}, u32[]{:S(2)}) copy-start(bf16[256,256]{1,0:T(8,128)(2,1)} %constant.76.clone.deal_low) | copy-start | bytes 393220
  23.8 34.0 %copy-start.14 = (bf16[256,256]{1,0:T(8,128)(2,1)S(1)}, bf16[256,256]{1,0:T(8,128)(2,1)}, u32[]{:S(2)}) copy-start(bf16[256,256]{1,0:T(8,128)(2,1)} %constant.75.clone.deal_high) | copy-start | bytes 393220
  57.8 26.1 %copy-start.19 = (f32[2,32,256]{2,1,0:T(8,128)S(1)}, f32[2,32,256]{2,1,0:T(8,128)}, u32[]{:S(2)}) copy-start(f32[2,32,256]{2,1,0:T(8,128)} %constant.78.clone.sin_main) | copy-start | bytes 196612
  57.8 26.1 %copy-start.20 = (f32[2,32,256]{2,1,0:T(8,128)S(1)}, f32[2,32,256]{2,1,0:T(8,128)}, u32[]{:S(2)}) copy-start(f32[2,32,256]{2,1,0:T(8,128)} %constant.77.clone.cos_main) | copy-start | bytes 196612
  59.5 24.4 %copy-start.7 = (bf16[128,512]{1,0:T(8,128)(2,1)S(1)}, bf16[128,512]{1,0:T(8,128)(2,1)}, u32[]{:S(2)}) copy-start(bf16[128,512]{1,0:T(8,128)(2,1)} %constant.84.clone.zone_low) | copy-start | bytes 393220
  59.5 24.4 %copy-start.8 = (bf16[128,512]{1,0:T(8,128)(2,1)S(1)}, bf16[128,512]{1,0:T(8,128)(2,1)}, u32[]{:S(2)}) copy-start(bf16[128,512]{1,0:T(8,128)(2,1)} %constant.83.clone.zone_high) | copy-start | bytes 393220
  59.5 24.4 %copy-start.9 = (bf16[256,256]{1,0:T(8,128)(2,1)S(1)}, bf16[256,256]{1,0:T(8,128)(2,1)}, u32[]{:S(2)}) copy-start(bf16[256,256]{1,0:T(8,128)(2,1)} %constant.82.clone.main_low) | copy-start | bytes 393220
  59.5 24.4 %copy-start.10 = (bf16[256,256]{1,0:T(8,128)(2,1)S(1)}, bf16[256,256]{1,0:T(8,128)(2,1)}, u32[]{:S(2)}) copy-start(bf16[256,256]{1,0:T(8,128)(2,1)} %constant.81.clone.main_high) | copy-start | bytes 393220
  59.5 24.4 %copy-start.11 = (f32[128,256]{1,0:T(8,128)S(1)}, f32[128,256]{1,0:T(8,128)}, u32[]{:S(2)}) copy-start(f32[128,256]{1,0:T(8,128)} %constant.80.clone.sin_zone) | copy-start | bytes 393220
  59.5 24.4 %copy-start.12 = (f32[128,256]{1,0:T(8,128)S(1)}, f32[128,256]{1,0:T(8,128)}, u32[]{:S(2)}) copy-start(f32[128,256]{1,0:T(8,128)} %constant.79.clone.cos_zone) | copy-start | bytes 393220
  86.6 7.5 %collective-permute-start.1 = (f32[4,32,256]{2,1,0:T(8,128)S(1)}, f32[4,32,256]{2,1,0:T(8,128)S(1)}, u32[]{:S(2)}, u32[]{:S(2)}) collective-permute-start(f32[4,32,256]{2,1,0:T(8,128)S(1)} %get-tuple-element.9), channel_id=1, source_target_pairs={{0,1},{1,0},{2,3},{3,2},{4,5},{5,4},{6,7},{7,6},{8,9},{9,8},{10,11... | collective-permute-start | bytes 393224 | tf_op jit(solution)/shard_map/ppermute | solution.py:428
  (7 other events, 46.8 us)

commit v4 on v3

--- a/solution.py
+++ b/solution.py
@@ -35,11 +35,11 @@
 def pair(matrix):
     high = matrix.astype(np.float32).astype(ml_dtypes.bfloat16)
     low = (matrix - high.astype(np.float64)).astype(np.float32).astype(ml_dtypes.bfloat16)
-    return high, low
+    return np.stack([high, low])
 
 
 def circle(phase):
-    return np.cos(phase).astype(np.float32), np.sin(phase).astype(np.float32)
+    return np.stack([np.cos(phase), np.sin(phase)]).astype(np.float32)
 
 
 @functools.cache
@@ -54,9 +54,8 @@
     n, ca, cj = col // 16, col // 8 % 2, col % 8
     base = np.exp(1j * angles(i[:, None] * n[None, :], 8)) * (1j ** ca)[None, :]
     same = jj[:, None] == cj[None, :]
-    for name, factor in (("slope", 1j), ("lift", 1.0)):
-        halves = [np.where(same, part(base * factor * s, a[:, None]), 0.0) for s in (1, 1j)]
-        out[name] = pair(np.concatenate(halves, 0))
+    halves = [np.where(same, part(base * s, a[:, None]), 0.0) for s in (1j, -1, 1, 1j)]
+    out["rows_mix"] = pair(np.concatenate(halves, 0))
     x0 = 4 * np.arange(2)[:, None] + np.arange(64)[None, :] // 16
     out["rows_turn"] = circle(angles(x0[:, :, None] * k256, NX))
     lane = np.arange(128)
@@ -71,8 +70,9 @@
         gather[1, k, f, y0 * 4 + i] = -turn[k].imag
         if k < 64:
             gather_lift[k, y0 * 4 + i] = turn[k].real if k < 32 else -turn[k].imag
-    out["gather"] = pair(gather.reshape(256, 512))
-    out["gather_lift"] = pair(gather_lift)
+    gather = np.concatenate([gather.reshape(256, 512), np.zeros((256, 128))], 1)
+    gather[:128, 512:] = gather_lift
+    out["gather"] = pair(gather)
     deal = np.zeros((2, 128, 2, 128))
     for k in range(128):
         f, a, i, jj = k // 64, k // 32 % 2, k // 8 % 4, k % 8
@@ -145,9 +145,10 @@
                 out[z, base + 8 * a : base + 8 * a + 8, :] = rows
 
 
-def source_kernel(place, offsets, zone, out):
+def source_kernel(place, offsets, zone, out, places, beyond):
     tile = place[0]
-    own = 4 * place[2] + place[1]
+    core = place[2]
+    own = 4 * core + place[1]
     ox = offsets[tile, 0]
     oy = offsets[tile, 1]
     lane = iota((128, 128), 1)
@@ -166,10 +167,27 @@
     g = jnp.where(g < 128, g, g - 256)
     left = cos_of(8 * g * (2 * oy + (lane & 63)) + jnp.where(lane < 64, 0, 1024))
     out[...] = dot3(split(left), split(right))
+    row = iota((16, 256), 0)
+    spot = iota((16, 256), 1)
+    edge = jnp.zeros((8, 256), jnp.int32)
+    tile_of = iota((8, 256), 1) >> 2
+    for t in range(0, 64, 4):
+        target = jnp.zeros((16, 256), jnp.int32)
+        for k in range(4):
+            x = offsets[t + k, 0]
+            target = jnp.where((row >> 2) == k, x >> 3, target)
+            edge = jnp.where(tile_of == t + k, 2 * (x & 7), edge)
+        near = (target + (row & 3) + 4 * core) & 255
+        far = (target + 8) & 255
+        places[4 * t : 4 * t + 16, :] = jnp.where(spot == near, 1.0, 0.0).astype(bf16)
+        places[256 + 4 * t : 272 + 4 * t, :] = jnp.where(spot == far, 1.0, 0.0).astype(bf16)
+    edge = jnp.where(((iota((8, 256), 1) & 3) == 0) & (core == 0), edge, 0)
+    for p in range(16):
+        beyond[8 * p : 8 * p + 8, :] = jnp.where(edge > p, 1.0, 0.0)
 
 
 def rows_kernel(
-    place, own, other, slope_high, slope_low, lift_high, lift_low, cos_turn, sin_turn, high, low, out
+    place, own, other, mix, turn, circles, out
 ):
     first_ky = 32 * place[0] + 8 * place[1]
     core = place[2]
@@ -189,14 +207,13 @@
         terms = (wave_x * eta, wave_y * eta, wave_x * phi, wave_y * phi, kappa * phi)
         for f in range(5):
             tiles[f].append(terms[f])
-    cosine = cos_turn[core]
-    sine = sin_turn[core]
-    slope_mix = (slope_high[...], slope_low[...])
-    lift_mix = (lift_high[...], lift_low[...])
+    cosine = turn[0, core]
+    sine = turn[1, core]
     parts = [[], []]
     for f in range(5):
         rows = split(jnp.concatenate(tiles[f], 0))
-        both = dot3(slope_mix if f < 4 else lift_mix, rows)
+        kind = slice(0, 128) if f < 4 else slice(128, 256)
+        both = dot3((mix[0, kind], mix[1, kind]), rows)
         first = both[:64]
         second = both[64:]
         turned = (first * cosine + second * sine).reshape(4, 2, 8, 256)
@@ -209,44 +226,30 @@
             )
     real, imag = parts
     words = real[:4] + imag[:4] + [real[4], imag[4], -imag[4], real[4]]
-    result = dot3((high[...], low[...]), split(jnp.concatenate(words, 0)), ((1,), (1,)))
+    result = dot3(circles, split(jnp.concatenate(words, 0)), ((1,), (1,)))
     for q in range(3):
         out[pl.ds(q, 256, stride=3), :] = result[:, 128 * q : 128 * q + 128]
 
 
-def columns_kernel(
-    terms,
-    source,
-    high,
-    low,
-    cos_turn,
-    sin_turn,
-    gather_high,
-    gather_low,
-    gather_lift_high,
-    gather_lift_low,
-    deal_high,
-    deal_low,
-    out,
-):
+def columns_kernel(terms, source, circles, turn, gather, deal, out):
     words = split(
         jnp.concatenate([terms[pl.ds(q, 256, stride=3), :] for q in range(3)], 1)
     )
-    with_cos = dot3((high[:, :256], low[:, :256]), words)
-    with_sin = dot3((high[:, 256:], low[:, 256:]), words)
+    with_cos = dot3((circles[0, :, :256], circles[1, :, :256]), words)
+    with_sin = dot3((circles[0, :, 256:], circles[1, :, 256:]), words)
     real = with_cos[:, :128] - with_sin[:, 128:256]
     imag = with_sin[:, :128] + with_cos[:, 128:256]
     lane = iota((256, 128), 1)
     rolled = pltpu.roll(with_sin[:, 256:], 64, 1)
     lift = with_cos[:, 256:] + jnp.where(lane < 64, rolled, -rolled)
-    cosine = cos_turn[...]
-    sine = sin_turn[...]
+    cosine = turn[0]
+    sine = turn[1]
     slopes = split(
         jnp.concatenate([real * cosine - imag * sine, real * sine + imag * cosine], 1)
     )
     lift = split(lift * cosine + pltpu.roll(lift, 64, 1) * sine)
-    fields = dot3(slopes, (gather_high[...], gather_low[...]))
-    lift = dot3(lift, (gather_lift_high[...], gather_lift_low[...]))
+    fields = dot3(slopes, (gather[0, :, :512], gather[1, :, :512]))
+    lift = dot3(lift, (gather[0, :128, 512:], gather[1, :128, 512:]))
     slope_ex, slope_ey, slope_px, slope_py = (
         fields[:, 128 * k : 128 * k + 128] for k in range(4)
     )
@@ -255,72 +258,27 @@
     )
     second_term = 0.5 * (lift * lift - slope_px * slope_px - slope_py * slope_py)
     products = jnp.concatenate([first_order, second_term], 1) * (time_step * spread)
-    both = dot3(split(products), (deal_high[...], deal_low[...]))
+    both = dot3(split(products), deal)
     first = both[:, :128]
     second = both[:, 128:]
     turned = jnp.concatenate([first * cosine + second * sine, second * cosine - first * sine], 0)
-    out[pl.ds(0, 256, stride=3), :] = dot3((high[...], low[...]), split(turned))
+    out[pl.ds(0, 256, stride=3), :] = dot3(circles, split(turned))
     out[pl.ds(1, 256, stride=3), :] = source[:, :128]
     out[pl.ds(2, 256, stride=3), :] = source[:, 128:]
 
 
 def rows_back_kernel(
-    place,
-    offsets,
-    terms,
-    high,
-    low,
-    cos_main,
-    sin_main,
-    cos_zone,
-    sin_zone,
-    main_high,
-    main_low,
-    zone_high,
-    zone_low,
-    out,
-    away,
-    ends,
+    place, terms, places, beyond, circles, main_turn, zone_turn, main_mix, zone_mix, out
 ):
     core = place[2]
-    depth = iota((8, 256), 0)
-    spot = iota((8, 256), 1)
-    lane = iota((8, 128), 1)
-    row = iota((8, 128), 0)
-    cells = [[], []]
-    places = []
-    last_places = []
-    bases = []
-    for t in range(0, 64, 2):
-        ox = offsets[t, 0], offsets[t + 1, 0]
-        base = ox[0] >> 3, ox[1] >> 3
-        bases += base
-        edge = jnp.where(row < 4, 8 * (2 * (ox[0] & 7)), 8 * (2 * (ox[1] & 7)))
-        edge = jnp.where(((row & 3) == 0) & (core == 0), edge, 0)
-        beyond = lane < edge
-        for a in range(2):
-            tile = terms[pl.ds(12 * t + 1 + a, 8, stride=3), :]
-            cells[a].append(jnp.where(beyond, 0.0, tile))
-            moved = jnp.where(beyond, tile, 0.0)
-            ends[t : t + 1, 128 * a : 128 * a + 128] = moved[0:1, :]
-            ends[t + 1 : t + 2, 128 * a : 128 * a + 128] = moved[4:5, :]
-        target = jnp.where(depth < 4, base[0], base[1]) + (depth & 3) + 4 * core
-        places.append(jnp.where(spot == (target & 255), 1.0, 0.0))
-    for t in range(0, 64, 8):
-        target = jnp.zeros((8, 256), jnp.int32)
-        for k in range(8):
-            target = jnp.where(depth == k, bases[t + k], target)
-        last_places.append(jnp.where(spot == ((target + 8) & 255), 1.0, 0.0))
-    where_to = jnp.concatenate(places, 0).astype(bf16)
-    last_to = jnp.concatenate(last_places, 0).astype(bf16)
-    cells = jnp.concatenate([jnp.concatenate(half, 0) for half in cells], 1)
-    near = split(cells.T)
-    far = split(ends[...].T)
-    grid = (dot(near[0], where_to) + dot(near[1], where_to)) + (
-        dot(far[0], last_to) + dot(far[1], last_to)
-    )
+    cells = jnp.concatenate(
+        [terms[pl.ds(1, 256, stride=3), :], terms[pl.ds(2, 256, stride=3), :]], 1
+    ).T
+    far = cells * jnp.concatenate([beyond[...], beyond[...]], 0)
+    high, low = split(jnp.concatenate([cells - far, far], 1))
+    grid = dot(high, places[...]) + dot(low, places[...])
     main = terms[pl.ds(0, 256, stride=3), :].T
-    both = dot3(split(jnp.concatenate([main, grid], 0)), (high[...], low[...]))
+    both = dot3(split(jnp.concatenate([main, grid], 0)), circles)
 
     def turned(lines, cosine, sine):
         with_cos = lines[:, :, :256]
@@ -332,22 +290,17 @@
             jnp.concatenate([real.reshape(count, 256), imag.reshape(count, 256)], 0)
         )
 
-    main = turned(both[:128].reshape(4, 32, 512), cos_main[core][None], sin_main[core][None])
-    zone = turned(both[128:].reshape(2, 128, 512), cos_zone[...][None], sin_zone[...][None])
-    main = dot3((main_high[...], main_low[...]), main)
-    zone = dot3((zone_high[...], zone_low[...]), zone)
+    main = turned(both[:128].reshape(4, 32, 512), main_turn[0, core][None], main_turn[1, core][None])
+    zone = turned(both[128:].reshape(2, 128, 512), zone_turn[0][None], zone_turn[1][None])
+    main = dot3(main_mix, main)
+    zone = dot3(zone_mix, zone)
     odd = 1.0 - 2.0 * core.astype(f32)
-    blocks = []
     for n in range(8):
         block = main[32 * n : 32 * n + 32]
         if n % 2:
             block = block * odd
-        blocks.append(
-            jnp.concatenate([block[:16] + zone[16 * n : 16 * n + 16], block[16:]], 0)
-        )
-    for z in range(4):
-        out[z] = jnp.where(core == 0, blocks[2 * z], blocks[2 * z + 1])
-        away[z] = jnp.where(core == 0, blocks[2 * z + 1], blocks[2 * z])
+        out[n, 0:16, :] = block[:16] + zone[16 * n : 16 * n + 16]
+        out[n, 16:32, :] = block[16:]
 
 
 def finish_kernel(place, terms, eta, phi, eta_next, phi_next):
@@ -360,24 +313,25 @@
             surface = eta[a, rows, :]
             potential = phi[a, rows, :]
             part_of = slice(8 * a, 8 * a + 8)
-            eta_next[a, rows, :] = surface + kappa * potential + terms[z, part_of, :]
+            added = terms[2 * z, part_of, :] + terms[2 * z + 1, part_of, :]
+            eta_next[a, rows, :] = surface + kappa * potential + added
             part_of = slice(16 + 8 * a, 24 + 8 * a)
-            linear = potential - (time_step * gravity) * surface
-            phi_next[a, rows, :] = linear + terms[z, part_of, :]
-
-
-def call(kernel, shapes, scalars, arrays, scratch=(), flops=0, limit=24):
+            added = terms[2 * z, part_of, :] + terms[2 * z + 1, part_of, :]
+            phi_next[a, rows, :] = potential - (time_step * gravity) * surface + added
+
+
+def call(kernel, shapes, scalars, arrays, flops=0, limit=24, types=None):
     single = isinstance(shapes, tuple)
     shapes = [shapes] if single else shapes
+    types = [f32] * len(shapes) if types is None else types
     vmem = pl.BlockSpec(memory_space=pltpu.VMEM)
     smem = pl.BlockSpec(memory_space=pltpu.SMEM)
     moved = sum(4 * math.prod(s) for s in shapes) + sum(x.size * x.dtype.itemsize for x in arrays)
     result = pl.pallas_call(
         kernel,
-        out_shape=[jax.ShapeDtypeStruct(s, f32) for s in shapes],
+        out_shape=[jax.ShapeDtypeStruct(s, t) for s, t in zip(shapes, types)],
         in_specs=[smem] * len(scalars) + [vmem] * len(arrays),
         out_specs=[vmem] * len(shapes),
-        scratch_shapes=list(scratch),
         compiler_params=pltpu.CompilerParams(vmem_limit_bytes=limit * 1024 * 1024),
         cost_estimate=pl.CostEstimate(flops=flops, bytes_accessed=moved, transcendentals=0),
         name=kernel.__name__,
@@ -386,31 +340,32 @@
 
 
 def stage_deal(eta, phi):
-    return call(deal_kernel, (4, 32, 256), [], [eta, phi], limit=56)
+    return call(deal_kernel, (4, 32, 256), [], [eta, phi], limit=56, flops=2**33)
 
 
 def stage_source(place, offsets, zone):
-    return call(source_kernel, (256, 256), [place, offsets], [zone], flops=2**26)
+    shapes = [(256, 256), (512, 256), (128, 256)]
+    types = [f32, bf16, f32]
+    return call(source_kernel, shapes, [place, offsets], [zone], flops=2**26, types=types)
 
 
 def stage_rows(place, own, other):
     t = tables()
-    constants = [*t["slope"], *t["lift"], *t["rows_turn"], *t["turn"]]
-    return call(rows_kernel, (768, 128), [place], [own, other, *constants], flops=2**30)
+    arrays = [own, other, t["rows_mix"], t["rows_turn"], t["turn"]]
+    return call(rows_kernel, (768, 128), [place], arrays, flops=2**30)
 
 
 def stage_columns(terms, source):
     t = tables()
-    constants = [*t["turn"], *t["y_turn"], *t["gather"], *t["gather_lift"], *t["deal"]]
-    return call(columns_kernel, (768, 128), [], [terms, source, *constants], flops=2**30)
-
-
-def stage_rows_back(place, offsets, terms):
+    arrays = [terms, source, t["turn"], t["y_turn"], t["gather"], t["deal"]]
+    return call(columns_kernel, (768, 128), [], arrays, flops=2**30)
+
+
+def stage_rows_back(place, terms, places, beyond):
     t = tables()
-    constants = [*t["turn"], *t["main_turn"], *t["zone_turn"], *t["main_mix"], *t["zone_mix"]]
-    scratch = [pltpu.VMEM((64, 256), f32)]
-    arrays = [terms, *constants]
-    return call(rows_back_kernel, [(4, 32, 256)] * 2, [place, offsets], arrays, scratch, flops=2**29)
+    arrays = [terms, places, beyond, t["turn"], t["main_turn"], t["zone_turn"]]
+    arrays += [t["main_mix"], t["zone_mix"]]
+    return call(rows_back_kernel, (8, 32, 256), [place], arrays, flops=2**29)
 
 
 def stage_finish(place, terms, eta, phi):
@@ -427,13 +382,11 @@
     def across(rows):
         return lax.ppermute(rows, "core", [(0, 1), (1, 0)])
 
-    own = swap(stage_deal(eta_modes, phi_modes), "lane")
-    source = stage_source(place, offsets, zone_field)
-    own, source = lax.optimization_barrier((own, source))
+    own, place = lax.optimization_barrier((swap(stage_deal(eta_modes, phi_modes), "lane"), place))
+    source, places, beyond = stage_source(place, offsets, zone_field)
     columns = turn(stage_rows(place, own, across(own)))
     rows = turn(stage_columns(columns, source))
-    share, away = stage_rows_back(place, offsets, rows)
-    terms = swap(share + across(away), "lane")
+    terms = swap(stage_rows_back(place, rows, places, beyond), ("lane", "core"))
     return tuple(stage_finish(place, terms, eta_modes, phi_modes))
 
 

time: 103 us -> 103 us (level)
  blocking collectives: 65.6 us -> 40 us
  waiting for transfers between devices: 4.36 us -> 18.8 us
  starting transfers between devices: 19.9 us -> 31.9 us
    all_to_all x2 -> x1, blocking collectives: 58.2 us -> 23.7 us  [turn(): return swap(words.reshape(256, 1, 384), ('wide', 'lane')).reshape(768, 128)]
    all_to_all x1 -> x2, starting transfers between devices: 7.94 us -> 26.5 us  [the longest x1 18.5 us: turn(): return swap(words.reshape(256, 1, 384), ('wide', 'lane')).reshape(768, 128)]
    all_to_all x1 -> x2, waiting for transfers between devices: 2.43 us -> 17.8 us  [the longest x1 13.1 us: turn(): return swap(words.reshape(256, 1, 384), ('wide', 'lane')).reshape(768, 128)]
    all_to_all x1, blocking collectives: 7.4 us -> 16.3 us  [local(): terms = swap(stage_rows_back(place, rows, places, beyond), ('lane', 'core'))]
    ppermute x2 -> x1, starting transfers between devices: 11.9 us -> 5.41 us  [across(): return lax.ppermute(rows, 'core', [(0, 1), (1, 0)])]
where the time goes in v4:
time: 103 us
  blocking collectives  40 us (39%)
  starting transfers between devices  31.9 us (31%)
  waiting for transfers between devices  18.8 us (18%)
  Pallas kernels  10.6 us (10%)
    all_to_all x1, blocking collectives, turn(): return swap(words.reshape(256, 1, 384), ('wide', 'lane')).reshape(768, 128)  23.7 us
    all_to_all x1, starting transfers between devices, turn(): return swap(words.reshape(256, 1, 384), ('wide', 'lane')).reshape(768, 128)  18.5 us
    all_to_all x1, blocking collectives, local(): terms = swap(stage_rows_back(place, rows, places, beyond), ('lane', 'core'))  16.3 us
    all_to_all x1, waiting for transfers between devices, turn(): return swap(words.reshape(256, 1, 384), ('wide', 'lane')).reshape(768, 128)  13.1 us
    pallas_call x6, Pallas kernels, call(): pl.pallas_call(kernel, out_shape=[jax.ShapeDtypeStruct(s, t) for s, t in...  10.6 us
    all_to_all x1, starting transfers between devices, local(): swap(stage_deal(eta_modes, phi_modes), 'lane')  7.94 us
    ppermute x1, starting transfers between devices, across(): return lax.ppermute(rows, 'core', [(0, 1), (1, 0)])  5.41 us
    all_to_all x1, waiting for transfers between devices, local(): swap(stage_deal(eta_modes, phi_modes), 'lane')  4.69 us
  transfers between devices with their start and end apart: 3, of which 3 were waited for; matrix products, arithmetic and copies ran while one was open for 0% of the time, Pallas kernels for 2%

profile of v4, /device:TPU:1, one launch (start us, length us, event | category | flops | bytes accessed | tf_op | source)
XLA Modules:
  0.0 103.0 jit_solution(8191906081355246247)
XLA Ops:
  0.6 0.0 copy-start
  0.6 0.0 copy-start.12
  0.7 1.6 %deal_kernel.1 = f32[4,32,256]{2,1,0:T(8,128)} custom-call(f32[2,32,256]{2,1,0:T(8,128)} %eta.3, f32[2,32,256]{2,1,0:T(8,128)} %phi.3), custom_call_target="tpu_custom_call" | custom-call | flops 8589934592 | bytes 262144 | tf_op jit(solution)/shard_map/deal_kernel/pallas_call | solution.py:330
  2.3 7.9 %all-to-all-start = ((f32[4,32,256]{2,1,0:T(8,128)}), f32[4,32,256]{2,1,0:T(8,128)S(1)}, u32[]{:S(2)}, u32[]{:S(2)}) async-start(f32[4,32,256]{2,1,0:T(8,128)} %deal_kernel.1), calls=%async_computation | async-start | bytes 262144 | tf_op jit(solution)/shard_map/all_to_all | solution.py:385
  10.2 0.1 pad_add_fusion.place
  10.3 4.7 %all-to-all-done.own = f32[4,32,256]{2,1,0:T(8,128)S(1)} async-done(((f32[4,32,256]{2,1,0:T(8,128)}), f32[4,32,256]{2,1,0:T(8,128)S(1)}, u32[]{:S(2)}, u32[]{:S(2)}) %all-to-all-start) | async-done | bytes 131104 | tf_op jit(solution)/shard_map/all_to_all | solution.py:385
  15.0 5.4 %collective-permute-start = (f32[4,32,256]{2,1,0:T(8,128)S(1)}, f32[4,32,256]{2,1,0:T(8,128)S(1)}, u32[]{:S(2)}, u32[]{:S(2)}) collective-permute-start(f32[4,32,256]{2,1,0:T(8,128)S(1)} %all-to-all-done.own), channel_id=1, source_target_pairs={{0,1},{1,0},{2,3},{3,2},{4,5},{5,4},{6,7},{7,6},{8,9},{9,8},{10,11... | collective-permute-start | bytes 393224 | tf_op jit(solution)/shard_map/ppermute | solution.py:383
  20.4 1.0 collective-permute-done.other
  21.4 0.0 copy-start.10
  21.4 2.3 %rows_kernel.1 = f32[768,128]{1,0:T(8,128)} custom-call(s32[3]{0:T(128)S(1)} %pad_add_fusion.place, f32[4,32,256]{2,1,0:T(8,128)S(1)} %all-to-all-done.own, f32[4,32,256]{2,1,0:T(8,128)S(1)} %collective-permute-done.other, bf16[2,256,128]{2,1,0:T(8,128)(2,1)S(1)} %copy-done.12, f32[2,2,64,256]{3,2,1,0:T(8,128)S(1)} %copy-done.11, ...), custom_call_target="tpu_custom_call" | custom-call | flops 1073741824 | bytes 1572864 | tf_op jit(solution)/shard_map/rows_kernel/pallas_call | solution.py:330
  23.7 18.5 %all-to-all-start.1 = ((f32[256,1,384]{2,1,0:T(1,128)}), f32[256,1,384]{2,1,0:T(1,128)S(1)}, u32[]{:S(2)}, u32[]{:S(2)}) async-start(f32[256,1,384]{2,1,0:T(1,128)} %bitcast.3), calls=%async_computation.1 | async-start | bytes 786432 | tf_op jit(solution)/shard_map/all_to_all | solution.py:380
  42.2 0.1 copy.18.offsets
  42.3 0.7 copy-done.7
  43.0 1.7 %source_kernel.1 = (f32[256,256]{1,0:T(8,128)S(1)}, bf16[512,256]{1,0:T(8,128)(2,1)S(1)}, f32[128,256]{1,0:T(8,128)S(1)}) custom-call(s32[3]{0:T(128)S(1)} %pad_add_fusion.place, s32[64,2]{1,0:T(8,128)S(1)} %copy.18.offsets, f32[64,128]{1,0:T(8,128)S(1)} %copy-done.7), custom_call_target="tpu_custom_call" | custom-call | flops 67108864 | bytes 950272 | tf_op jit(solution)/shard_map/source_kernel/pallas_call | solution.py:330
  44.7 13.1 %all-to-all-done.1 = f32[256,1,384]{2,1,0:T(1,128)S(1)} async-done(((f32[256,1,384]{2,1,0:T(1,128)}), f32[256,1,384]{2,1,0:T(1,128)S(1)}, u32[]{:S(2)}, u32[]{:S(2)}) %all-to-all-start.1) | async-done | bytes 393248 | tf_op jit(solution)/shard_map/all_to_all | solution.py:380
  57.9 0.0 copy-start.4
  57.9 1.7 %columns_kernel.1 = f32[768,128]{1,0:T(8,128)S(1)} custom-call(f32[768,128]{1,0:T(8,128)S(1)} %bitcast.8, f32[256,256]{1,0:T(8,128)S(1)} %get-tuple-element.9.source, bf16[2,256,512]{2,1,0:T(8,128)(2,1)S(1)} %copy-done, f32[2,256,128]{2,1,0:T(8,128)S(1)} %copy-done.10, bf16[2,256,640]{2,1,0:T(8,128)(2,1)S(1)} %copy-done.8, bf16[2,256,256]{2,1,0:T(8,128)(2,1)S(1)} %copy-done.9), custom_call_target="tpu_custom_call" | custom-call | flops 1073741824 | bytes 2752512 | tf_op jit(solution)/shard_map/columns_kernel/pallas_call | solution.py:330
  59.6 0.0 copy-start.1
  59.6 0.0 copy-start.2
  59.6 0.0 copy-start.3
  59.6 23.7 %all_to_all.20 = f32[256,1,384]{2,1,0:T(1,128)S(1)} all-to-all(f32[256,1,384]{2,1,0:T(1,128)S(1)} %bitcast.9), channel_id=1, replica_groups=mesh['wide'=64,'lane'=4,'core'=2] {'wide','lane'}, dimensions={0} | all-to-all | bytes 786432 | tf_op jit(solution)/shard_map/all_to_all | solution.py:380
  83.3 2.1 %rows_back_kernel.1 = f32[8,32,256]{2,1,0:T(8,128)S(1)} custom-call(s32[3]{0:T(128)S(1)} %pad_add_fusion.place, f32[768,128]{1,0:T(8,128)S(1)} %bitcast.7, bf16[512,256]{1,0:T(8,128)(2,1)S(1)} %get-tuple-element.10.places, f32[128,256]{1,0:T(8,128)S(1)} %get-tuple-element.11.beyond, bf16[2,256,512]{2,1,0:T(8,128)(2,1)S(1)} %copy-done, ...), custom_call_target="tpu_custom_call" | custom-call | flops 536870912 | bytes 2490368 | tf_op jit(solution)/shard_map/rows_back_kernel/pallas_call | solution.py:330
  85.4 16.3 %all_to_all.21.terms = f32[8,32,256]{2,1,0:T(8,128)S(1)} all-to-all(f32[8,32,256]{2,1,0:T(8,128)S(1)} %rows_back_kernel.1), channel_id=1, replica_groups=mesh['wide'=64,'lane'=4,'core'=2] {'lane','core'}, dimensions={0} | all-to-all | bytes 524288 | tf_op jit(solution)/shard_map/all_to_all | solution.py:389
  101.7 1.2 %finish_kernel.1 = (f32[2,32,256]{2,1,0:T(8,128)}, f32[2,32,256]{2,1,0:T(8,128)}) custom-call(s32[3]{0:T(128)S(1)} %pad_add_fusion.place, f32[8,32,256]{2,1,0:T(8,128)S(1)} %all_to_all.21.terms, f32[2,32,256]{2,1,0:T(8,128)S(1)} %copy-done.5, f32[2,32,256]{2,1,0:T(8,128)S(1)} %copy-done.6), custom_call_target="tpu_custom_call" | custom-call | bytes 524288 | tf_op jit(solution)/shard_map/finish_kernel/pallas_call | solution.py:330
  (20 shorter events, 0.0 us)
Async XLA Ops:
  0.6 20.7 %copy-start = (bf16[2,256,512]{2,1,0:T(8,128)(2,1)S(1)}, bf16[2,256,512]{2,1,0:T(8,128)(2,1)}, u32[]{:S(2)}) copy-start(bf16[2,256,512]{2,1,0:T(8,128)(2,1)} %constant.35.clone.circles) | copy-start | bytes 1572868
  0.6 20.7 %copy-start.12 = (bf16[2,256,128]{2,1,0:T(8,128)(2,1)S(1)}, bf16[2,256,128]{2,1,0:T(8,128)(2,1)}, u32[]{:S(2)}) copy-start(bf16[2,256,128]{2,1,0:T(8,128)(2,1)} %constant.33.clone.mix) | copy-start | bytes 393220
  2.3 19.1 %copy-start.11 = (f32[2,2,64,256]{3,2,1,0:T(8,128)S(1)}, f32[2,2,64,256]{3,2,1,0:T(8,128)}, u32[]{:S(2)}) copy-start(f32[2,2,64,256]{3,2,1,0:T(8,128)} %constant.34.clone.turn) | copy-start | bytes 786436
  2.3 12.7 %all-to-all-start = ((f32[4,32,256]{2,1,0:T(8,128)}), f32[4,32,256]{2,1,0:T(8,128)S(1)}, u32[]{:S(2)}, u32[]{:S(2)}) async-start(f32[4,32,256]{2,1,0:T(8,128)} %deal_kernel.1), calls=%async_computation | async-start | bytes 262144 | tf_op jit(solution)/shard_map/all_to_all | solution.py:385
  15.0 6.4 %collective-permute-start = (f32[4,32,256]{2,1,0:T(8,128)S(1)}, f32[4,32,256]{2,1,0:T(8,128)S(1)}, u32[]{:S(2)}, u32[]{:S(2)}) collective-permute-start(f32[4,32,256]{2,1,0:T(8,128)S(1)} %all-to-all-done.own), channel_id=1, source_target_pairs={{0,1},{1,0},{2,3},{3,2},{4,5},{5,4},{6,7},{7,6},{8,9},{9,8},{10,11... | collective-permute-start | bytes 393224 | tf_op jit(solution)/shard_map/ppermute | solution.py:383
  21.4 36.5 %copy-start.9 = (bf16[2,256,256]{2,1,0:T(8,128)(2,1)S(1)}, bf16[2,256,256]{2,1,0:T(8,128)(2,1)}, u32[]{:S(2)}) copy-start(bf16[2,256,256]{2,1,0:T(8,128)(2,1)} %constant.38.clone.deal) | copy-start | bytes 786436
  21.4 36.5 %copy-start.10 = (f32[2,256,128]{2,1,0:T(8,128)S(1)}, f32[2,256,128]{2,1,0:T(8,128)}, u32[]{:S(2)}) copy-start(f32[2,256,128]{2,1,0:T(8,128)} %constant.36.clone.turn) | copy-start | bytes 786436
  23.7 34.2 %copy-start.8 = (bf16[2,256,640]{2,1,0:T(8,128)(2,1)S(1)}, bf16[2,256,640]{2,1,0:T(8,128)(2,1)}, u32[]{:S(2)}) copy-start(bf16[2,256,640]{2,1,0:T(8,128)(2,1)} %constant.37.clone.gather) | copy-start | bytes 1966084
  23.7 18.5 %copy-start.13 = (s32[64,2]{0,1:T(2,128)S(1)}, s32[64,2]{0,1:T(2,128)}, u32[]{:S(2)}) copy-start(s32[64,2]{0,1:T(2,128)} %param.17) | copy-start | bytes 1540
  23.7 34.1 %all-to-all-start.1 = ((f32[256,1,384]{2,1,0:T(1,128)}), f32[256,1,384]{2,1,0:T(1,128)S(1)}, u32[]{:S(2)}, u32[]{:S(2)}) async-start(f32[256,1,384]{2,1,0:T(1,128)} %bitcast.3), calls=%async_computation.1 | async-start | bytes 786432 | tf_op jit(solution)/shard_map/all_to_all | solution.py:380
  42.2 0.8 copy-start.7
  57.9 25.4 %copy-start.4 = (f32[2,2,32,256]{3,2,1,0:T(8,128)S(1)}, f32[2,2,32,256]{3,2,1,0:T(8,128)}, u32[]{:S(2)}) copy-start(f32[2,2,32,256]{3,2,1,0:T(8,128)} %constant.39.clone.main_turn) | copy-start | bytes 393220
  59.6 23.7 %copy-start.1 = (bf16[2,128,512]{2,1,0:T(8,128)(2,1)S(1)}, bf16[2,128,512]{2,1,0:T(8,128)(2,1)}, u32[]{:S(2)}) copy-start(bf16[2,128,512]{2,1,0:T(8,128)(2,1)} %constant.42.clone.zone_mix) | copy-start | bytes 786436
  59.6 23.7 %copy-start.2 = (bf16[2,256,256]{2,1,0:T(8,128)(2,1)S(1)}, bf16[2,256,256]{2,1,0:T(8,128)(2,1)}, u32[]{:S(2)}) copy-start(bf16[2,256,256]{2,1,0:T(8,128)(2,1)} %constant.41.clone.main_mix) | copy-start | bytes 786436
  59.6 23.7 %copy-start.3 = (f32[2,128,256]{2,1,0:T(8,128)S(1)}, f32[2,128,256]{2,1,0:T(8,128)}, u32[]{:S(2)}) copy-start(f32[2,128,256]{2,1,0:T(8,128)} %constant.40.clone.zone_turn) | copy-start | bytes 786436
  85.4 16.3 %copy-start.5 = (f32[2,32,256]{2,1,0:T(8,128)S(1)}, f32[2,32,256]{2,1,0:T(8,128)}, u32[]{:S(2)}) copy-start(f32[2,32,256]{2,1,0:T(8,128)} %eta.3) | copy-start | bytes 196612
  85.4 16.3 %copy-start.6 = (f32[2,32,256]{2,1,0:T(8,128)S(1)}, f32[2,32,256]{2,1,0:T(8,128)}, u32[]{:S(2)}) copy-start(f32[2,32,256]{2,1,0:T(8,128)} %phi.3) | copy-start | bytes 196612

commit v5 on v4

--- a/solution.py
+++ b/solution.py
@@ -142,7 +142,8 @@
         for source, base in ((eta, 0), (phi, 16)):
             for a in range(2):
                 rows = source[a, 8 * z : 8 * z + 8, :]
-                out[z, base + 8 * a : base + 8 * a + 8, :] = rows
+                for c in range(2):
+                    out[2 * z + c, base + 8 * a : base + 8 * a + 8, :] = rows
 
 
 def source_kernel(place, offsets, zone, out, places, beyond):
@@ -186,9 +187,7 @@
         beyond[8 * p : 8 * p + 8, :] = jnp.where(edge > p, 1.0, 0.0)
 
 
-def rows_kernel(
-    place, own, other, mix, turn, circles, out
-):
+def rows_kernel(place, modes, mix, turn, circles, out):
     first_ky = 32 * place[0] + 8 * place[1]
     core = place[2]
     odd = 1.0 - 2.0 * core.astype(f32)
@@ -197,10 +196,8 @@
     for n in range(8):
         wave_x = wave_of(256 * n + iota((16, 256), 1)) * TURN_X
         kappa = jnp.sqrt(wave_x * wave_x + wave_y * wave_y)
-        mine, theirs = (own, other) if n % 2 == 0 else (other, own)
-        z = n // 2
-        eta = jnp.where(core == 0, mine[z, 0:16, :], theirs[z, 0:16, :])
-        phi = jnp.where(core == 0, mine[z, 16:32, :], theirs[z, 16:32, :])
+        eta = modes[n, 0:16, :]
+        phi = modes[n, 16:32, :]
         if n % 2:
             eta = eta * odd
             phi = phi * odd
@@ -340,7 +337,7 @@
 
 
 def stage_deal(eta, phi):
-    return call(deal_kernel, (4, 32, 256), [], [eta, phi], limit=56, flops=2**33)
+    return call(deal_kernel, (8, 32, 256), [], [eta, phi], limit=56, flops=2**33)
 
 
 def stage_source(place, offsets, zone):
@@ -349,9 +346,9 @@
     return call(source_kernel, shapes, [place, offsets], [zone], flops=2**26, types=types)
 
 
-def stage_rows(place, own, other):
+def stage_rows(place, modes):
     t = tables()
-    arrays = [own, other, t["rows_mix"], t["rows_turn"], t["turn"]]
+    arrays = [modes, t["rows_mix"], t["rows_turn"], t["turn"]]
     return call(rows_kernel, (768, 128), [place], arrays, flops=2**30)
 
 
@@ -379,12 +376,10 @@
     def turn(words):
         return swap(words.reshape(256, 1, 384), ("wide", "lane")).reshape(768, 128)
 
-    def across(rows):
-        return lax.ppermute(rows, "core", [(0, 1), (1, 0)])
-
-    own, place = lax.optimization_barrier((swap(stage_deal(eta_modes, phi_modes), "lane"), place))
-    source, places, beyond = stage_source(place, offsets, zone_field)
-    columns = turn(stage_rows(place, own, across(own)))
+    modes = swap(stage_deal(eta_modes, phi_modes), ("lane", "core"))
+    ready = stage_source(place, offsets, zone_field)
+    modes, (source, places, beyond) = lax.optimization_barrier((modes, ready))
+    columns = turn(stage_rows(place, modes))
     rows = turn(stage_columns(columns, source))
     terms = swap(stage_rows_back(place, rows, places, beyond), ("lane", "core"))
     return tuple(stage_finish(place, terms, eta_modes, phi_modes))

time: 103 us -> 102 us (level)
  blocking collectives: 40 us -> 73.4 us
  starting transfers between devices: 31.9 us -> 10.3 us
  waiting for transfers between devices: 18.8 us -> 6.25 us
    all_to_all x1 -> x2, blocking collectives: 23.7 us -> 57 us  [turn(): return swap(words.reshape(256, 1, 384), ('wide', 'lane')).reshape(768, 128)]
    all_to_all x2 -> x1, starting transfers between devices: 26.5 us -> 10.3 us  [local(): modes = swap(stage_deal(eta_modes, phi_modes), ('lane', 'core'))]
    all_to_all x2 -> x1, waiting for transfers between devices: 17.8 us -> 6.25 us  [local(): modes = swap(stage_deal(eta_modes, phi_modes), ('lane', 'core'))]
    ppermute x1 -> x0, starting transfers between devices: 5.41 us -> none  [across(): return lax.ppermute(rows, 'core', [(0, 1), (1, 0)])]
  transfers between devices with their start and end apart: 3 -> 1, of which waited for: 3 -> 1; matrix products, arithmetic and copies ran while one was open for 0% -> 0% of each run, Pallas kernels for 2% -> 2%
where the time goes in v5:
time: 102 us; the launch traced here: 101 us
  blocking collectives  73.4 us (72%)
  starting transfers between devices  10.3 us (10%)
  Pallas kernels  9.87 us (10%)
  waiting for transfers between devices  6.25 us (6%)
    all_to_all x2, blocking collectives, turn(): return swap(words.reshape(256, 1, 384), ('wide', 'lane')).reshape(768, 128)  57 us
    all_to_all x1, blocking collectives, local(): terms = swap(stage_rows_back(place, rows, places, beyond), ('lane', 'core'))  16.4 us
    all_to_all x1, starting transfers between devices, local(): modes = swap(stage_deal(eta_modes, phi_modes), ('lane', 'core'))  10.3 us
    pallas_call x6, Pallas kernels, call(): pl.pallas_call(kernel, out_shape=[jax.ShapeDtypeStruct(s, t) for s, t in...  9.87 us
    all_to_all x1, waiting for transfers between devices, local(): modes = swap(stage_deal(eta_modes, phi_modes), ('lane', 'core'))  6.25 us
  transfers between devices with their start and end apart: 1, of which 1 were waited for; matrix products, arithmetic and copies ran while one was open for 0% of the time, Pallas kernels for 2%

profile of v5, /device:TPU:1, one launch (start us, length us, event | category | flops | bytes accessed | tf_op | source)
XLA Modules:
  0.0 101.5 jit_solution(12452212806201524485)
XLA Ops:
  0.6 0.0 copy-start.12
  0.6 1.6 %deal_kernel.1 = f32[8,32,256]{2,1,0:T(8,128)} custom-call(f32[2,32,256]{2,1,0:T(8,128)} %eta.3, f32[2,32,256]{2,1,0:T(8,128)} %phi.3), custom_call_target="tpu_custom_call" | custom-call | flops 8589934592 | bytes 393216 | tf_op jit(solution)/shard_map/deal_kernel/pallas_call | solution.py:327
  2.3 10.3 %all-to-all-start = ((f32[8,32,256]{2,1,0:T(8,128)}), f32[8,32,256]{2,1,0:T(8,128)S(1)}, u32[]{:S(2)}, u32[]{:S(2)}) async-start(f32[8,32,256]{2,1,0:T(8,128)} %deal_kernel.1), calls=%async_computation | async-start | bytes 524288 | tf_op jit(solution)/shard_map/all_to_all | solution.py:379
  12.6 0.1 copy.17.offsets
  12.7 0.1 pad_add_fusion.place
  12.8 0.6 copy-done.7
  13.3 1.7 %source_kernel.1 = (f32[256,256]{1,0:T(8,128)S(1)}, bf16[512,256]{1,0:T(8,128)(2,1)S(1)}, f32[128,256]{1,0:T(8,128)S(1)}) custom-call(s32[3]{0:T(128)S(1)} %pad_add_fusion.place, s32[64,2]{1,0:T(8,128)S(1)} %copy.17.offsets, f32[64,128]{1,0:T(8,128)S(1)} %copy-done.7), custom_call_target="tpu_custom_call" | custom-call | flops 67108864 | bytes 950272 | tf_op jit(solution)/shard_map/source_kernel/pallas_call | solution.py:327
  15.1 6.3 %all-to-all-done.modes = f32[8,32,256]{2,1,0:T(8,128)S(1)} async-done(((f32[8,32,256]{2,1,0:T(8,128)}), f32[8,32,256]{2,1,0:T(8,128)S(1)}, u32[]{:S(2)}, u32[]{:S(2)}) %all-to-all-start) | async-done | bytes 262176 | tf_op jit(solution)/shard_map/all_to_all | solution.py:379
  21.3 0.0 copy-start.9
  21.3 0.0 copy-start.10
  21.4 1.5 %rows_kernel.1 = f32[768,128]{1,0:T(8,128)S(1)} custom-call(s32[3]{0:T(128)S(1)} %pad_add_fusion.place, f32[8,32,256]{2,1,0:T(8,128)S(1)} %all-to-all-done.modes, bf16[2,256,128]{2,1,0:T(8,128)(2,1)S(1)} %copy-done.12, f32[2,2,64,256]{3,2,1,0:T(8,128)S(1)} %copy-done.11, bf16[2,256,512]{2,1,0:T(8,128)(2,1)S(1)} %copy-done), custom_call_target="tpu_custom_call" | custom-call | flops 1073741824 | bytes 1572864 | tf_op jit(solution)/shard_map/rows_kernel/pallas_call | solution.py:327
  22.9 0.0 copy-start.8
  22.9 33.0 %all_to_all.20 = f32[256,1,384]{2,1,0:T(1,128)S(1)} all-to-all(f32[256,1,384]{2,1,0:T(1,128)S(1)} %bitcast.10), channel_id=1, replica_groups=mesh['wide'=64,'lane'=4,'core'=2] {'wide','lane'}, dimensions={0} | all-to-all | bytes 786432 | tf_op jit(solution)/shard_map/all_to_all | solution.py:377
  55.9 0.0 copy-start.4
  55.9 1.7 %columns_kernel.1 = f32[768,128]{1,0:T(8,128)S(1)} custom-call(f32[768,128]{1,0:T(8,128)S(1)} %bitcast.8, f32[256,256]{1,0:T(8,128)S(1)} %get-tuple-element.13.source, bf16[2,256,512]{2,1,0:T(8,128)(2,1)S(1)} %copy-done, f32[2,256,128]{2,1,0:T(8,128)S(1)} %copy-done.10, bf16[2,256,640]{2,1,0:T(8,128)(2,1)S(1)} %copy-done.8, bf16[2,256,256]{2,1,0:T(8,128)(2,1)S(1)} %copy-done.9), custom_call_target="tpu_custom_call" | custom-call | flops 1073741824 | bytes 2752512 | tf_op jit(solution)/shard_map/columns_kernel/pallas_call | solution.py:327
  57.6 0.0 copy-start.1
  57.6 0.0 copy-start.2
  57.6 0.0 copy-start.3
  57.6 24.0 %all_to_all.21 = f32[256,1,384]{2,1,0:T(1,128)S(1)} all-to-all(f32[256,1,384]{2,1,0:T(1,128)S(1)} %bitcast.9), channel_id=1, replica_groups=mesh['wide'=64,'lane'=4,'core'=2] {'wide','lane'}, dimensions={0} | all-to-all | bytes 786432 | tf_op jit(solution)/shard_map/all_to_all | solution.py:377
  81.7 2.1 %rows_back_kernel.1 = f32[8,32,256]{2,1,0:T(8,128)S(1)} custom-call(s32[3]{0:T(128)S(1)} %pad_add_fusion.place, f32[768,128]{1,0:T(8,128)S(1)} %bitcast.7, bf16[512,256]{1,0:T(8,128)(2,1)S(1)} %get-tuple-element.14.places, f32[128,256]{1,0:T(8,128)S(1)} %get-tuple-element.15.beyond, bf16[2,256,512]{2,1,0:T(8,128)(2,1)S(1)} %copy-done, ...), custom_call_target="tpu_custom_call" | custom-call | flops 536870912 | bytes 2490368 | tf_op jit(solution)/shard_map/rows_back_kernel/pallas_call | solution.py:327
  83.8 0.0 copy-start.5
  83.8 0.0 copy-start.6
  83.8 16.4 %all_to_all.22.terms = f32[8,32,256]{2,1,0:T(8,128)S(1)} all-to-all(f32[8,32,256]{2,1,0:T(8,128)S(1)} %rows_back_kernel.1), channel_id=1, replica_groups=mesh['wide'=64,'lane'=4,'core'=2] {'lane','core'}, dimensions={0} | all-to-all | bytes 524288 | tf_op jit(solution)/shard_map/all_to_all | solution.py:384
  100.3 1.2 %finish_kernel.1 = (f32[2,32,256]{2,1,0:T(8,128)}, f32[2,32,256]{2,1,0:T(8,128)}) custom-call(s32[3]{0:T(128)S(1)} %pad_add_fusion.place, f32[8,32,256]{2,1,0:T(8,128)S(1)} %all_to_all.22.terms, f32[2,32,256]{2,1,0:T(8,128)S(1)} %copy-done.5, f32[2,32,256]{2,1,0:T(8,128)S(1)} %copy-done.6), custom_call_target="tpu_custom_call" | custom-call | bytes 524288 | tf_op jit(solution)/shard_map/finish_kernel/pallas_call | solution.py:327
  (17 shorter events, 0.0 us)
Async XLA Ops:
  0.6 20.7 %copy-start.12 = (bf16[2,256,128]{2,1,0:T(8,128)(2,1)S(1)}, bf16[2,256,128]{2,1,0:T(8,128)(2,1)}, u32[]{:S(2)}) copy-start(bf16[2,256,128]{2,1,0:T(8,128)(2,1)} %constant.33.clone.mix) | copy-start | bytes 393220
  2.3 10.3 %copy-start.13 = (s32[64,2]{0,1:T(2,128)S(1)}, s32[64,2]{0,1:T(2,128)}, u32[]{:S(2)}) copy-start(s32[64,2]{0,1:T(2,128)} %param.17) | copy-start | bytes 1540
  2.3 19.1 %copy-start = (bf16[2,256,512]{2,1,0:T(8,128)(2,1)S(1)}, bf16[2,256,512]{2,1,0:T(8,128)(2,1)}, u32[]{:S(2)}) copy-start(bf16[2,256,512]{2,1,0:T(8,128)(2,1)} %constant.35.clone.circles) | copy-start | bytes 1572868
  2.3 19.0 %all-to-all-start = ((f32[8,32,256]{2,1,0:T(8,128)}), f32[8,32,256]{2,1,0:T(8,128)S(1)}, u32[]{:S(2)}, u32[]{:S(2)}) async-start(f32[8,32,256]{2,1,0:T(8,128)} %deal_kernel.1), calls=%async_computation | async-start | bytes 524288 | tf_op jit(solution)/shard_map/all_to_all | solution.py:379
  12.6 0.8 copy-start.7
  12.6 8.7 %copy-start.11 = (f32[2,2,64,256]{3,2,1,0:T(8,128)S(1)}, f32[2,2,64,256]{3,2,1,0:T(8,128)}, u32[]{:S(2)}) copy-start(f32[2,2,64,256]{3,2,1,0:T(8,128)} %constant.34.clone.turn) | copy-start | bytes 786436
  21.3 34.6 %copy-start.9 = (bf16[2,256,256]{2,1,0:T(8,128)(2,1)S(1)}, bf16[2,256,256]{2,1,0:T(8,128)(2,1)}, u32[]{:S(2)}) copy-start(bf16[2,256,256]{2,1,0:T(8,128)(2,1)} %constant.38.clone.deal) | copy-start | bytes 786436
  21.3 34.5 %copy-start.10 = (f32[2,256,128]{2,1,0:T(8,128)S(1)}, f32[2,256,128]{2,1,0:T(8,128)}, u32[]{:S(2)}) copy-start(f32[2,256,128]{2,1,0:T(8,128)} %constant.36.clone.turn) | copy-start | bytes 786436
  22.9 33.0 %copy-start.8 = (bf16[2,256,640]{2,1,0:T(8,128)(2,1)S(1)}, bf16[2,256,640]{2,1,0:T(8,128)(2,1)}, u32[]{:S(2)}) copy-start(bf16[2,256,640]{2,1,0:T(8,128)(2,1)} %constant.37.clone.gather) | copy-start | bytes 1966084
  55.9 25.8 %copy-start.4 = (f32[2,2,32,256]{3,2,1,0:T(8,128)S(1)}, f32[2,2,32,256]{3,2,1,0:T(8,128)}, u32[]{:S(2)}) copy-start(f32[2,2,32,256]{3,2,1,0:T(8,128)} %constant.39.clone.main_turn) | copy-start | bytes 393220
  57.6 24.1 %copy-start.1 = (bf16[2,128,512]{2,1,0:T(8,128)(2,1)S(1)}, bf16[2,128,512]{2,1,0:T(8,128)(2,1)}, u32[]{:S(2)}) copy-start(bf16[2,128,512]{2,1,0:T(8,128)(2,1)} %constant.42.clone.zone_mix) | copy-start | bytes 786436
  57.6 24.1 %copy-start.2 = (bf16[2,256,256]{2,1,0:T(8,128)(2,1)S(1)}, bf16[2,256,256]{2,1,0:T(8,128)(2,1)}, u32[]{:S(2)}) copy-start(bf16[2,256,256]{2,1,0:T(8,128)(2,1)} %constant.41.clone.main_mix) | copy-start | bytes 786436
  57.6 24.1 %copy-start.3 = (f32[2,128,256]{2,1,0:T(8,128)S(1)}, f32[2,128,256]{2,1,0:T(8,128)}, u32[]{:S(2)}) copy-start(f32[2,128,256]{2,1,0:T(8,128)} %constant.40.clone.zone_turn) | copy-start | bytes 786436
  83.8 16.5 %copy-start.5 = (f32[2,32,256]{2,1,0:T(8,128)S(1)}, f32[2,32,256]{2,1,0:T(8,128)}, u32[]{:S(2)}) copy-start(f32[2,32,256]{2,1,0:T(8,128)} %eta.3) | copy-start | bytes 196612
  83.8 16.5 %copy-start.6 = (f32[2,32,256]{2,1,0:T(8,128)S(1)}, f32[2,32,256]{2,1,0:T(8,128)}, u32[]{:S(2)}) copy-start(f32[2,32,256]{2,1,0:T(8,128)} %phi.3) | copy-start | bytes 196612

commit v6 on v5

--- a/solution.py
+++ b/solution.py
@@ -48,6 +48,10 @@
     k256 = np.arange(256)
     phase = angles(k256[:, None] * k256[None, :], 256)
     out["turn"] = pair(np.concatenate([np.cos(phase), np.sin(phase)], 1))
+    held = np.arange(256) % 64 * 4 + np.arange(256) // 64
+    phase = angles(k256[:, None] * held[None, :], 256)
+    out["into_y"] = pair(np.concatenate([np.cos(phase), np.sin(phase)], 1))
+    out["from_y"] = pair(np.concatenate([np.cos(phase).T, np.sin(phase).T], 1))
     row = np.arange(64)
     i, a, jj = row // 16, row // 8 % 2, row % 8
     col = np.arange(128)
@@ -113,7 +117,10 @@
 
 
 def dot3(left, right, dims=((1,), (0,))):
-    return dot(left[0], right[0], dims) + (dot(left[0], right[1], dims) + dot(left[1], right[0], dims))
+    along = dims[0][0], dims[1][0]
+    left = jnp.concatenate([left[0], left[0], left[1]], along[0])
+    right = jnp.concatenate([right[0], right[1], right[0]], along[1])
+    return dot(left, right, dims)
 
 
 def iota(shape, dim):
@@ -137,13 +144,22 @@
     return jnp.where(index < 1024, index, index - 2048).astype(f32)
 
 
-def deal_kernel(eta, phi, out):
-    for z in range(4):
-        for source, base in ((eta, 0), (phi, 16)):
-            for a in range(2):
-                rows = source[a, 8 * z : 8 * z + 8, :]
-                for c in range(2):
-                    out[2 * z + c, base + 8 * a : base + 8 * a + 8, :] = rows
+def deal_kernel(eta, phi, out, held, arrived, left):
+    copies = [
+        pltpu.make_async_copy(source, held.at[k], arrived.at[k])
+        for k, source in enumerate((eta, phi))
+    ]
+    for copy in copies:
+        copy.start()
+    dealt = []
+    for k in range(2):
+        copies[k].wait()
+        for n in range(8):
+            rows = held.at[k, :, 8 * (n % 4) : 8 * (n % 4) + 8, :]
+            dealt.append(pltpu.make_async_copy(rows, out.at[n, k], left.at[8 * k + n]))
+            dealt[-1].start()
+    for copy in dealt:
+        copy.wait()
 
 
 def source_kernel(place, offsets, zone, out, places, beyond):
@@ -165,24 +181,28 @@
     )
     lane = iota((256, 128), 1)
     g = iota((256, 128), 0)
+    g = 4 * (g & 63) + (g >> 6)
     g = jnp.where(g < 128, g, g - 256)
     left = cos_of(8 * g * (2 * oy + (lane & 63)) + jnp.where(lane < 64, 0, 1024))
     out[...] = dot3(split(left), split(right))
     row = iota((16, 256), 0)
     spot = iota((16, 256), 1)
     edge = jnp.zeros((8, 256), jnp.int32)
-    tile_of = iota((8, 256), 1) >> 2
-    for t in range(0, 64, 4):
+    tile_of = iota((8, 256), 1) & 63
+    for t in range(0, 64, 16):
         target = jnp.zeros((16, 256), jnp.int32)
-        for k in range(4):
+        for k in range(16):
             x = offsets[t + k, 0]
-            target = jnp.where((row >> 2) == k, x >> 3, target)
+            target = jnp.where(row == k, x >> 3, target)
             edge = jnp.where(tile_of == t + k, 2 * (x & 7), edge)
-        near = (target + (row & 3) + 4 * core) & 255
         far = (target + 8) & 255
-        places[4 * t : 4 * t + 16, :] = jnp.where(spot == near, 1.0, 0.0).astype(bf16)
-        places[256 + 4 * t : 272 + 4 * t, :] = jnp.where(spot == far, 1.0, 0.0).astype(bf16)
-    edge = jnp.where(((iota((8, 256), 1) & 3) == 0) & (core == 0), edge, 0)
+        for z in range(4):
+            near = (target + z + 4 * core) & 255
+            first = 64 * z + t
+            places[first : first + 16, :] = jnp.where(spot == near, 1.0, 0.0).astype(bf16)
+            first += 256
+            places[first : first + 16, :] = jnp.where(spot == far, 1.0, 0.0).astype(bf16)
+    edge = jnp.where((iota((8, 256), 1) < 64) & (core == 0), edge, 0)
     for p in range(16):
         beyond[8 * p : 8 * p + 8, :] = jnp.where(edge > p, 1.0, 0.0)
 
@@ -196,8 +216,9 @@
     for n in range(8):
         wave_x = wave_of(256 * n + iota((16, 256), 1)) * TURN_X
         kappa = jnp.sqrt(wave_x * wave_x + wave_y * wave_y)
-        eta = modes[n, 0:16, :]
-        phi = modes[n, 16:32, :]
+        block = 4 * (n % 2) + n // 2
+        eta = modes[block, 0:16, :]
+        phi = modes[block, 16:32, :]
         if n % 2:
             eta = eta * odd
             phi = phi * odd
@@ -228,12 +249,12 @@
         out[pl.ds(q, 256, stride=3), :] = result[:, 128 * q : 128 * q + 128]
 
 
-def columns_kernel(terms, source, circles, turn, gather, deal, out):
+def columns_kernel(terms, source, into_y, from_y, turn, gather, deal, out):
     words = split(
         jnp.concatenate([terms[pl.ds(q, 256, stride=3), :] for q in range(3)], 1)
     )
-    with_cos = dot3((circles[0, :, :256], circles[1, :, :256]), words)
-    with_sin = dot3((circles[0, :, 256:], circles[1, :, 256:]), words)
+    with_cos = dot3((into_y[0, :, :256], into_y[1, :, :256]), words)
+    with_sin = dot3((into_y[0, :, 256:], into_y[1, :, 256:]), words)
     real = with_cos[:, :128] - with_sin[:, 128:256]
     imag = with_sin[:, :128] + with_cos[:, 128:256]
     lane = iota((256, 128), 1)
@@ -259,7 +280,7 @@
     first = both[:, :128]
     second = both[:, 128:]
     turned = jnp.concatenate([first * cosine + second * sine, second * cosine - first * sine], 0)
-    out[pl.ds(0, 256, stride=3), :] = dot3(circles, split(turned))
+    out[pl.ds(0, 256, stride=3), :] = dot3(from_y, split(turned))
     out[pl.ds(1, 256, stride=3), :] = source[:, :128]
     out[pl.ds(2, 256, stride=3), :] = source[:, 128:]
 
@@ -296,8 +317,9 @@
         block = main[32 * n : 32 * n + 32]
         if n % 2:
             block = block * odd
-        out[n, 0:16, :] = block[:16] + zone[16 * n : 16 * n + 16]
-        out[n, 16:32, :] = block[16:]
+        where = 4 * (n % 2) + n // 2
+        out[where, 0:16, :] = block[:16] + zone[16 * n : 16 * n + 16]
+        out[where, 16:32, :] = block[16:]
 
 
 def finish_kernel(place, terms, eta, phi, eta_next, phi_next):
@@ -310,10 +332,10 @@
             surface = eta[a, rows, :]
             potential = phi[a, rows, :]
             part_of = slice(8 * a, 8 * a + 8)
-            added = terms[2 * z, part_of, :] + terms[2 * z + 1, part_of, :]
+            added = terms[z, part_of, :] + terms[4 + z, part_of, :]
             eta_next[a, rows, :] = surface + kappa * potential + added
             part_of = slice(16 + 8 * a, 24 + 8 * a)
-            added = terms[2 * z, part_of, :] + terms[2 * z + 1, part_of, :]
+            added = terms[z, part_of, :] + terms[4 + z, part_of, :]
             phi_next[a, rows, :] = potential - (time_step * gravity) * surface + added
 
 
@@ -337,7 +359,22 @@
 
 
 def stage_deal(eta, phi):
-    return call(deal_kernel, (8, 32, 256), [], [eta, phi], limit=56, flops=2**33)
+    far = pl.BlockSpec(memory_space=pltpu.HBM)
+    dealt = pl.pallas_call(
+        deal_kernel,
+        out_shape=jax.ShapeDtypeStruct((8, 2, 2, 8, 256), f32),
+        in_specs=[far, far],
+        out_specs=pl.BlockSpec(memory_space=pl.ANY),
+        scratch_shapes=[
+            pltpu.VMEM((2, 2, 32, 256), f32),
+            pltpu.SemaphoreType.DMA((2,)),
+            pltpu.SemaphoreType.DMA((16,)),
+        ],
+        compiler_params=pltpu.CompilerParams(vmem_limit_bytes=56 * 1024 * 1024),
+        cost_estimate=pl.CostEstimate(flops=2**33, bytes_accessed=2**19, transcendentals=0),
+        name="deal_kernel",
+    )(eta, phi)
+    return dealt.reshape(8, 32, 256)
 
 
 def stage_source(place, offsets, zone):
@@ -354,7 +391,7 @@
 
 def stage_columns(terms, source):
     t = tables()
-    arrays = [terms, source, t["turn"], t["y_turn"], t["gather"], t["deal"]]
+    arrays = [terms, source, t["into_y"], t["from_y"], t["y_turn"], t["gather"], t["deal"]]
     return call(columns_kernel, (768, 128), [], arrays, flops=2**30)
 
 
@@ -374,14 +411,14 @@
     swap = functools.partial(lax.all_to_all, split_axis=0, concat_axis=0, tiled=True)
 
     def turn(words):
-        return swap(words.reshape(256, 1, 384), ("wide", "lane")).reshape(768, 128)
-
-    modes = swap(stage_deal(eta_modes, phi_modes), ("lane", "core"))
+        return swap(words.reshape(256, 1, 384), ("lane", "wide")).reshape(768, 128)
+
+    modes = swap(stage_deal(eta_modes, phi_modes), ("core", "lane"))
     ready = stage_source(place, offsets, zone_field)
     modes, (source, places, beyond) = lax.optimization_barrier((modes, ready))
     columns = turn(stage_rows(place, modes))
     rows = turn(stage_columns(columns, source))
-    terms = swap(stage_rows_back(place, rows, places, beyond), ("lane", "core"))
+    terms = swap(stage_rows_back(place, rows, places, beyond), ("core", "lane"))
     return tuple(stage_finish(place, terms, eta_modes, phi_modes))
 
 

time: 102 us -> 104 us (1.020)
  blocking collectives: 73.4 us -> 74.9 us
    pallas_call x6 -> x5, Pallas kernels: 9.87 us -> 7.82 us  [call(): pl.pallas_call(kernel, out_shape=[jax.ShapeDtypeStruct(s, t) for s, t in...]
    pallas_call x0 -> x1, Pallas kernels: none -> 1.74 us  [stage_deal(): pl.pallas_call(deal_kernel, out_shape=jax.ShapeDtypeStruct((8, 2, 2, 8, 2...]
    all_to_all x3, blocking collectives: 73.4 us -> 74.9 us  [the longest x2 59.8 us: turn(): return swap(words.reshape(256, 1, 384), ('lane', 'wide')).reshape(768, 128)]
where the time goes in v6:
time: 104 us; the launch traced here: 103 us
  blocking collectives  74.9 us (72%)
  starting transfers between devices  10.4 us (10%)
  Pallas kernels  9.57 us (9%)
  waiting for transfers between devices  6.66 us (6%)
    all_to_all x2, blocking collectives, turn(): return swap(words.reshape(256, 1, 384), ('lane', 'wide')).reshape(768, 128)  59.8 us
    all_to_all x1, blocking collectives, local(): terms = swap(stage_rows_back(place, rows, places, beyond), ('core', 'lane'))  15.1 us
    all_to_all x1, starting transfers between devices, local(): modes = swap(stage_deal(eta_modes, phi_modes), ('core', 'lane'))  10.4 us
    pallas_call x5, Pallas kernels, call(): pl.pallas_call(kernel, out_shape=[jax.ShapeDtypeStruct(s, t) for s, t in...  7.82 us
    all_to_all x1, waiting for transfers between devices, local(): modes = swap(stage_deal(eta_modes, phi_modes), ('core', 'lane'))  6.66 us
  transfers between devices with their start and end apart: 1, of which 1 were waited for; matrix products, arithmetic and copies ran while one was open for 0% of the time, Pallas kernels for 2%

profile of v6, /device:TPU:1, one launch (start us, length us, event | category | flops | bytes accessed | tf_op | source)
XLA Modules:
  0.0 103.1 jit_solution(4562505508211740126)
XLA Ops:
  0.6 0.0 copy-start.14
  0.6 1.7 %deal_kernel.1 = f32[8,2,2,8,256]{4,3,2,1,0:T(8,128)} custom-call(f32[2,32,256]{2,1,0:T(8,128)} %eta.3, f32[2,32,256]{2,1,0:T(8,128)} %phi.3), custom_call_target="tpu_custom_call" | custom-call | flops 8589934592 | bytes 524288 | tf_op jit(solution)/shard_map/deal_kernel/pallas_call | solution.py:363
  2.4 0.0 copy-start
  2.4 10.4 %all-to-all-start = ((f32[8,32,256]{2,1,0:T(8,128)}), f32[8,32,256]{2,1,0:T(8,128)S(1)}, u32[]{:S(2)}, u32[]{:S(2)}) async-start(f32[8,32,256]{2,1,0:T(8,128)} %bitcast.12), calls=%async_computation | async-start | bytes 524288 | tf_op jit(solution)/shard_map/all_to_all | solution.py:416
  12.8 0.1 copy.19.offsets
  12.9 0.1 pad_add_fusion.place
  13.0 0.6 copy-done.7
  13.5 1.6 %source_kernel.1 = (f32[256,256]{1,0:T(8,128)S(1)}, bf16[512,256]{1,0:T(8,128)(2,1)S(1)}, f32[128,256]{1,0:T(8,128)S(1)}) custom-call(s32[3]{0:T(128)S(1)} %pad_add_fusion.place, s32[64,2]{1,0:T(8,128)S(1)} %copy.19.offsets, f32[64,128]{1,0:T(8,128)S(1)} %copy-done.7), custom_call_target="tpu_custom_call" | custom-call | flops 67108864 | bytes 950272 | tf_op jit(solution)/shard_map/source_kernel/pallas_call | solution.py:349
  15.2 6.7 %all-to-all-done.modes = f32[8,32,256]{2,1,0:T(8,128)S(1)} async-done(((f32[8,32,256]{2,1,0:T(8,128)}), f32[8,32,256]{2,1,0:T(8,128)S(1)}, u32[]{:S(2)}, u32[]{:S(2)}) %all-to-all-start) | async-done | bytes 262176 | tf_op jit(solution)/shard_map/all_to_all | solution.py:416
  21.8 0.0 copy-start.9
  21.8 0.0 copy-start.10
  21.9 0.0 copy-start.11
  21.9 0.0 copy-start.12
  21.9 1.4 %rows_kernel.1 = f32[768,128]{1,0:T(8,128)S(1)} custom-call(s32[3]{0:T(128)S(1)} %pad_add_fusion.place, f32[8,32,256]{2,1,0:T(8,128)S(1)} %all-to-all-done.modes, bf16[2,256,128]{2,1,0:T(8,128)(2,1)S(1)} %copy-done.14, f32[2,2,64,256]{3,2,1,0:T(8,128)S(1)} %copy-done.13, bf16[2,256,512]{2,1,0:T(8,128)(2,1)S(1)} %copy-done), custom_call_target="tpu_custom_call" | custom-call | flops 1073741824 | bytes 1572864 | tf_op jit(solution)/shard_map/rows_kernel/pallas_call | solution.py:349
  23.3 0.0 copy-start.8
  23.3 34.5 %all_to_all.20 = f32[256,1,384]{2,1,0:T(1,128)S(1)} all-to-all(f32[256,1,384]{2,1,0:T(1,128)S(1)} %bitcast.11), channel_id=1, replica_groups=mesh['wide'=64,'lane'=4,'core'=2] {'lane','wide'}, dimensions={0} | all-to-all | bytes 786432 | tf_op jit(solution)/shard_map/all_to_all | solution.py:414
  57.9 0.0 copy-start.4
  57.9 1.6 %columns_kernel.1 = f32[768,128]{1,0:T(8,128)S(1)} custom-call(f32[768,128]{1,0:T(8,128)S(1)} %bitcast.9, f32[256,256]{1,0:T(8,128)S(1)} %get-tuple-element.13.source, bf16[2,256,512]{2,1,0:T(8,128)(2,1)S(1)} %copy-done.10, bf16[2,256,512]{2,1,0:T(8,128)(2,1)S(1)} %copy-done.9, f32[2,256,128]{2,1,0:T(8,128)S(1)} %copy-done.12, ...), custom_call_target="tpu_custom_call" | custom-call | flops 1073741824 | bytes 3276800 | tf_op jit(solution)/shard_map/columns_kernel/pallas_call | solution.py:349
  59.6 0.0 copy-start.1
  59.6 0.0 copy-start.3
  59.6 25.3 %all_to_all.21 = f32[256,1,384]{2,1,0:T(1,128)S(1)} all-to-all(f32[256,1,384]{2,1,0:T(1,128)S(1)} %bitcast.10), channel_id=1, replica_groups=mesh['wide'=64,'lane'=4,'core'=2] {'lane','wide'}, dimensions={0} | all-to-all | bytes 786432 | tf_op jit(solution)/shard_map/all_to_all | solution.py:414
  84.9 1.9 %rows_back_kernel.1 = f32[8,32,256]{2,1,0:T(8,128)S(1)} custom-call(s32[3]{0:T(128)S(1)} %pad_add_fusion.place, f32[768,128]{1,0:T(8,128)S(1)} %bitcast.8, bf16[512,256]{1,0:T(8,128)(2,1)S(1)} %get-tuple-element.14.places, f32[128,256]{1,0:T(8,128)S(1)} %get-tuple-element.15.beyond, bf16[2,256,512]{2,1,0:T(8,128)(2,1)S(1)} %copy-done, ...), custom_call_target="tpu_custom_call" | custom-call | flops 536870912 | bytes 2490368 | tf_op jit(solution)/shard_map/rows_back_kernel/pallas_call | solution.py:349
  86.8 15.1 %all_to_all.22.terms = f32[8,32,256]{2,1,0:T(8,128)S(1)} all-to-all(f32[8,32,256]{2,1,0:T(8,128)S(1)} %rows_back_kernel.1), channel_id=1, replica_groups=mesh['wide'=64,'lane'=4,'core'=2] {'core','lane'}, dimensions={0} | all-to-all | bytes 524288 | tf_op jit(solution)/shard_map/all_to_all | solution.py:421
  101.9 1.2 %finish_kernel.1 = (f32[2,32,256]{2,1,0:T(8,128)}, f32[2,32,256]{2,1,0:T(8,128)}) custom-call(s32[3]{0:T(128)S(1)} %pad_add_fusion.place, f32[8,32,256]{2,1,0:T(8,128)S(1)} %all_to_all.22.terms, f32[2,32,256]{2,1,0:T(8,128)S(1)} %copy-done.5, f32[2,32,256]{2,1,0:T(8,128)S(1)} %copy-done.6), custom_call_target="tpu_custom_call" | custom-call | bytes 524288 | tf_op jit(solution)/shard_map/finish_kernel/pallas_call | solution.py:349
  (21 shorter events, 0.1 us)
Async XLA Ops:
  0.6 21.2 %copy-start.14 = (bf16[2,256,128]{2,1,0:T(8,128)(2,1)S(1)}, bf16[2,256,128]{2,1,0:T(8,128)(2,1)}, u32[]{:S(2)}) copy-start(bf16[2,256,128]{2,1,0:T(8,128)(2,1)} %constant.37.clone.mix) | copy-start | bytes 393220
  2.4 19.4 %copy-start = (bf16[2,256,512]{2,1,0:T(8,128)(2,1)S(1)}, bf16[2,256,512]{2,1,0:T(8,128)(2,1)}, u32[]{:S(2)}) copy-start(bf16[2,256,512]{2,1,0:T(8,128)(2,1)} %constant.39.clone.circles) | copy-start | bytes 1572868
  2.4 10.4 %copy-start.15 = (s32[64,2]{0,1:T(2,128)S(1)}, s32[64,2]{0,1:T(2,128)}, u32[]{:S(2)}) copy-start(s32[64,2]{0,1:T(2,128)} %param.19) | copy-start | bytes 1540
  2.4 19.4 %all-to-all-start = ((f32[8,32,256]{2,1,0:T(8,128)}), f32[8,32,256]{2,1,0:T(8,128)S(1)}, u32[]{:S(2)}, u32[]{:S(2)}) async-start(f32[8,32,256]{2,1,0:T(8,128)} %bitcast.12), calls=%async_computation | async-start | bytes 524288 | tf_op jit(solution)/shard_map/all_to_all | solution.py:416
  12.8 0.8 copy-start.7
  12.8 9.1 %copy-start.13 = (f32[2,2,64,256]{3,2,1,0:T(8,128)S(1)}, f32[2,2,64,256]{3,2,1,0:T(8,128)}, u32[]{:S(2)}) copy-start(f32[2,2,64,256]{3,2,1,0:T(8,128)} %constant.38.clone.turn) | copy-start | bytes 786436
  21.8 36.1 %copy-start.9 = (bf16[2,256,512]{2,1,0:T(8,128)(2,1)S(1)}, bf16[2,256,512]{2,1,0:T(8,128)(2,1)}, u32[]{:S(2)}) copy-start(bf16[2,256,512]{2,1,0:T(8,128)(2,1)} %constant.41.clone.from_y) | copy-start | bytes 1572868
  21.8 36.1 %copy-start.10 = (bf16[2,256,512]{2,1,0:T(8,128)(2,1)S(1)}, bf16[2,256,512]{2,1,0:T(8,128)(2,1)}, u32[]{:S(2)}) copy-start(bf16[2,256,512]{2,1,0:T(8,128)(2,1)} %constant.40.clone.into_y) | copy-start | bytes 1572868
  21.9 36.0 %copy-start.11 = (bf16[2,256,256]{2,1,0:T(8,128)(2,1)S(1)}, bf16[2,256,256]{2,1,0:T(8,128)(2,1)}, u32[]{:S(2)}) copy-start(bf16[2,256,256]{2,1,0:T(8,128)(2,1)} %constant.44.clone.deal) | copy-start | bytes 786436
  21.9 36.0 %copy-start.12 = (f32[2,256,128]{2,1,0:T(8,128)S(1)}, f32[2,256,128]{2,1,0:T(8,128)}, u32[]{:S(2)}) copy-start(f32[2,256,128]{2,1,0:T(8,128)} %constant.42.clone.turn) | copy-start | bytes 786436
  23.3 34.6 %copy-start.8 = (bf16[2,256,640]{2,1,0:T(8,128)(2,1)S(1)}, bf16[2,256,640]{2,1,0:T(8,128)(2,1)}, u32[]{:S(2)}) copy-start(bf16[2,256,640]{2,1,0:T(8,128)(2,1)} %constant.43.clone.gather) | copy-start | bytes 1966084
  57.9 26.9 %copy-start.4 = (f32[2,2,32,256]{3,2,1,0:T(8,128)S(1)}, f32[2,2,32,256]{3,2,1,0:T(8,128)}, u32[]{:S(2)}) copy-start(f32[2,2,32,256]{3,2,1,0:T(8,128)} %constant.45.clone.main_turn) | copy-start | bytes 393220
  59.6 25.3 %copy-start.1 = (bf16[2,128,512]{2,1,0:T(8,128)(2,1)S(1)}, bf16[2,128,512]{2,1,0:T(8,128)(2,1)}, u32[]{:S(2)}) copy-start(bf16[2,128,512]{2,1,0:T(8,128)(2,1)} %constant.48.clone.zone_mix) | copy-start | bytes 786436
  59.6 25.3 %copy-start.2 = (bf16[2,256,256]{2,1,0:T(8,128)(2,1)S(1)}, bf16[2,256,256]{2,1,0:T(8,128)(2,1)}, u32[]{:S(2)}) copy-start(bf16[2,256,256]{2,1,0:T(8,128)(2,1)} %constant.47.clone.main_mix) | copy-start | bytes 786436
  59.6 25.3 %copy-start.3 = (f32[2,128,256]{2,1,0:T(8,128)S(1)}, f32[2,128,256]{2,1,0:T(8,128)}, u32[]{:S(2)}) copy-start(f32[2,128,256]{2,1,0:T(8,128)} %constant.46.clone.zone_turn) | copy-start | bytes 786436
  86.8 15.1 %copy-start.5 = (f32[2,32,256]{2,1,0:T(8,128)S(1)}, f32[2,32,256]{2,1,0:T(8,128)}, u32[]{:S(2)}) copy-start(f32[2,32,256]{2,1,0:T(8,128)} %eta.3) | copy-start | bytes 196612
  86.8 15.1 %copy-start.6 = (f32[2,32,256]{2,1,0:T(8,128)S(1)}, f32[2,32,256]{2,1,0:T(8,128)}, u32[]{:S(2)}) copy-start(f32[2,32,256]{2,1,0:T(8,128)} %phi.3) | copy-start | bytes 196612

commit v7 on v5

--- a/solution.py
+++ b/solution.py
@@ -113,7 +113,10 @@
 
 
 def dot3(left, right, dims=((1,), (0,))):
-    return dot(left[0], right[0], dims) + (dot(left[0], right[1], dims) + dot(left[1], right[0], dims))
+    along = dims[0][0], dims[1][0]
+    left = jnp.concatenate([left[0], left[0], left[1]], along[0])
+    right = jnp.concatenate([right[0], right[1], right[0]], along[1])
+    return dot(left, right, dims)
 
 
 def iota(shape, dim):
@@ -143,7 +146,7 @@
             for a in range(2):
                 rows = source[a, 8 * z : 8 * z + 8, :]
                 for c in range(2):
-                    out[2 * z + c, base + 8 * a : base + 8 * a + 8, :] = rows
+                    out[4 * c + z, base + 8 * a : base + 8 * a + 8, :] = rows
 
 
 def source_kernel(place, offsets, zone, out, places, beyond):
@@ -196,8 +199,9 @@
     for n in range(8):
         wave_x = wave_of(256 * n + iota((16, 256), 1)) * TURN_X
         kappa = jnp.sqrt(wave_x * wave_x + wave_y * wave_y)
-        eta = modes[n, 0:16, :]
-        phi = modes[n, 16:32, :]
+        block = 4 * (n % 2) + n // 2
+        eta = modes[block, 0:16, :]
+        phi = modes[block, 16:32, :]
         if n % 2:
             eta = eta * odd
             phi = phi * odd
@@ -272,8 +276,8 @@
         [terms[pl.ds(1, 256, stride=3), :], terms[pl.ds(2, 256, stride=3), :]], 1
     ).T
     far = cells * jnp.concatenate([beyond[...], beyond[...]], 0)
-    high, low = split(jnp.concatenate([cells - far, far], 1))
-    grid = dot(high, places[...]) + dot(low, places[...])
+    cells = jnp.concatenate(split(jnp.concatenate([cells - far, far], 1)), 1)
+    grid = dot(cells, jnp.concatenate([places[...], places[...]], 0))
     main = terms[pl.ds(0, 256, stride=3), :].T
     both = dot3(split(jnp.concatenate([main, grid], 0)), circles)
 
@@ -296,8 +300,9 @@
         block = main[32 * n : 32 * n + 32]
         if n % 2:
             block = block * odd
-        out[n, 0:16, :] = block[:16] + zone[16 * n : 16 * n + 16]
-        out[n, 16:32, :] = block[16:]
+        where = 4 * (n % 2) + n // 2
+        out[where, 0:16, :] = block[:16] + zone[16 * n : 16 * n + 16]
+        out[where, 16:32, :] = block[16:]
 
 
 def finish_kernel(place, terms, eta, phi, eta_next, phi_next):
@@ -310,10 +315,10 @@
             surface = eta[a, rows, :]
             potential = phi[a, rows, :]
             part_of = slice(8 * a, 8 * a + 8)
-            added = terms[2 * z, part_of, :] + terms[2 * z + 1, part_of, :]
+            added = terms[z, part_of, :] + terms[4 + z, part_of, :]
             eta_next[a, rows, :] = surface + kappa * potential + added
             part_of = slice(16 + 8 * a, 24 + 8 * a)
-            added = terms[2 * z, part_of, :] + terms[2 * z + 1, part_of, :]
+            added = terms[z, part_of, :] + terms[4 + z, part_of, :]
             phi_next[a, rows, :] = potential - (time_step * gravity) * surface + added
 
 
@@ -376,12 +381,12 @@
     def turn(words):
         return swap(words.reshape(256, 1, 384), ("wide", "lane")).reshape(768, 128)
 
-    modes = swap(stage_deal(eta_modes, phi_modes), ("lane", "core"))
+    modes = swap(stage_deal(eta_modes, phi_modes), ("core", "lane"))
     ready = stage_source(place, offsets, zone_field)
     modes, (source, places, beyond) = lax.optimization_barrier((modes, ready))
     columns = turn(stage_rows(place, modes))
     rows = turn(stage_columns(columns, source))
-    terms = swap(stage_rows_back(place, rows, places, beyond), ("lane", "core"))
+    terms = swap(stage_rows_back(place, rows, places, beyond), ("core", "lane"))
     return tuple(stage_finish(place, terms, eta_modes, phi_modes))
 
 

time: 102 us -> 103 us (level)
    all_to_all x2, blocking collectives: 57 us -> 58.1 us  [turn(): return swap(words.reshape(256, 1, 384), ('wide', 'lane')).reshape(768, 128)]
where the time goes in v7:
time: 103 us; the launch traced here: 102 us
  blocking collectives  74.3 us (72%)
  starting transfers between devices  10.3 us (10%)
  Pallas kernels  9.45 us (9%)
  waiting for transfers between devices  6.64 us (6%)
    all_to_all x2, blocking collectives, turn(): return swap(words.reshape(256, 1, 384), ('wide', 'lane')).reshape(768, 128)  58.1 us
    all_to_all x1, blocking collectives, local(): terms = swap(stage_rows_back(place, rows, places, beyond), ('core', 'lane'))  16.2 us
    all_to_all x1, starting transfers between devices, local(): modes = swap(stage_deal(eta_modes, phi_modes), ('core', 'lane'))  10.3 us
    pallas_call x6, Pallas kernels, call(): pl.pallas_call(kernel, out_shape=[jax.ShapeDtypeStruct(s, t) for s, t in...  9.45 us
    all_to_all x1, waiting for transfers between devices, local(): modes = swap(stage_deal(eta_modes, phi_modes), ('core', 'lane'))  6.64 us
  transfers between devices with their start and end apart: 1, of which 1 were waited for; matrix products, arithmetic and copies ran while one was open for 0% of the time, Pallas kernels for 2%

profile of v7, /device:TPU:1, one launch (start us, length us, event | category | flops | bytes accessed | tf_op | source)
XLA Modules:
  0.0 102.3 jit_solution(6181482818612767984)
XLA Ops:
  0.6 0.0 copy-start.12
  0.6 1.6 %deal_kernel.1 = f32[8,32,256]{2,1,0:T(8,128)} custom-call(f32[2,32,256]{2,1,0:T(8,128)} %eta.3, f32[2,32,256]{2,1,0:T(8,128)} %phi.3), custom_call_target="tpu_custom_call" | custom-call | flops 8589934592 | bytes 393216 | tf_op jit(solution)/shard_map/deal_kernel/pallas_call | solution.py:332
  2.3 10.3 %all-to-all-start = ((f32[8,32,256]{2,1,0:T(8,128)}), f32[8,32,256]{2,1,0:T(8,128)S(1)}, u32[]{:S(2)}, u32[]{:S(2)}) async-start(f32[8,32,256]{2,1,0:T(8,128)} %deal_kernel.1), calls=%async_computation | async-start | bytes 524288 | tf_op jit(solution)/shard_map/all_to_all | solution.py:384
  12.6 0.1 copy.17.offsets
  12.7 0.1 pad_add_fusion.place
  12.8 0.6 copy-done.7
  13.4 1.6 %source_kernel.1 = (f32[256,256]{1,0:T(8,128)S(1)}, bf16[512,256]{1,0:T(8,128)(2,1)S(1)}, f32[128,256]{1,0:T(8,128)S(1)}) custom-call(s32[3]{0:T(128)S(1)} %pad_add_fusion.place, s32[64,2]{1,0:T(8,128)S(1)} %copy.17.offsets, f32[64,128]{1,0:T(8,128)S(1)} %copy-done.7), custom_call_target="tpu_custom_call" | custom-call | flops 67108864 | bytes 950272 | tf_op jit(solution)/shard_map/source_kernel/pallas_call | solution.py:332
  15.0 6.6 %all-to-all-done.modes = f32[8,32,256]{2,1,0:T(8,128)S(1)} async-done(((f32[8,32,256]{2,1,0:T(8,128)}), f32[8,32,256]{2,1,0:T(8,128)S(1)}, u32[]{:S(2)}, u32[]{:S(2)}) %all-to-all-start) | async-done | bytes 262176 | tf_op jit(solution)/shard_map/all_to_all | solution.py:384
  21.7 0.0 copy-start.9
  21.7 0.0 copy-start.10
  21.7 1.4 %rows_kernel.1 = f32[768,128]{1,0:T(8,128)S(1)} custom-call(s32[3]{0:T(128)S(1)} %pad_add_fusion.place, f32[8,32,256]{2,1,0:T(8,128)S(1)} %all-to-all-done.modes, bf16[2,256,128]{2,1,0:T(8,128)(2,1)S(1)} %copy-done.12, f32[2,2,64,256]{3,2,1,0:T(8,128)S(1)} %copy-done.11, bf16[2,256,512]{2,1,0:T(8,128)(2,1)S(1)} %copy-done), custom_call_target="tpu_custom_call" | custom-call | flops 1073741824 | bytes 1572864 | tf_op jit(solution)/shard_map/rows_kernel/pallas_call | solution.py:332
  23.1 0.0 copy-start.8
  23.2 33.8 %all_to_all.20 = f32[256,1,384]{2,1,0:T(1,128)S(1)} all-to-all(f32[256,1,384]{2,1,0:T(1,128)S(1)} %bitcast.10), channel_id=1, replica_groups=mesh['wide'=64,'lane'=4,'core'=2] {'wide','lane'}, dimensions={0} | all-to-all | bytes 786432 | tf_op jit(solution)/shard_map/all_to_all | solution.py:382
  57.0 0.0 copy-start.4
  57.0 1.6 %columns_kernel.1 = f32[768,128]{1,0:T(8,128)S(1)} custom-call(f32[768,128]{1,0:T(8,128)S(1)} %bitcast.8, f32[256,256]{1,0:T(8,128)S(1)} %get-tuple-element.13.source, bf16[2,256,512]{2,1,0:T(8,128)(2,1)S(1)} %copy-done, f32[2,256,128]{2,1,0:T(8,128)S(1)} %copy-done.10, bf16[2,256,640]{2,1,0:T(8,128)(2,1)S(1)} %copy-done.8, bf16[2,256,256]{2,1,0:T(8,128)(2,1)S(1)} %copy-done.9), custom_call_target="tpu_custom_call" | custom-call | flops 1073741824 | bytes 2752512 | tf_op jit(solution)/shard_map/columns_kernel/pallas_call | solution.py:332
  58.6 0.0 copy-start.1
  58.6 0.0 copy-start.2
  58.6 0.0 copy-start.3
  58.6 24.2 %all_to_all.21 = f32[256,1,384]{2,1,0:T(1,128)S(1)} all-to-all(f32[256,1,384]{2,1,0:T(1,128)S(1)} %bitcast.9), channel_id=1, replica_groups=mesh['wide'=64,'lane'=4,'core'=2] {'wide','lane'}, dimensions={0} | all-to-all | bytes 786432 | tf_op jit(solution)/shard_map/all_to_all | solution.py:382
  82.9 1.9 %rows_back_kernel.1 = f32[8,32,256]{2,1,0:T(8,128)S(1)} custom-call(s32[3]{0:T(128)S(1)} %pad_add_fusion.place, f32[768,128]{1,0:T(8,128)S(1)} %bitcast.7, bf16[512,256]{1,0:T(8,128)(2,1)S(1)} %get-tuple-element.14.places, f32[128,256]{1,0:T(8,128)S(1)} %get-tuple-element.15.beyond, bf16[2,256,512]{2,1,0:T(8,128)(2,1)S(1)} %copy-done, ...), custom_call_target="tpu_custom_call" | custom-call | flops 536870912 | bytes 2490368 | tf_op jit(solution)/shard_map/rows_back_kernel/pallas_call | solution.py:332
  84.8 0.0 copy-start.5
  84.8 0.0 copy-start.6
  84.8 16.2 %all_to_all.22.terms = f32[8,32,256]{2,1,0:T(8,128)S(1)} all-to-all(f32[8,32,256]{2,1,0:T(8,128)S(1)} %rows_back_kernel.1), channel_id=1, replica_groups=mesh['wide'=64,'lane'=4,'core'=2] {'core','lane'}, dimensions={0} | all-to-all | bytes 524288 | tf_op jit(solution)/shard_map/all_to_all | solution.py:389
  101.1 1.2 %finish_kernel.1 = (f32[2,32,256]{2,1,0:T(8,128)}, f32[2,32,256]{2,1,0:T(8,128)}) custom-call(s32[3]{0:T(128)S(1)} %pad_add_fusion.place, f32[8,32,256]{2,1,0:T(8,128)S(1)} %all_to_all.22.terms, f32[2,32,256]{2,1,0:T(8,128)S(1)} %copy-done.5, f32[2,32,256]{2,1,0:T(8,128)S(1)} %copy-done.6), custom_call_target="tpu_custom_call" | custom-call | bytes 524288 | tf_op jit(solution)/shard_map/finish_kernel/pallas_call | solution.py:332
  (17 shorter events, 0.0 us)
Async XLA Ops:
  0.6 21.0 %copy-start.12 = (bf16[2,256,128]{2,1,0:T(8,128)(2,1)S(1)}, bf16[2,256,128]{2,1,0:T(8,128)(2,1)}, u32[]{:S(2)}) copy-start(bf16[2,256,128]{2,1,0:T(8,128)(2,1)} %constant.33.clone.mix) | copy-start | bytes 393220
  2.3 10.4 %copy-start.13 = (s32[64,2]{0,1:T(2,128)S(1)}, s32[64,2]{0,1:T(2,128)}, u32[]{:S(2)}) copy-start(s32[64,2]{0,1:T(2,128)} %param.17) | copy-start | bytes 1540
  2.3 19.4 %copy-start = (bf16[2,256,512]{2,1,0:T(8,128)(2,1)S(1)}, bf16[2,256,512]{2,1,0:T(8,128)(2,1)}, u32[]{:S(2)}) copy-start(bf16[2,256,512]{2,1,0:T(8,128)(2,1)} %constant.35.clone.circles) | copy-start | bytes 1572868
  2.3 19.4 %all-to-all-start = ((f32[8,32,256]{2,1,0:T(8,128)}), f32[8,32,256]{2,1,0:T(8,128)S(1)}, u32[]{:S(2)}, u32[]{:S(2)}) async-start(f32[8,32,256]{2,1,0:T(8,128)} %deal_kernel.1), calls=%async_computation | async-start | bytes 524288 | tf_op jit(solution)/shard_map/all_to_all | solution.py:384
  12.6 0.8 copy-start.7
  12.6 9.1 %copy-start.11 = (f32[2,2,64,256]{3,2,1,0:T(8,128)S(1)}, f32[2,2,64,256]{3,2,1,0:T(8,128)}, u32[]{:S(2)}) copy-start(f32[2,2,64,256]{3,2,1,0:T(8,128)} %constant.34.clone.turn) | copy-start | bytes 786436
  21.7 35.3 %copy-start.9 = (bf16[2,256,256]{2,1,0:T(8,128)(2,1)S(1)}, bf16[2,256,256]{2,1,0:T(8,128)(2,1)}, u32[]{:S(2)}) copy-start(bf16[2,256,256]{2,1,0:T(8,128)(2,1)} %constant.38.clone.deal) | copy-start | bytes 786436
  21.7 35.3 %copy-start.10 = (f32[2,256,128]{2,1,0:T(8,128)S(1)}, f32[2,256,128]{2,1,0:T(8,128)}, u32[]{:S(2)}) copy-start(f32[2,256,128]{2,1,0:T(8,128)} %constant.36.clone.turn) | copy-start | bytes 786436
  23.1 33.8 %copy-start.8 = (bf16[2,256,640]{2,1,0:T(8,128)(2,1)S(1)}, bf16[2,256,640]{2,1,0:T(8,128)(2,1)}, u32[]{:S(2)}) copy-start(bf16[2,256,640]{2,1,0:T(8,128)(2,1)} %constant.37.clone.gather) | copy-start | bytes 1966084
  57.0 25.9 %copy-start.4 = (f32[2,2,32,256]{3,2,1,0:T(8,128)S(1)}, f32[2,2,32,256]{3,2,1,0:T(8,128)}, u32[]{:S(2)}) copy-start(f32[2,2,32,256]{3,2,1,0:T(8,128)} %constant.39.clone.main_turn) | copy-start | bytes 393220
  58.6 24.3 %copy-start.1 = (bf16[2,128,512]{2,1,0:T(8,128)(2,1)S(1)}, bf16[2,128,512]{2,1,0:T(8,128)(2,1)}, u32[]{:S(2)}) copy-start(bf16[2,128,512]{2,1,0:T(8,128)(2,1)} %constant.42.clone.zone_mix) | copy-start | bytes 786436
  58.6 24.3 %copy-start.2 = (bf16[2,256,256]{2,1,0:T(8,128)(2,1)S(1)}, bf16[2,256,256]{2,1,0:T(8,128)(2,1)}, u32[]{:S(2)}) copy-start(bf16[2,256,256]{2,1,0:T(8,128)(2,1)} %constant.41.clone.main_mix) | copy-start | bytes 786436
  58.6 24.3 %copy-start.3 = (f32[2,128,256]{2,1,0:T(8,128)S(1)}, f32[2,128,256]{2,1,0:T(8,128)}, u32[]{:S(2)}) copy-start(f32[2,128,256]{2,1,0:T(8,128)} %constant.40.clone.zone_turn) | copy-start | bytes 786436
  84.8 16.2 %copy-start.5 = (f32[2,32,256]{2,1,0:T(8,128)S(1)}, f32[2,32,256]{2,1,0:T(8,128)}, u32[]{:S(2)}) copy-start(f32[2,32,256]{2,1,0:T(8,128)} %eta.3) | copy-start | bytes 196612
  84.8 16.2 %copy-start.6 = (f32[2,32,256]{2,1,0:T(8,128)S(1)}, f32[2,32,256]{2,1,0:T(8,128)}, u32[]{:S(2)}) copy-start(f32[2,32,256]{2,1,0:T(8,128)} %phi.3) | copy-start | bytes 196612

commit v8 on v7

--- a/solution.py
+++ b/solution.py
@@ -379,7 +379,7 @@
     swap = functools.partial(lax.all_to_all, split_axis=0, concat_axis=0, tiled=True)
 
     def turn(words):
-        return swap(words.reshape(256, 1, 384), ("wide", "lane")).reshape(768, 128)
+        return swap(words.reshape(256, 3, 1, 128), ("wide", "lane")).reshape(768, 128)
 
     modes = swap(stage_deal(eta_modes, phi_modes), ("core", "lane"))
     ready = stage_source(place, offsets, zone_field)

time: 103 us -> 103 us (level)
  no operation moved by 1% of the time
where the time goes in v8:
time: 103 us; the launch traced here: 102 us
  blocking collectives  74.3 us (72%)
  starting transfers between devices  10.3 us (10%)
  Pallas kernels  9.45 us (9%)
  waiting for transfers between devices  6.64 us (6%)
    all_to_all x2, blocking collectives, turn(): swap(words.reshape(256, 3, 1, 128), ('wide', 'lane')).reshape(768, 128)  58.1 us
    all_to_all x1, blocking collectives, local(): terms = swap(stage_rows_back(place, rows, places, beyond), ('core', 'lane'))  16.2 us
    all_to_all x1, starting transfers between devices, local(): modes = swap(stage_deal(eta_modes, phi_modes), ('core', 'lane'))  10.3 us
    pallas_call x6, Pallas kernels, call(): pl.pallas_call(kernel, out_shape=[jax.ShapeDtypeStruct(s, t) for s, t in...  9.45 us
    all_to_all x1, waiting for transfers between devices, local(): modes = swap(stage_deal(eta_modes, phi_modes), ('core', 'lane'))  6.64 us
  transfers between devices with their start and end apart: 1, of which 1 were waited for; matrix products, arithmetic and copies ran while one was open for 0% of the time, Pallas kernels for 2%

profile of v8, /device:TPU:1, one launch (start us, length us, event | category | flops | bytes accessed | tf_op | source)
XLA Modules:
  0.0 102.3 jit_solution(6181482818612767984)
XLA Ops:
  0.6 0.0 copy-start.12
  0.6 1.6 %deal_kernel.1 = f32[8,32,256]{2,1,0:T(8,128)} custom-call(f32[2,32,256]{2,1,0:T(8,128)} %eta.3, f32[2,32,256]{2,1,0:T(8,128)} %phi.3), custom_call_target="tpu_custom_call" | custom-call | flops 8589934592 | bytes 393216 | tf_op jit(solution)/shard_map/deal_kernel/pallas_call | solution.py:332
  2.3 10.3 %all-to-all-start = ((f32[8,32,256]{2,1,0:T(8,128)}), f32[8,32,256]{2,1,0:T(8,128)S(1)}, u32[]{:S(2)}, u32[]{:S(2)}) async-start(f32[8,32,256]{2,1,0:T(8,128)} %deal_kernel.1), calls=%async_computation | async-start | bytes 524288 | tf_op jit(solution)/shard_map/all_to_all | solution.py:384
  12.6 0.1 copy.18.offsets
  12.7 0.1 pad_add_fusion.place
  12.8 0.6 copy-done.7
  13.4 1.6 %source_kernel.1 = (f32[256,256]{1,0:T(8,128)S(1)}, bf16[512,256]{1,0:T(8,128)(2,1)S(1)}, f32[128,256]{1,0:T(8,128)S(1)}) custom-call(s32[3]{0:T(128)S(1)} %pad_add_fusion.place, s32[64,2]{1,0:T(8,128)S(1)} %copy.18.offsets, f32[64,128]{1,0:T(8,128)S(1)} %copy-done.7), custom_call_target="tpu_custom_call" | custom-call | flops 67108864 | bytes 950272 | tf_op jit(solution)/shard_map/source_kernel/pallas_call | solution.py:332
  15.0 6.6 %all-to-all-done.modes = f32[8,32,256]{2,1,0:T(8,128)S(1)} async-done(((f32[8,32,256]{2,1,0:T(8,128)}), f32[8,32,256]{2,1,0:T(8,128)S(1)}, u32[]{:S(2)}, u32[]{:S(2)}) %all-to-all-start) | async-done | bytes 262176 | tf_op jit(solution)/shard_map/all_to_all | solution.py:384
  21.7 0.0 copy-start.9
  21.7 0.0 copy-start.10
  21.7 1.4 %rows_kernel.1 = f32[768,128]{1,0:T(8,128)S(1)} custom-call(s32[3]{0:T(128)S(1)} %pad_add_fusion.place, f32[8,32,256]{2,1,0:T(8,128)S(1)} %all-to-all-done.modes, bf16[2,256,128]{2,1,0:T(8,128)(2,1)S(1)} %copy-done.12, f32[2,2,64,256]{3,2,1,0:T(8,128)S(1)} %copy-done.11, bf16[2,256,512]{2,1,0:T(8,128)(2,1)S(1)} %copy-done), custom_call_target="tpu_custom_call" | custom-call | flops 1073741824 | bytes 1572864 | tf_op jit(solution)/shard_map/rows_kernel/pallas_call | solution.py:332
  23.1 0.0 copy-start.8
  23.2 33.8 %all_to_all.20 = f32[256,3,1,128]{3,2,1,0:T(1,128)S(1)} all-to-all(f32[256,3,1,128]{3,2,1,0:T(1,128)S(1)} %bitcast.10), channel_id=1, replica_groups=mesh['wide'=64,'lane'=4,'core'=2] {'wide','lane'}, dimensions={0} | all-to-all | bytes 786432 | tf_op jit(solution)/shard_map/all_to_all | solution.py:382
  57.0 0.0 copy-start.4
  57.0 1.6 %columns_kernel.1 = f32[768,128]{1,0:T(8,128)S(1)} custom-call(f32[768,128]{1,0:T(8,128)S(1)} %bitcast.8, f32[256,256]{1,0:T(8,128)S(1)} %get-tuple-element.13.source, bf16[2,256,512]{2,1,0:T(8,128)(2,1)S(1)} %copy-done, f32[2,256,128]{2,1,0:T(8,128)S(1)} %copy-done.10, bf16[2,256,640]{2,1,0:T(8,128)(2,1)S(1)} %copy-done.8, bf16[2,256,256]{2,1,0:T(8,128)(2,1)S(1)} %copy-done.9), custom_call_target="tpu_custom_call" | custom-call | flops 1073741824 | bytes 2752512 | tf_op jit(solution)/shard_map/columns_kernel/pallas_call | solution.py:332
  58.6 0.0 copy-start.1
  58.6 0.0 copy-start.2
  58.6 0.0 copy-start.3
  58.6 24.2 %all_to_all.21 = f32[256,3,1,128]{3,2,1,0:T(1,128)S(1)} all-to-all(f32[256,3,1,128]{3,2,1,0:T(1,128)S(1)} %bitcast.9), channel_id=1, replica_groups=mesh['wide'=64,'lane'=4,'core'=2] {'wide','lane'}, dimensions={0} | all-to-all | bytes 786432 | tf_op jit(solution)/shard_map/all_to_all | solution.py:382
  82.9 1.9 %rows_back_kernel.1 = f32[8,32,256]{2,1,0:T(8,128)S(1)} custom-call(s32[3]{0:T(128)S(1)} %pad_add_fusion.place, f32[768,128]{1,0:T(8,128)S(1)} %bitcast.7, bf16[512,256]{1,0:T(8,128)(2,1)S(1)} %get-tuple-element.14.places, f32[128,256]{1,0:T(8,128)S(1)} %get-tuple-element.15.beyond, bf16[2,256,512]{2,1,0:T(8,128)(2,1)S(1)} %copy-done, ...), custom_call_target="tpu_custom_call" | custom-call | flops 536870912 | bytes 2490368 | tf_op jit(solution)/shard_map/rows_back_kernel/pallas_call | solution.py:332
  84.8 0.0 copy-start.5
  84.8 0.0 copy-start.6
  84.8 16.2 %all_to_all.22.terms = f32[8,32,256]{2,1,0:T(8,128)S(1)} all-to-all(f32[8,32,256]{2,1,0:T(8,128)S(1)} %rows_back_kernel.1), channel_id=1, replica_groups=mesh['wide'=64,'lane'=4,'core'=2] {'core','lane'}, dimensions={0} | all-to-all | bytes 524288 | tf_op jit(solution)/shard_map/all_to_all | solution.py:389
  101.1 1.2 %finish_kernel.1 = (f32[2,32,256]{2,1,0:T(8,128)}, f32[2,32,256]{2,1,0:T(8,128)}) custom-call(s32[3]{0:T(128)S(1)} %pad_add_fusion.place, f32[8,32,256]{2,1,0:T(8,128)S(1)} %all_to_all.22.terms, f32[2,32,256]{2,1,0:T(8,128)S(1)} %copy-done.5, f32[2,32,256]{2,1,0:T(8,128)S(1)} %copy-done.6), custom_call_target="tpu_custom_call" | custom-call | bytes 524288 | tf_op jit(solution)/shard_map/finish_kernel/pallas_call | solution.py:332
  (17 shorter events, 0.0 us)
Async XLA Ops:
  0.6 21.0 %copy-start.12 = (bf16[2,256,128]{2,1,0:T(8,128)(2,1)S(1)}, bf16[2,256,128]{2,1,0:T(8,128)(2,1)}, u32[]{:S(2)}) copy-start(bf16[2,256,128]{2,1,0:T(8,128)(2,1)} %constant.33.clone.mix) | copy-start | bytes 393220
  2.3 10.4 %copy-start.13 = (s32[64,2]{0,1:T(2,128)S(1)}, s32[64,2]{0,1:T(2,128)}, u32[]{:S(2)}) copy-start(s32[64,2]{0,1:T(2,128)} %param.17) | copy-start | bytes 1540
  2.3 19.4 %copy-start = (bf16[2,256,512]{2,1,0:T(8,128)(2,1)S(1)}, bf16[2,256,512]{2,1,0:T(8,128)(2,1)}, u32[]{:S(2)}) copy-start(bf16[2,256,512]{2,1,0:T(8,128)(2,1)} %constant.35.clone.circles) | copy-start | bytes 1572868
  2.3 19.4 %all-to-all-start = ((f32[8,32,256]{2,1,0:T(8,128)}), f32[8,32,256]{2,1,0:T(8,128)S(1)}, u32[]{:S(2)}, u32[]{:S(2)}) async-start(f32[8,32,256]{2,1,0:T(8,128)} %deal_kernel.1), calls=%async_computation | async-start | bytes 524288 | tf_op jit(solution)/shard_map/all_to_all | solution.py:384
  12.6 0.8 copy-start.7
  12.6 9.1 %copy-start.11 = (f32[2,2,64,256]{3,2,1,0:T(8,128)S(1)}, f32[2,2,64,256]{3,2,1,0:T(8,128)}, u32[]{:S(2)}) copy-start(f32[2,2,64,256]{3,2,1,0:T(8,128)} %constant.34.clone.turn) | copy-start | bytes 786436
  21.7 35.3 %copy-start.9 = (bf16[2,256,256]{2,1,0:T(8,128)(2,1)S(1)}, bf16[2,256,256]{2,1,0:T(8,128)(2,1)}, u32[]{:S(2)}) copy-start(bf16[2,256,256]{2,1,0:T(8,128)(2,1)} %constant.38.clone.deal) | copy-start | bytes 786436
  21.7 35.3 %copy-start.10 = (f32[2,256,128]{2,1,0:T(8,128)S(1)}, f32[2,256,128]{2,1,0:T(8,128)}, u32[]{:S(2)}) copy-start(f32[2,256,128]{2,1,0:T(8,128)} %constant.36.clone.turn) | copy-start | bytes 786436
  23.1 33.8 %copy-start.8 = (bf16[2,256,640]{2,1,0:T(8,128)(2,1)S(1)}, bf16[2,256,640]{2,1,0:T(8,128)(2,1)}, u32[]{:S(2)}) copy-start(bf16[2,256,640]{2,1,0:T(8,128)(2,1)} %constant.37.clone.gather) | copy-start | bytes 1966084
  57.0 25.9 %copy-start.4 = (f32[2,2,32,256]{3,2,1,0:T(8,128)S(1)}, f32[2,2,32,256]{3,2,1,0:T(8,128)}, u32[]{:S(2)}) copy-start(f32[2,2,32,256]{3,2,1,0:T(8,128)} %constant.39.clone.main_turn) | copy-start | bytes 393220
  58.6 24.3 %copy-start.1 = (bf16[2,128,512]{2,1,0:T(8,128)(2,1)S(1)}, bf16[2,128,512]{2,1,0:T(8,128)(2,1)}, u32[]{:S(2)}) copy-start(bf16[2,128,512]{2,1,0:T(8,128)(2,1)} %constant.42.clone.zone_mix) | copy-start | bytes 786436
  58.6 24.3 %copy-start.2 = (bf16[2,256,256]{2,1,0:T(8,128)(2,1)S(1)}, bf16[2,256,256]{2,1,0:T(8,128)(2,1)}, u32[]{:S(2)}) copy-start(bf16[2,256,256]{2,1,0:T(8,128)(2,1)} %constant.41.clone.main_mix) | copy-start | bytes 786436
  58.6 24.3 %copy-start.3 = (f32[2,128,256]{2,1,0:T(8,128)S(1)}, f32[2,128,256]{2,1,0:T(8,128)}, u32[]{:S(2)}) copy-start(f32[2,128,256]{2,1,0:T(8,128)} %constant.40.clone.zone_turn) | copy-start | bytes 786436
  84.8 16.2 %copy-start.5 = (f32[2,32,256]{2,1,0:T(8,128)S(1)}, f32[2,32,256]{2,1,0:T(8,128)}, u32[]{:S(2)}) copy-start(f32[2,32,256]{2,1,0:T(8,128)} %eta.3) | copy-start | bytes 196612
  84.8 16.2 %copy-start.6 = (f32[2,32,256]{2,1,0:T(8,128)S(1)}, f32[2,32,256]{2,1,0:T(8,128)}, u32[]{:S(2)}) copy-start(f32[2,32,256]{2,1,0:T(8,128)} %phi.3) | copy-start | bytes 196612

commit v9 on v8

--- a/solution.py
+++ b/solution.py
@@ -140,6 +140,10 @@
     return jnp.where(index < 1024, index, index - 2048).astype(f32)
 
 
+def order_of(n):
+    return 4 * (n >> 1 & 1) + 2 * (n >> 2) + (n & 1)
+
+
 def deal_kernel(eta, phi, out):
     for z in range(4):
         for source, base in ((eta, 0), (phi, 16)):
@@ -151,8 +155,8 @@
 
 def source_kernel(place, offsets, zone, out, places, beyond):
     tile = place[0]
-    core = place[2]
-    own = 4 * core + place[1]
+    half = place[2]
+    own = 4 * half + place[1]
     ox = offsets[tile, 0]
     oy = offsets[tile, 1]
     lane = iota((128, 128), 1)
@@ -181,25 +185,25 @@
             x = offsets[t + k, 0]
             target = jnp.where((row >> 2) == k, x >> 3, target)
             edge = jnp.where(tile_of == t + k, 2 * (x & 7), edge)
-        near = (target + (row & 3) + 4 * core) & 255
+        near = (target + (row & 3) + 4 * half) & 255
         far = (target + 8) & 255
         places[4 * t : 4 * t + 16, :] = jnp.where(spot == near, 1.0, 0.0).astype(bf16)
         places[256 + 4 * t : 272 + 4 * t, :] = jnp.where(spot == far, 1.0, 0.0).astype(bf16)
-    edge = jnp.where(((iota((8, 256), 1) & 3) == 0) & (core == 0), edge, 0)
+    edge = jnp.where(((iota((8, 256), 1) & 3) == 0) & (half == 0), edge, 0)
     for p in range(16):
         beyond[8 * p : 8 * p + 8, :] = jnp.where(edge > p, 1.0, 0.0)
 
 
 def rows_kernel(place, modes, mix, turn, circles, out):
     first_ky = 32 * place[0] + 8 * place[1]
-    core = place[2]
-    odd = 1.0 - 2.0 * core.astype(f32)
+    half = place[2]
+    odd = 1.0 - 2.0 * half.astype(f32)
     wave_y = wave_of(first_ky + (iota((16, 256), 0) & 7)) * TURN_Y
     tiles = [[], [], [], [], []]
     for n in range(8):
         wave_x = wave_of(256 * n + iota((16, 256), 1)) * TURN_X
         kappa = jnp.sqrt(wave_x * wave_x + wave_y * wave_y)
-        block = 4 * (n % 2) + n // 2
+        block = order_of(n)
         eta = modes[block, 0:16, :]
         phi = modes[block, 16:32, :]
         if n % 2:
@@ -208,8 +212,8 @@
         terms = (wave_x * eta, wave_y * eta, wave_x * phi, wave_y * phi, kappa * phi)
         for f in range(5):
             tiles[f].append(terms[f])
-    cosine = turn[0, core]
-    sine = turn[1, core]
+    cosine = turn[0, half]
+    sine = turn[1, half]
     parts = [[], []]
     for f in range(5):
         rows = split(jnp.concatenate(tiles[f], 0))
@@ -271,7 +275,7 @@
 def rows_back_kernel(
     place, terms, places, beyond, circles, main_turn, zone_turn, main_mix, zone_mix, out
 ):
-    core = place[2]
+    half = place[2]
     cells = jnp.concatenate(
         [terms[pl.ds(1, 256, stride=3), :], terms[pl.ds(2, 256, stride=3), :]], 1
     ).T
@@ -291,16 +295,16 @@
             jnp.concatenate([real.reshape(count, 256), imag.reshape(count, 256)], 0)
         )
 
-    main = turned(both[:128].reshape(4, 32, 512), main_turn[0, core][None], main_turn[1, core][None])
+    main = turned(both[:128].reshape(4, 32, 512), main_turn[0, half][None], main_turn[1, half][None])
     zone = turned(both[128:].reshape(2, 128, 512), zone_turn[0][None], zone_turn[1][None])
     main = dot3(main_mix, main)
     zone = dot3(zone_mix, zone)
-    odd = 1.0 - 2.0 * core.astype(f32)
+    odd = 1.0 - 2.0 * half.astype(f32)
     for n in range(8):
         block = main[32 * n : 32 * n + 32]
         if n % 2:
             block = block * odd
-        where = 4 * (n % 2) + n // 2
+        where = order_of(n)
         out[where, 0:16, :] = block[:16] + zone[16 * n : 16 * n + 16]
         out[where, 16:32, :] = block[16:]
 
@@ -308,7 +312,8 @@
 def finish_kernel(place, terms, eta, phi, eta_next, phi_next):
     for z in range(4):
         rows = slice(8 * z, 8 * z + 8)
-        wave_x = wave_of(256 * (2 * place[1] + place[2]) + iota((8, 256), 1)) * TURN_X
+        own = 4 * (place[1] >> 1) + 2 * place[2] + (place[1] & 1)
+        wave_x = wave_of(256 * own + iota((8, 256), 1)) * TURN_X
         wave_y = wave_of(32 * place[0] + 8 * z + iota((8, 256), 0)) * TURN_Y
         kappa = time_step * jnp.sqrt(wave_x * wave_x + wave_y * wave_y)
         for a in range(2):
@@ -375,25 +380,27 @@
 
 
 def local(eta_modes, phi_modes, zone_field, offsets):
-    place = jnp.stack([lax.axis_index(axis) for axis in ("wide", "lane", "core")]).astype(jnp.int32)
+    w, h, c, core = (lax.axis_index(axis) for axis in ("wide", "high", "half", "core"))
+    place = jnp.stack([w, 2 * h + core, c]).astype(jnp.int32)
     swap = functools.partial(lax.all_to_all, split_axis=0, concat_axis=0, tiled=True)
 
     def turn(words):
-        return swap(words.reshape(256, 3, 1, 128), ("wide", "lane")).reshape(768, 128)
-
-    modes = swap(stage_deal(eta_modes, phi_modes), ("core", "lane"))
+        return swap(words.reshape(256, 1, 384), ("wide", "high", "core")).reshape(768, 128)
+
+    modes = swap(stage_deal(eta_modes, phi_modes), ("half", "high", "core"))
     ready = stage_source(place, offsets, zone_field)
     modes, (source, places, beyond) = lax.optimization_barrier((modes, ready))
     columns = turn(stage_rows(place, modes))
     rows = turn(stage_columns(columns, source))
-    terms = swap(stage_rows_back(place, rows, places, beyond), ("core", "lane"))
+    terms = swap(stage_rows_back(place, rows, places, beyond), ("half", "high", "core"))
     return tuple(stage_finish(place, terms, eta_modes, phi_modes))
 
 
 def solution(mesh):
     wide, narrow = mesh.devices.shape
-    chips = Mesh(mesh.devices.reshape(wide, narrow // 2, 2), ("wide", "lane", "core"))
-    modes = P(None, "wide", ("lane", "core"))
+    shape = (wide, narrow // 4, 2, 2)
+    chips = Mesh(mesh.devices.reshape(shape), ("wide", "high", "half", "core"))
+    modes = P(None, "wide", ("high", "half", "core"))
     in_specs = (modes, modes, P("wide", None), P())
     return jax.shard_map(
         local, mesh=chips, in_specs=in_specs, out_specs=(modes, modes), check_vma=False

time: 103 us -> 103 us (level); the launches traced: 102 us -> 101 us
  waiting for transfers between devices: 6.64 us -> 3.94 us
  blocking collectives: 74.3 us -> 75.9 us
    all_to_all x1, waiting for transfers between devices: 6.64 us -> 3.94 us  [local(): modes = swap(stage_deal(eta_modes, phi_modes), ('half', 'high', 'core'))]
    all_to_all x3, blocking collectives: 74.3 us -> 75.9 us  [the longest x2 66.6 us: turn(): swap(words.reshape(256, 1, 384), ('wide', 'high', 'core')).reshape(768, 128)]
where the time goes in v9:
time: 103 us; the launch traced here: 101 us
  blocking collectives  75.9 us (74%)
  starting transfers between devices  10.3 us (10%)
  Pallas kernels  9.45 us (9%)
  waiting for transfers between devices  3.94 us (4%)
    all_to_all x2, blocking collectives, turn(): swap(words.reshape(256, 1, 384), ('wide', 'high', 'core')).reshape(768, 128)  66.6 us
    all_to_all x1, starting transfers between devices, local(): modes = swap(stage_deal(eta_modes, phi_modes), ('half', 'high', 'core'))  10.3 us
    pallas_call x6, Pallas kernels, call(): pl.pallas_call(kernel, out_shape=[jax.ShapeDtypeStruct(s, t) for s, t in...  9.45 us
    all_to_all x1, blocking collectives, local(): swap(stage_rows_back(place, rows, places, beyond), ('half', 'high', 'core'))  9.26 us
    all_to_all x1, waiting for transfers between devices, local(): modes = swap(stage_deal(eta_modes, phi_modes), ('half', 'high', 'core'))  3.94 us
  transfers between devices with their start and end apart: 1, of which 1 were waited for; matrix products, arithmetic and copies ran while one was open for 0% of the time, Pallas kernels for 2%

profile of v9, /device:TPU:1, one launch (start us, length us, event | category | flops | bytes accessed | tf_op | source)
XLA Modules:
  0.0 101.2 jit_solution(5052768729337575105)
XLA Ops:
  0.6 0.0 copy-start.12
  0.6 1.6 %deal_kernel.1 = f32[8,32,256]{2,1,0:T(8,128)} custom-call(f32[2,32,256]{2,1,0:T(8,128)} %eta.3, f32[2,32,256]{2,1,0:T(8,128)} %phi.3), custom_call_target="tpu_custom_call" | custom-call | flops 8589934592 | bytes 393216 | tf_op jit(solution)/shard_map/deal_kernel/pallas_call | solution.py:337
  2.3 10.3 %all-to-all-start = ((f32[8,32,256]{2,1,0:T(8,128)}), f32[8,32,256]{2,1,0:T(8,128)S(1)}, u32[]{:S(2)}, u32[]{:S(2)}) async-start(f32[8,32,256]{2,1,0:T(8,128)} %deal_kernel.1), calls=%async_computation | async-start | bytes 524288 | tf_op jit(solution)/shard_map/all_to_all | solution.py:390
  12.6 0.1 copy.17.offsets
  12.7 0.1 pad_add_fusion.place
  12.8 0.6 copy-done.7
  13.3 1.6 %source_kernel.1 = (f32[256,256]{1,0:T(8,128)S(1)}, bf16[512,256]{1,0:T(8,128)(2,1)S(1)}, f32[128,256]{1,0:T(8,128)S(1)}) custom-call(s32[3]{0:T(128)S(1)} %pad_add_fusion.place, s32[64,2]{1,0:T(8,128)S(1)} %copy.17.offsets, f32[64,128]{1,0:T(8,128)S(1)} %copy-done.7), custom_call_target="tpu_custom_call" | custom-call | flops 67108864 | bytes 950272 | tf_op jit(solution)/shard_map/source_kernel/pallas_call | solution.py:337
  15.0 3.9 %all-to-all-done.modes = f32[8,32,256]{2,1,0:T(8,128)S(1)} async-done(((f32[8,32,256]{2,1,0:T(8,128)}), f32[8,32,256]{2,1,0:T(8,128)S(1)}, u32[]{:S(2)}, u32[]{:S(2)}) %all-to-all-start) | async-done | bytes 262176 | tf_op jit(solution)/shard_map/all_to_all | solution.py:390
  18.9 0.0 copy-start.9
  19.0 0.0 copy-start.10
  19.0 1.4 %rows_kernel.1 = f32[768,128]{1,0:T(8,128)S(1)} custom-call(s32[3]{0:T(128)S(1)} %pad_add_fusion.place, f32[8,32,256]{2,1,0:T(8,128)S(1)} %all-to-all-done.modes, bf16[2,256,128]{2,1,0:T(8,128)(2,1)S(1)} %copy-done.12, f32[2,2,64,256]{3,2,1,0:T(8,128)S(1)} %copy-done.11, bf16[2,256,512]{2,1,0:T(8,128)(2,1)S(1)} %copy-done), custom_call_target="tpu_custom_call" | custom-call | flops 1073741824 | bytes 1572864 | tf_op jit(solution)/shard_map/rows_kernel/pallas_call | solution.py:337
  20.4 0.0 copy-start.8
  20.4 39.4 %all_to_all.20 = f32[256,1,384]{2,1,0:T(1,128)S(1)} all-to-all(f32[256,1,384]{2,1,0:T(1,128)S(1)} %bitcast.10), channel_id=1, replica_groups=mesh['wide'=64,'high'=2,'half'=2,'core'=2] {'wide','high','core'}, dimensions={0} | all-to-all | bytes 786432 | tf_op jit(solution)/shard_map/all_to_all | solution.py:388
  59.8 0.0 copy-start.4
  59.8 1.6 %columns_kernel.1 = f32[768,128]{1,0:T(8,128)S(1)} custom-call(f32[768,128]{1,0:T(8,128)S(1)} %bitcast.8, f32[256,256]{1,0:T(8,128)S(1)} %get-tuple-element.13.source, bf16[2,256,512]{2,1,0:T(8,128)(2,1)S(1)} %copy-done, f32[2,256,128]{2,1,0:T(8,128)S(1)} %copy-done.10, bf16[2,256,640]{2,1,0:T(8,128)(2,1)S(1)} %copy-done.8, bf16[2,256,256]{2,1,0:T(8,128)(2,1)S(1)} %copy-done.9), custom_call_target="tpu_custom_call" | custom-call | flops 1073741824 | bytes 2752512 | tf_op jit(solution)/shard_map/columns_kernel/pallas_call | solution.py:337
  61.4 0.0 copy-start.1
  61.4 0.0 copy-start.2
  61.5 0.0 copy-start.3
  61.5 27.2 %all_to_all.21 = f32[256,1,384]{2,1,0:T(1,128)S(1)} all-to-all(f32[256,1,384]{2,1,0:T(1,128)S(1)} %bitcast.9), channel_id=1, replica_groups=mesh['wide'=64,'high'=2,'half'=2,'core'=2] {'wide','high','core'}, dimensions={0} | all-to-all | bytes 786432 | tf_op jit(solution)/shard_map/all_to_all | solution.py:388
  88.7 1.9 %rows_back_kernel.1 = f32[8,32,256]{2,1,0:T(8,128)S(1)} custom-call(s32[3]{0:T(128)S(1)} %pad_add_fusion.place, f32[768,128]{1,0:T(8,128)S(1)} %bitcast.7, bf16[512,256]{1,0:T(8,128)(2,1)S(1)} %get-tuple-element.14.places, f32[128,256]{1,0:T(8,128)S(1)} %get-tuple-element.15.beyond, bf16[2,256,512]{2,1,0:T(8,128)(2,1)S(1)} %copy-done, ...), custom_call_target="tpu_custom_call" | custom-call | flops 536870912 | bytes 2490368 | tf_op jit(solution)/shard_map/rows_back_kernel/pallas_call | solution.py:337
  90.6 0.0 copy-start.5
  90.7 0.0 copy-start.6
  90.7 9.3 %all_to_all.22.terms = f32[8,32,256]{2,1,0:T(8,128)S(1)} all-to-all(f32[8,32,256]{2,1,0:T(8,128)S(1)} %rows_back_kernel.1), channel_id=1, replica_groups=mesh['wide'=64,'high'=2,'half'=2,'core'=2] {'half','high','core'}, dimensions={0} | all-to-all | bytes 524288 | tf_op jit(solution)/shard_map/all_to_all | solution.py:395
  99.9 1.2 %finish_kernel.1 = (f32[2,32,256]{2,1,0:T(8,128)}, f32[2,32,256]{2,1,0:T(8,128)}) custom-call(s32[3]{0:T(128)S(1)} %pad_add_fusion.place, f32[8,32,256]{2,1,0:T(8,128)S(1)} %all_to_all.22.terms, f32[2,32,256]{2,1,0:T(8,128)S(1)} %copy-done.5, f32[2,32,256]{2,1,0:T(8,128)S(1)} %copy-done.6), custom_call_target="tpu_custom_call" | custom-call | bytes 524288 | tf_op jit(solution)/shard_map/finish_kernel/pallas_call | solution.py:337
  (17 shorter events, 0.0 us)
Async XLA Ops:
  0.6 18.3 %copy-start.12 = (bf16[2,256,128]{2,1,0:T(8,128)(2,1)S(1)}, bf16[2,256,128]{2,1,0:T(8,128)(2,1)}, u32[]{:S(2)}) copy-start(bf16[2,256,128]{2,1,0:T(8,128)(2,1)} %constant.38.clone.mix) | copy-start | bytes 393220
  2.3 10.3 %copy-start.13 = (s32[64,2]{0,1:T(2,128)S(1)}, s32[64,2]{0,1:T(2,128)}, u32[]{:S(2)}) copy-start(s32[64,2]{0,1:T(2,128)} %param.17) | copy-start | bytes 1540
  2.3 16.7 %copy-start = (bf16[2,256,512]{2,1,0:T(8,128)(2,1)S(1)}, bf16[2,256,512]{2,1,0:T(8,128)(2,1)}, u32[]{:S(2)}) copy-start(bf16[2,256,512]{2,1,0:T(8,128)(2,1)} %constant.40.clone.circles) | copy-start | bytes 1572868
  2.3 16.7 %all-to-all-start = ((f32[8,32,256]{2,1,0:T(8,128)}), f32[8,32,256]{2,1,0:T(8,128)S(1)}, u32[]{:S(2)}, u32[]{:S(2)}) async-start(f32[8,32,256]{2,1,0:T(8,128)} %deal_kernel.1), calls=%async_computation | async-start | bytes 524288 | tf_op jit(solution)/shard_map/all_to_all | solution.py:390
  12.6 0.8 copy-start.7
  12.6 6.4 %copy-start.11 = (f32[2,2,64,256]{3,2,1,0:T(8,128)S(1)}, f32[2,2,64,256]{3,2,1,0:T(8,128)}, u32[]{:S(2)}) copy-start(f32[2,2,64,256]{3,2,1,0:T(8,128)} %constant.39.clone.turn) | copy-start | bytes 786436
  18.9 40.8 %copy-start.9 = (bf16[2,256,256]{2,1,0:T(8,128)(2,1)S(1)}, bf16[2,256,256]{2,1,0:T(8,128)(2,1)}, u32[]{:S(2)}) copy-start(bf16[2,256,256]{2,1,0:T(8,128)(2,1)} %constant.43.clone.deal) | copy-start | bytes 786436
  19.0 40.8 %copy-start.10 = (f32[2,256,128]{2,1,0:T(8,128)S(1)}, f32[2,256,128]{2,1,0:T(8,128)}, u32[]{:S(2)}) copy-start(f32[2,256,128]{2,1,0:T(8,128)} %constant.41.clone.turn) | copy-start | bytes 786436
  20.4 39.4 %copy-start.8 = (bf16[2,256,640]{2,1,0:T(8,128)(2,1)S(1)}, bf16[2,256,640]{2,1,0:T(8,128)(2,1)}, u32[]{:S(2)}) copy-start(bf16[2,256,640]{2,1,0:T(8,128)(2,1)} %constant.42.clone.gather) | copy-start | bytes 1966084
  59.8 28.9 %copy-start.4 = (f32[2,2,32,256]{3,2,1,0:T(8,128)S(1)}, f32[2,2,32,256]{3,2,1,0:T(8,128)}, u32[]{:S(2)}) copy-start(f32[2,2,32,256]{3,2,1,0:T(8,128)} %constant.44.clone.main_turn) | copy-start | bytes 393220
  61.4 27.3 %copy-start.1 = (bf16[2,128,512]{2,1,0:T(8,128)(2,1)S(1)}, bf16[2,128,512]{2,1,0:T(8,128)(2,1)}, u32[]{:S(2)}) copy-start(bf16[2,128,512]{2,1,0:T(8,128)(2,1)} %constant.47.clone.zone_mix) | copy-start | bytes 786436
  61.4 27.3 %copy-start.2 = (bf16[2,256,256]{2,1,0:T(8,128)(2,1)S(1)}, bf16[2,256,256]{2,1,0:T(8,128)(2,1)}, u32[]{:S(2)}) copy-start(bf16[2,256,256]{2,1,0:T(8,128)(2,1)} %constant.46.clone.main_mix) | copy-start | bytes 786436
  61.5 27.3 %copy-start.3 = (f32[2,128,256]{2,1,0:T(8,128)S(1)}, f32[2,128,256]{2,1,0:T(8,128)}, u32[]{:S(2)}) copy-start(f32[2,128,256]{2,1,0:T(8,128)} %constant.45.clone.zone_turn) | copy-start | bytes 786436
  90.6 9.3 %copy-start.5 = (f32[2,32,256]{2,1,0:T(8,128)S(1)}, f32[2,32,256]{2,1,0:T(8,128)}, u32[]{:S(2)}) copy-start(f32[2,32,256]{2,1,0:T(8,128)} %eta.3) | copy-start | bytes 196612
  90.7 9.3 %copy-start.6 = (f32[2,32,256]{2,1,0:T(8,128)S(1)}, f32[2,32,256]{2,1,0:T(8,128)}, u32[]{:S(2)}) copy-start(f32[2,32,256]{2,1,0:T(8,128)} %phi.3) | copy-start | bytes 196612

commit v10 on v5

--- a/solution.py
+++ b/solution.py
@@ -113,7 +113,10 @@
 
 
 def dot3(left, right, dims=((1,), (0,))):
-    return dot(left[0], right[0], dims) + (dot(left[0], right[1], dims) + dot(left[1], right[0], dims))
+    along = dims[0][0], dims[1][0]
+    left = jnp.concatenate([left[0], left[0], left[1]], along[0])
+    right = jnp.concatenate([right[0], right[1], right[0]], along[1])
+    return dot(left, right, dims)
 
 
 def iota(shape, dim):
@@ -272,8 +275,8 @@
         [terms[pl.ds(1, 256, stride=3), :], terms[pl.ds(2, 256, stride=3), :]], 1
     ).T
     far = cells * jnp.concatenate([beyond[...], beyond[...]], 0)
-    high, low = split(jnp.concatenate([cells - far, far], 1))
-    grid = dot(high, places[...]) + dot(low, places[...])
+    cells = jnp.concatenate(split(jnp.concatenate([cells - far, far], 1)), 1)
+    grid = dot(cells, jnp.concatenate([places[...], places[...]], 0))
     main = terms[pl.ds(0, 256, stride=3), :].T
     both = dot3(split(jnp.concatenate([main, grid], 0)), circles)
 

time: 102 us -> 102 us (level)
  no operation moved by 1% of the time
where the time goes in v10:
time: 102 us; the launch traced here: 101 us
  blocking collectives  73.5 us (72%)
  starting transfers between devices  10.3 us (10%)
  Pallas kernels  9.46 us (9%)
  waiting for transfers between devices  6.32 us (6%)
    all_to_all x2, blocking collectives, turn(): return swap(words.reshape(256, 1, 384), ('wide', 'lane')).reshape(768, 128)  57.1 us
    all_to_all x1, blocking collectives, local(): terms = swap(stage_rows_back(place, rows, places, beyond), ('lane', 'core'))  16.4 us
    all_to_all x1, starting transfers between devices, local(): modes = swap(stage_deal(eta_modes, phi_modes), ('lane', 'core'))  10.3 us
    pallas_call x6, Pallas kernels, call(): pl.pallas_call(kernel, out_shape=[jax.ShapeDtypeStruct(s, t) for s, t in...  9.46 us
    all_to_all x1, waiting for transfers between devices, local(): modes = swap(stage_deal(eta_modes, phi_modes), ('lane', 'core'))  6.32 us
  transfers between devices with their start and end apart: 1, of which 1 were waited for; matrix products, arithmetic and copies ran while one was open for 0% of the time, Pallas kernels for 2%

profile of v10, /device:TPU:1, one launch (start us, length us, event | category | flops | bytes accessed | tf_op | source)
XLA Modules:
  0.0 101.1 jit_solution(1837529061243478530)
XLA Ops:
  0.6 0.0 copy-start.12
  0.6 1.6 %deal_kernel.1 = f32[8,32,256]{2,1,0:T(8,128)} custom-call(f32[2,32,256]{2,1,0:T(8,128)} %eta.3, f32[2,32,256]{2,1,0:T(8,128)} %phi.3), custom_call_target="tpu_custom_call" | custom-call | flops 8589934592 | bytes 393216 | tf_op jit(solution)/shard_map/deal_kernel/pallas_call | solution.py:330
  2.3 10.3 %all-to-all-start = ((f32[8,32,256]{2,1,0:T(8,128)}), f32[8,32,256]{2,1,0:T(8,128)S(1)}, u32[]{:S(2)}, u32[]{:S(2)}) async-start(f32[8,32,256]{2,1,0:T(8,128)} %deal_kernel.1), calls=%async_computation | async-start | bytes 524288 | tf_op jit(solution)/shard_map/all_to_all | solution.py:382
  12.6 0.1 copy.17.offsets
  12.7 0.1 pad_add_fusion.place
  12.8 0.6 copy-done.7
  13.3 1.6 %source_kernel.1 = (f32[256,256]{1,0:T(8,128)S(1)}, bf16[512,256]{1,0:T(8,128)(2,1)S(1)}, f32[128,256]{1,0:T(8,128)S(1)}) custom-call(s32[3]{0:T(128)S(1)} %pad_add_fusion.place, s32[64,2]{1,0:T(8,128)S(1)} %copy.17.offsets, f32[64,128]{1,0:T(8,128)S(1)} %copy-done.7), custom_call_target="tpu_custom_call" | custom-call | flops 67108864 | bytes 950272 | tf_op jit(solution)/shard_map/source_kernel/pallas_call | solution.py:330
  15.0 6.3 %all-to-all-done.modes = f32[8,32,256]{2,1,0:T(8,128)S(1)} async-done(((f32[8,32,256]{2,1,0:T(8,128)}), f32[8,32,256]{2,1,0:T(8,128)S(1)}, u32[]{:S(2)}, u32[]{:S(2)}) %all-to-all-start) | async-done | bytes 262176 | tf_op jit(solution)/shard_map/all_to_all | solution.py:382
  21.3 0.0 copy-start.9
  21.3 0.0 copy-start.10
  21.4 1.4 %rows_kernel.1 = f32[768,128]{1,0:T(8,128)S(1)} custom-call(s32[3]{0:T(128)S(1)} %pad_add_fusion.place, f32[8,32,256]{2,1,0:T(8,128)S(1)} %all-to-all-done.modes, bf16[2,256,128]{2,1,0:T(8,128)(2,1)S(1)} %copy-done.12, f32[2,2,64,256]{3,2,1,0:T(8,128)S(1)} %copy-done.11, bf16[2,256,512]{2,1,0:T(8,128)(2,1)S(1)} %copy-done), custom_call_target="tpu_custom_call" | custom-call | flops 1073741824 | bytes 1572864 | tf_op jit(solution)/shard_map/rows_kernel/pallas_call | solution.py:330
  22.8 0.0 copy-start.8
  22.8 33.0 %all_to_all.20 = f32[256,1,384]{2,1,0:T(1,128)S(1)} all-to-all(f32[256,1,384]{2,1,0:T(1,128)S(1)} %bitcast.10), channel_id=1, replica_groups=mesh['wide'=64,'lane'=4,'core'=2] {'wide','lane'}, dimensions={0} | all-to-all | bytes 786432 | tf_op jit(solution)/shard_map/all_to_all | solution.py:380
  55.8 0.0 copy-start.4
  55.8 1.6 %columns_kernel.1 = f32[768,128]{1,0:T(8,128)S(1)} custom-call(f32[768,128]{1,0:T(8,128)S(1)} %bitcast.8, f32[256,256]{1,0:T(8,128)S(1)} %get-tuple-element.13.source, bf16[2,256,512]{2,1,0:T(8,128)(2,1)S(1)} %copy-done, f32[2,256,128]{2,1,0:T(8,128)S(1)} %copy-done.10, bf16[2,256,640]{2,1,0:T(8,128)(2,1)S(1)} %copy-done.8, bf16[2,256,256]{2,1,0:T(8,128)(2,1)S(1)} %copy-done.9), custom_call_target="tpu_custom_call" | custom-call | flops 1073741824 | bytes 2752512 | tf_op jit(solution)/shard_map/columns_kernel/pallas_call | solution.py:330
  57.4 0.0 copy-start.1
  57.4 0.0 copy-start.2
  57.4 0.0 copy-start.3
  57.5 24.1 %all_to_all.21 = f32[256,1,384]{2,1,0:T(1,128)S(1)} all-to-all(f32[256,1,384]{2,1,0:T(1,128)S(1)} %bitcast.9), channel_id=1, replica_groups=mesh['wide'=64,'lane'=4,'core'=2] {'wide','lane'}, dimensions={0} | all-to-all | bytes 786432 | tf_op jit(solution)/shard_map/all_to_all | solution.py:380
  81.6 1.9 %rows_back_kernel.1 = f32[8,32,256]{2,1,0:T(8,128)S(1)} custom-call(s32[3]{0:T(128)S(1)} %pad_add_fusion.place, f32[768,128]{1,0:T(8,128)S(1)} %bitcast.7, bf16[512,256]{1,0:T(8,128)(2,1)S(1)} %get-tuple-element.14.places, f32[128,256]{1,0:T(8,128)S(1)} %get-tuple-element.15.beyond, bf16[2,256,512]{2,1,0:T(8,128)(2,1)S(1)} %copy-done, ...), custom_call_target="tpu_custom_call" | custom-call | flops 536870912 | bytes 2490368 | tf_op jit(solution)/shard_map/rows_back_kernel/pallas_call | solution.py:330
  83.5 0.0 copy-start.5
  83.5 0.0 copy-start.6
  83.5 16.4 %all_to_all.22.terms = f32[8,32,256]{2,1,0:T(8,128)S(1)} all-to-all(f32[8,32,256]{2,1,0:T(8,128)S(1)} %rows_back_kernel.1), channel_id=1, replica_groups=mesh['wide'=64,'lane'=4,'core'=2] {'lane','core'}, dimensions={0} | all-to-all | bytes 524288 | tf_op jit(solution)/shard_map/all_to_all | solution.py:387
  99.9 1.2 %finish_kernel.1 = (f32[2,32,256]{2,1,0:T(8,128)}, f32[2,32,256]{2,1,0:T(8,128)}) custom-call(s32[3]{0:T(128)S(1)} %pad_add_fusion.place, f32[8,32,256]{2,1,0:T(8,128)S(1)} %all_to_all.22.terms, f32[2,32,256]{2,1,0:T(8,128)S(1)} %copy-done.5, f32[2,32,256]{2,1,0:T(8,128)S(1)} %copy-done.6), custom_call_target="tpu_custom_call" | custom-call | bytes 524288 | tf_op jit(solution)/shard_map/finish_kernel/pallas_call | solution.py:330
  (17 shorter events, 0.0 us)
Async XLA Ops:
  0.6 20.7 %copy-start.12 = (bf16[2,256,128]{2,1,0:T(8,128)(2,1)S(1)}, bf16[2,256,128]{2,1,0:T(8,128)(2,1)}, u32[]{:S(2)}) copy-start(bf16[2,256,128]{2,1,0:T(8,128)(2,1)} %constant.33.clone.mix) | copy-start | bytes 393220
  2.3 10.3 %copy-start.13 = (s32[64,2]{0,1:T(2,128)S(1)}, s32[64,2]{0,1:T(2,128)}, u32[]{:S(2)}) copy-start(s32[64,2]{0,1:T(2,128)} %param.17) | copy-start | bytes 1540
  2.3 19.1 %copy-start = (bf16[2,256,512]{2,1,0:T(8,128)(2,1)S(1)}, bf16[2,256,512]{2,1,0:T(8,128)(2,1)}, u32[]{:S(2)}) copy-start(bf16[2,256,512]{2,1,0:T(8,128)(2,1)} %constant.35.clone.circles) | copy-start | bytes 1572868
  2.3 19.0 %all-to-all-start = ((f32[8,32,256]{2,1,0:T(8,128)}), f32[8,32,256]{2,1,0:T(8,128)S(1)}, u32[]{:S(2)}, u32[]{:S(2)}) async-start(f32[8,32,256]{2,1,0:T(8,128)} %deal_kernel.1), calls=%async_computation | async-start | bytes 524288 | tf_op jit(solution)/shard_map/all_to_all | solution.py:382
  12.6 0.8 copy-start.7
  12.6 8.7 %copy-start.11 = (f32[2,2,64,256]{3,2,1,0:T(8,128)S(1)}, f32[2,2,64,256]{3,2,1,0:T(8,128)}, u32[]{:S(2)}) copy-start(f32[2,2,64,256]{3,2,1,0:T(8,128)} %constant.34.clone.turn) | copy-start | bytes 786436
  21.3 34.5 %copy-start.9 = (bf16[2,256,256]{2,1,0:T(8,128)(2,1)S(1)}, bf16[2,256,256]{2,1,0:T(8,128)(2,1)}, u32[]{:S(2)}) copy-start(bf16[2,256,256]{2,1,0:T(8,128)(2,1)} %constant.38.clone.deal) | copy-start | bytes 786436
  21.3 34.4 %copy-start.10 = (f32[2,256,128]{2,1,0:T(8,128)S(1)}, f32[2,256,128]{2,1,0:T(8,128)}, u32[]{:S(2)}) copy-start(f32[2,256,128]{2,1,0:T(8,128)} %constant.36.clone.turn) | copy-start | bytes 786436
  22.8 33.0 %copy-start.8 = (bf16[2,256,640]{2,1,0:T(8,128)(2,1)S(1)}, bf16[2,256,640]{2,1,0:T(8,128)(2,1)}, u32[]{:S(2)}) copy-start(bf16[2,256,640]{2,1,0:T(8,128)(2,1)} %constant.37.clone.gather) | copy-start | bytes 1966084
  55.8 25.8 %copy-start.4 = (f32[2,2,32,256]{3,2,1,0:T(8,128)S(1)}, f32[2,2,32,256]{3,2,1,0:T(8,128)}, u32[]{:S(2)}) copy-start(f32[2,2,32,256]{3,2,1,0:T(8,128)} %constant.39.clone.main_turn) | copy-start | bytes 393220
  57.4 24.1 %copy-start.1 = (bf16[2,128,512]{2,1,0:T(8,128)(2,1)S(1)}, bf16[2,128,512]{2,1,0:T(8,128)(2,1)}, u32[]{:S(2)}) copy-start(bf16[2,128,512]{2,1,0:T(8,128)(2,1)} %constant.42.clone.zone_mix) | copy-start | bytes 786436
  57.4 24.1 %copy-start.2 = (bf16[2,256,256]{2,1,0:T(8,128)(2,1)S(1)}, bf16[2,256,256]{2,1,0:T(8,128)(2,1)}, u32[]{:S(2)}) copy-start(bf16[2,256,256]{2,1,0:T(8,128)(2,1)} %constant.41.clone.main_mix) | copy-start | bytes 786436
  57.4 24.1 %copy-start.3 = (f32[2,128,256]{2,1,0:T(8,128)S(1)}, f32[2,128,256]{2,1,0:T(8,128)}, u32[]{:S(2)}) copy-start(f32[2,128,256]{2,1,0:T(8,128)} %constant.40.clone.zone_turn) | copy-start | bytes 786436
  83.5 16.4 %copy-start.5 = (f32[2,32,256]{2,1,0:T(8,128)S(1)}, f32[2,32,256]{2,1,0:T(8,128)}, u32[]{:S(2)}) copy-start(f32[2,32,256]{2,1,0:T(8,128)} %eta.3) | copy-start | bytes 196612
  83.5 16.4 %copy-start.6 = (f32[2,32,256]{2,1,0:T(8,128)S(1)}, f32[2,32,256]{2,1,0:T(8,128)}, u32[]{:S(2)}) copy-start(f32[2,32,256]{2,1,0:T(8,128)} %phi.3) | copy-start | bytes 196612

commit v11 on v7

--- a/solution.py
+++ b/solution.py
@@ -146,7 +146,7 @@
             for a in range(2):
                 rows = source[a, 8 * z : 8 * z + 8, :]
                 for c in range(2):
-                    out[4 * c + z, base + 8 * a : base + 8 * a + 8, :] = rows
+                    out[2 * z + c, base + 8 * a : base + 8 * a + 8, :] = rows
 
 
 def source_kernel(place, offsets, zone, out, places, beyond):
@@ -199,9 +199,8 @@
     for n in range(8):
         wave_x = wave_of(256 * n + iota((16, 256), 1)) * TURN_X
         kappa = jnp.sqrt(wave_x * wave_x + wave_y * wave_y)
-        block = 4 * (n % 2) + n // 2
-        eta = modes[block, 0:16, :]
-        phi = modes[block, 16:32, :]
+        eta = modes[n, 0:16, :]
+        phi = modes[n, 16:32, :]
         if n % 2:
             eta = eta * odd
             phi = phi * odd
@@ -381,7 +380,7 @@
     def turn(words):
         return swap(words.reshape(256, 1, 384), ("wide", "lane")).reshape(768, 128)
 
-    modes = swap(stage_deal(eta_modes, phi_modes), ("core", "lane"))
+    modes = swap(stage_deal(eta_modes, phi_modes), ("lane", "core"))
     ready = stage_source(place, offsets, zone_field)
     modes, (source, places, beyond) = lax.optimization_barrier((modes, ready))
     columns = turn(stage_rows(place, modes))

time: 103 us -> 102 us (level)
  no operation moved by 1% of the time
where the time goes in v11:
time: 102 us; the launch traced here: 101 us
  blocking collectives  73.8 us (72%)
  starting transfers between devices  10.3 us (10%)
  Pallas kernels  9.46 us (9%)
  waiting for transfers between devices  6.32 us (6%)
    all_to_all x2, blocking collectives, turn(): return swap(words.reshape(256, 1, 384), ('wide', 'lane')).reshape(768, 128)  57.1 us
    all_to_all x1, blocking collectives, local(): terms = swap(stage_rows_back(place, rows, places, beyond), ('core', 'lane'))  16.7 us
    all_to_all x1, starting transfers between devices, local(): modes = swap(stage_deal(eta_modes, phi_modes), ('lane', 'core'))  10.3 us
    pallas_call x6, Pallas kernels, call(): pl.pallas_call(kernel, out_shape=[jax.ShapeDtypeStruct(s, t) for s, t in...  9.46 us
    all_to_all x1, waiting for transfers between devices, local(): modes = swap(stage_deal(eta_modes, phi_modes), ('lane', 'core'))  6.32 us
  transfers between devices with their start and end apart: 1, of which 1 were waited for; matrix products, arithmetic and copies ran while one was open for 0% of the time, Pallas kernels for 2%

profile of v11, /device:TPU:1, one launch (start us, length us, event | category | flops | bytes accessed | tf_op | source)
XLA Modules:
  0.0 101.5 jit_solution(5834592217022388772)
XLA Ops:
  0.6 0.0 copy-start.12
  0.6 1.6 %deal_kernel.1 = f32[8,32,256]{2,1,0:T(8,128)} custom-call(f32[2,32,256]{2,1,0:T(8,128)} %eta.3, f32[2,32,256]{2,1,0:T(8,128)} %phi.3), custom_call_target="tpu_custom_call" | custom-call | flops 8589934592 | bytes 393216 | tf_op jit(solution)/shard_map/deal_kernel/pallas_call | solution.py:331
  2.3 10.3 %all-to-all-start = ((f32[8,32,256]{2,1,0:T(8,128)}), f32[8,32,256]{2,1,0:T(8,128)S(1)}, u32[]{:S(2)}, u32[]{:S(2)}) async-start(f32[8,32,256]{2,1,0:T(8,128)} %deal_kernel.1), calls=%async_computation | async-start | bytes 524288 | tf_op jit(solution)/shard_map/all_to_all | solution.py:383
  12.6 0.1 copy.17.offsets
  12.7 0.1 pad_add_fusion.place
  12.8 0.6 copy-done.7
  13.3 1.6 %source_kernel.1 = (f32[256,256]{1,0:T(8,128)S(1)}, bf16[512,256]{1,0:T(8,128)(2,1)S(1)}, f32[128,256]{1,0:T(8,128)S(1)}) custom-call(s32[3]{0:T(128)S(1)} %pad_add_fusion.place, s32[64,2]{1,0:T(8,128)S(1)} %copy.17.offsets, f32[64,128]{1,0:T(8,128)S(1)} %copy-done.7), custom_call_target="tpu_custom_call" | custom-call | flops 67108864 | bytes 950272 | tf_op jit(solution)/shard_map/source_kernel/pallas_call | solution.py:331
  15.0 6.3 %all-to-all-done.modes = f32[8,32,256]{2,1,0:T(8,128)S(1)} async-done(((f32[8,32,256]{2,1,0:T(8,128)}), f32[8,32,256]{2,1,0:T(8,128)S(1)}, u32[]{:S(2)}, u32[]{:S(2)}) %all-to-all-start) | async-done | bytes 262176 | tf_op jit(solution)/shard_map/all_to_all | solution.py:383
  21.3 0.0 copy-start.9
  21.3 0.0 copy-start.10
  21.4 1.4 %rows_kernel.1 = f32[768,128]{1,0:T(8,128)S(1)} custom-call(s32[3]{0:T(128)S(1)} %pad_add_fusion.place, f32[8,32,256]{2,1,0:T(8,128)S(1)} %all-to-all-done.modes, bf16[2,256,128]{2,1,0:T(8,128)(2,1)S(1)} %copy-done.12, f32[2,2,64,256]{3,2,1,0:T(8,128)S(1)} %copy-done.11, bf16[2,256,512]{2,1,0:T(8,128)(2,1)S(1)} %copy-done), custom_call_target="tpu_custom_call" | custom-call | flops 1073741824 | bytes 1572864 | tf_op jit(solution)/shard_map/rows_kernel/pallas_call | solution.py:331
  22.8 0.0 copy-start.8
  22.8 33.0 %all_to_all.20 = f32[256,1,384]{2,1,0:T(1,128)S(1)} all-to-all(f32[256,1,384]{2,1,0:T(1,128)S(1)} %bitcast.10), channel_id=1, replica_groups=mesh['wide'=64,'lane'=4,'core'=2] {'wide','lane'}, dimensions={0} | all-to-all | bytes 786432 | tf_op jit(solution)/shard_map/all_to_all | solution.py:381
  55.8 0.0 copy-start.4
  55.8 1.6 %columns_kernel.1 = f32[768,128]{1,0:T(8,128)S(1)} custom-call(f32[768,128]{1,0:T(8,128)S(1)} %bitcast.8, f32[256,256]{1,0:T(8,128)S(1)} %get-tuple-element.13.source, bf16[2,256,512]{2,1,0:T(8,128)(2,1)S(1)} %copy-done, f32[2,256,128]{2,1,0:T(8,128)S(1)} %copy-done.10, bf16[2,256,640]{2,1,0:T(8,128)(2,1)S(1)} %copy-done.8, bf16[2,256,256]{2,1,0:T(8,128)(2,1)S(1)} %copy-done.9), custom_call_target="tpu_custom_call" | custom-call | flops 1073741824 | bytes 2752512 | tf_op jit(solution)/shard_map/columns_kernel/pallas_call | solution.py:331
  57.4 0.0 copy-start.1
  57.4 0.0 copy-start.2
  57.4 0.0 copy-start.3
  57.5 24.1 %all_to_all.21 = f32[256,1,384]{2,1,0:T(1,128)S(1)} all-to-all(f32[256,1,384]{2,1,0:T(1,128)S(1)} %bitcast.9), channel_id=1, replica_groups=mesh['wide'=64,'lane'=4,'core'=2] {'wide','lane'}, dimensions={0} | all-to-all | bytes 786432 | tf_op jit(solution)/shard_map/all_to_all | solution.py:381
  81.6 1.9 %rows_back_kernel.1 = f32[8,32,256]{2,1,0:T(8,128)S(1)} custom-call(s32[3]{0:T(128)S(1)} %pad_add_fusion.place, f32[768,128]{1,0:T(8,128)S(1)} %bitcast.7, bf16[512,256]{1,0:T(8,128)(2,1)S(1)} %get-tuple-element.14.places, f32[128,256]{1,0:T(8,128)S(1)} %get-tuple-element.15.beyond, bf16[2,256,512]{2,1,0:T(8,128)(2,1)S(1)} %copy-done, ...), custom_call_target="tpu_custom_call" | custom-call | flops 536870912 | bytes 2490368 | tf_op jit(solution)/shard_map/rows_back_kernel/pallas_call | solution.py:331
  83.5 0.0 copy-start.5
  83.5 0.0 copy-start.6
  83.5 16.7 %all_to_all.22.terms = f32[8,32,256]{2,1,0:T(8,128)S(1)} all-to-all(f32[8,32,256]{2,1,0:T(8,128)S(1)} %rows_back_kernel.1), channel_id=1, replica_groups=mesh['wide'=64,'lane'=4,'core'=2] {'core','lane'}, dimensions={0} | all-to-all | bytes 524288 | tf_op jit(solution)/shard_map/all_to_all | solution.py:388
  100.3 1.2 %finish_kernel.1 = (f32[2,32,256]{2,1,0:T(8,128)}, f32[2,32,256]{2,1,0:T(8,128)}) custom-call(s32[3]{0:T(128)S(1)} %pad_add_fusion.place, f32[8,32,256]{2,1,0:T(8,128)S(1)} %all_to_all.22.terms, f32[2,32,256]{2,1,0:T(8,128)S(1)} %copy-done.5, f32[2,32,256]{2,1,0:T(8,128)S(1)} %copy-done.6), custom_call_target="tpu_custom_call" | custom-call | bytes 524288 | tf_op jit(solution)/shard_map/finish_kernel/pallas_call | solution.py:331
  (17 shorter events, 0.0 us)
Async XLA Ops:
  0.6 20.7 %copy-start.12 = (bf16[2,256,128]{2,1,0:T(8,128)(2,1)S(1)}, bf16[2,256,128]{2,1,0:T(8,128)(2,1)}, u32[]{:S(2)}) copy-start(bf16[2,256,128]{2,1,0:T(8,128)(2,1)} %constant.33.clone.mix) | copy-start | bytes 393220
  2.3 10.3 %copy-start.13 = (s32[64,2]{0,1:T(2,128)S(1)}, s32[64,2]{0,1:T(2,128)}, u32[]{:S(2)}) copy-start(s32[64,2]{0,1:T(2,128)} %param.17) | copy-start | bytes 1540
  2.3 19.1 %copy-start = (bf16[2,256,512]{2,1,0:T(8,128)(2,1)S(1)}, bf16[2,256,512]{2,1,0:T(8,128)(2,1)}, u32[]{:S(2)}) copy-start(bf16[2,256,512]{2,1,0:T(8,128)(2,1)} %constant.35.clone.circles) | copy-start | bytes 1572868
  2.3 19.0 %all-to-all-start = ((f32[8,32,256]{2,1,0:T(8,128)}), f32[8,32,256]{2,1,0:T(8,128)S(1)}, u32[]{:S(2)}, u32[]{:S(2)}) async-start(f32[8,32,256]{2,1,0:T(8,128)} %deal_kernel.1), calls=%async_computation | async-start | bytes 524288 | tf_op jit(solution)/shard_map/all_to_all | solution.py:383
  12.6 0.8 copy-start.7
  12.6 8.7 %copy-start.11 = (f32[2,2,64,256]{3,2,1,0:T(8,128)S(1)}, f32[2,2,64,256]{3,2,1,0:T(8,128)}, u32[]{:S(2)}) copy-start(f32[2,2,64,256]{3,2,1,0:T(8,128)} %constant.34.clone.turn) | copy-start | bytes 786436
  21.3 34.5 %copy-start.9 = (bf16[2,256,256]{2,1,0:T(8,128)(2,1)S(1)}, bf16[2,256,256]{2,1,0:T(8,128)(2,1)}, u32[]{:S(2)}) copy-start(bf16[2,256,256]{2,1,0:T(8,128)(2,1)} %constant.38.clone.deal) | copy-start | bytes 786436
  21.3 34.4 %copy-start.10 = (f32[2,256,128]{2,1,0:T(8,128)S(1)}, f32[2,256,128]{2,1,0:T(8,128)}, u32[]{:S(2)}) copy-start(f32[2,256,128]{2,1,0:T(8,128)} %constant.36.clone.turn) | copy-start | bytes 786436
  22.8 33.0 %copy-start.8 = (bf16[2,256,640]{2,1,0:T(8,128)(2,1)S(1)}, bf16[2,256,640]{2,1,0:T(8,128)(2,1)}, u32[]{:S(2)}) copy-start(bf16[2,256,640]{2,1,0:T(8,128)(2,1)} %constant.37.clone.gather) | copy-start | bytes 1966084
  55.8 25.8 %copy-start.4 = (f32[2,2,32,256]{3,2,1,0:T(8,128)S(1)}, f32[2,2,32,256]{3,2,1,0:T(8,128)}, u32[]{:S(2)}) copy-start(f32[2,2,32,256]{3,2,1,0:T(8,128)} %constant.39.clone.main_turn) | copy-start | bytes 393220
  57.4 24.1 %copy-start.1 = (bf16[2,128,512]{2,1,0:T(8,128)(2,1)S(1)}, bf16[2,128,512]{2,1,0:T(8,128)(2,1)}, u32[]{:S(2)}) copy-start(bf16[2,128,512]{2,1,0:T(8,128)(2,1)} %constant.42.clone.zone_mix) | copy-start | bytes 786436
  57.4 24.1 %copy-start.2 = (bf16[2,256,256]{2,1,0:T(8,128)(2,1)S(1)}, bf16[2,256,256]{2,1,0:T(8,128)(2,1)}, u32[]{:S(2)}) copy-start(bf16[2,256,256]{2,1,0:T(8,128)(2,1)} %constant.41.clone.main_mix) | copy-start | bytes 786436
  57.4 24.1 %copy-start.3 = (f32[2,128,256]{2,1,0:T(8,128)S(1)}, f32[2,128,256]{2,1,0:T(8,128)}, u32[]{:S(2)}) copy-start(f32[2,128,256]{2,1,0:T(8,128)} %constant.40.clone.zone_turn) | copy-start | bytes 786436
  83.5 16.8 %copy-start.5 = (f32[2,32,256]{2,1,0:T(8,128)S(1)}, f32[2,32,256]{2,1,0:T(8,128)}, u32[]{:S(2)}) copy-start(f32[2,32,256]{2,1,0:T(8,128)} %eta.3) | copy-start | bytes 196612
  83.5 16.8 %copy-start.6 = (f32[2,32,256]{2,1,0:T(8,128)S(1)}, f32[2,32,256]{2,1,0:T(8,128)}, u32[]{:S(2)}) copy-start(f32[2,32,256]{2,1,0:T(8,128)} %phi.3) | copy-start | bytes 196612

commit v12 on v10

--- a/solution.py
+++ b/solution.py
@@ -303,21 +303,27 @@
         out[n, 16:32, :] = block[16:]
 
 
-def finish_kernel(place, terms, eta, phi, eta_next, phi_next):
-    for z in range(4):
-        rows = slice(8 * z, 8 * z + 8)
-        wave_x = wave_of(256 * (2 * place[1] + place[2]) + iota((8, 256), 1)) * TURN_X
-        wave_y = wave_of(32 * place[0] + 8 * z + iota((8, 256), 0)) * TURN_Y
-        kappa = time_step * jnp.sqrt(wave_x * wave_x + wave_y * wave_y)
-        for a in range(2):
-            surface = eta[a, rows, :]
-            potential = phi[a, rows, :]
-            part_of = slice(8 * a, 8 * a + 8)
-            added = terms[2 * z, part_of, :] + terms[2 * z + 1, part_of, :]
-            eta_next[a, rows, :] = surface + kappa * potential + added
-            part_of = slice(16 + 8 * a, 24 + 8 * a)
-            added = terms[2 * z, part_of, :] + terms[2 * z + 1, part_of, :]
-            phi_next[a, rows, :] = potential - (time_step * gravity) * surface + added
+def finish_kernel(place, terms, eta, phi, eta_next, phi_next, held, done):
+    copies = []
+    for k, out in enumerate((eta_next, phi_next)):
+        for z in range(4):
+            rows = slice(8 * z, 8 * z + 8)
+            wave_x = wave_of(256 * (2 * place[1] + place[2]) + iota((8, 256), 1)) * TURN_X
+            wave_y = wave_of(32 * place[0] + 8 * z + iota((8, 256), 0)) * TURN_Y
+            kappa = time_step * jnp.sqrt(wave_x * wave_x + wave_y * wave_y)
+            for a in range(2):
+                surface = eta[a, rows, :]
+                potential = phi[a, rows, :]
+                part_of = slice(16 * k + 8 * a, 16 * k + 8 * a + 8)
+                added = terms[2 * z, part_of, :] + terms[2 * z + 1, part_of, :]
+                if k == 0:
+                    held[k, a, rows, :] = surface + kappa * potential + added
+                else:
+                    held[k, a, rows, :] = potential - (time_step * gravity) * surface + added
+        copies.append(pltpu.make_async_copy(held.at[k], out, done.at[k]))
+        copies[-1].start()
+    for copy in copies:
+        copy.wait()
 
 
 def call(kernel, shapes, scalars, arrays, flops=0, limit=24, types=None):
@@ -369,7 +375,17 @@
 
 
 def stage_finish(place, terms, eta, phi):
-    return call(finish_kernel, [(2, 32, 256)] * 2, [place], [terms, eta, phi])
+    vmem = pl.BlockSpec(memory_space=pltpu.VMEM)
+    return pl.pallas_call(
+        finish_kernel,
+        out_shape=[jax.ShapeDtypeStruct((2, 32, 256), f32)] * 2,
+        in_specs=[pl.BlockSpec(memory_space=pltpu.SMEM), vmem, vmem, vmem],
+        out_specs=[pl.BlockSpec(memory_space=pl.ANY)] * 2,
+        scratch_shapes=[pltpu.VMEM((2, 2, 32, 256), f32), pltpu.SemaphoreType.DMA((2,))],
+        compiler_params=pltpu.CompilerParams(vmem_limit_bytes=24 * 1024 * 1024),
+        cost_estimate=pl.CostEstimate(flops=2**19, bytes_accessed=2**20, transcendentals=0),
+        name="finish_kernel",
+    )(place, terms, eta, phi)
 
 
 def local(eta_modes, phi_modes, zone_field, offsets):

time: 102 us -> 102 us (level)
    pallas_call x0 -> x1, Pallas kernels: none -> 1.24 us  [stage_finish(): pl.pallas_call(finish_kernel, out_shape=[jax.ShapeDtypeStruct((2, 32, 256...]
    pallas_call x6 -> x5, Pallas kernels: 9.46 us -> 8.23 us  [call(): pl.pallas_call(kernel, out_shape=[jax.ShapeDtypeStruct(s, t) for s, t in...]
where the time goes in v12:
time: 102 us; the launch traced here: 101 us
  blocking collectives  73.5 us (72%)
  starting transfers between devices  10.3 us (10%)
  Pallas kernels  9.48 us (9%)
  waiting for transfers between devices  6.32 us (6%)
    all_to_all x2, blocking collectives, turn(): return swap(words.reshape(256, 1, 384), ('wide', 'lane')).reshape(768, 128)  57.1 us
    all_to_all x1, blocking collectives, local(): terms = swap(stage_rows_back(place, rows, places, beyond), ('lane', 'core'))  16.4 us
    all_to_all x1, starting transfers between devices, local(): modes = swap(stage_deal(eta_modes, phi_modes), ('lane', 'core'))  10.3 us
    pallas_call x5, Pallas kernels, call(): pl.pallas_call(kernel, out_shape=[jax.ShapeDtypeStruct(s, t) for s, t in...  8.23 us
    all_to_all x1, waiting for transfers between devices, local(): modes = swap(stage_deal(eta_modes, phi_modes), ('lane', 'core'))  6.32 us
  transfers between devices with their start and end apart: 1, of which 1 were waited for; matrix products, arithmetic and copies ran while one was open for 0% of the time, Pallas kernels for 2%

profile of v12, /device:TPU:1, one launch (start us, length us, event | category | flops | bytes accessed | tf_op | source)
XLA Modules:
  0.0 101.2 jit_solution(12409250033382834562)
XLA Ops:
  0.6 0.0 copy-start.12
  0.6 1.6 %deal_kernel.1 = f32[8,32,256]{2,1,0:T(8,128)} custom-call(f32[2,32,256]{2,1,0:T(8,128)} %eta.3, f32[2,32,256]{2,1,0:T(8,128)} %phi.3), custom_call_target="tpu_custom_call" | custom-call | flops 8589934592 | bytes 393216 | tf_op jit(solution)/shard_map/deal_kernel/pallas_call | solution.py:336
  2.3 10.3 %all-to-all-start = ((f32[8,32,256]{2,1,0:T(8,128)}), f32[8,32,256]{2,1,0:T(8,128)S(1)}, u32[]{:S(2)}, u32[]{:S(2)}) async-start(f32[8,32,256]{2,1,0:T(8,128)} %deal_kernel.1), calls=%async_computation | async-start | bytes 524288 | tf_op jit(solution)/shard_map/all_to_all | solution.py:398
  12.6 0.1 copy.17.offsets
  12.7 0.1 pad_add_fusion.place
  12.8 0.6 copy-done.7
  13.3 1.6 %source_kernel.1 = (f32[256,256]{1,0:T(8,128)S(1)}, bf16[512,256]{1,0:T(8,128)(2,1)S(1)}, f32[128,256]{1,0:T(8,128)S(1)}) custom-call(s32[3]{0:T(128)S(1)} %pad_add_fusion.place, s32[64,2]{1,0:T(8,128)S(1)} %copy.17.offsets, f32[64,128]{1,0:T(8,128)S(1)} %copy-done.7), custom_call_target="tpu_custom_call" | custom-call | flops 67108864 | bytes 950272 | tf_op jit(solution)/shard_map/source_kernel/pallas_call | solution.py:336
  15.0 6.3 %all-to-all-done.modes = f32[8,32,256]{2,1,0:T(8,128)S(1)} async-done(((f32[8,32,256]{2,1,0:T(8,128)}), f32[8,32,256]{2,1,0:T(8,128)S(1)}, u32[]{:S(2)}, u32[]{:S(2)}) %all-to-all-start) | async-done | bytes 262176 | tf_op jit(solution)/shard_map/all_to_all | solution.py:398
  21.3 0.0 copy-start.9
  21.3 0.0 copy-start.10
  21.4 1.4 %rows_kernel.1 = f32[768,128]{1,0:T(8,128)S(1)} custom-call(s32[3]{0:T(128)S(1)} %pad_add_fusion.place, f32[8,32,256]{2,1,0:T(8,128)S(1)} %all-to-all-done.modes, bf16[2,256,128]{2,1,0:T(8,128)(2,1)S(1)} %copy-done.12, f32[2,2,64,256]{3,2,1,0:T(8,128)S(1)} %copy-done.11, bf16[2,256,512]{2,1,0:T(8,128)(2,1)S(1)} %copy-done), custom_call_target="tpu_custom_call" | custom-call | flops 1073741824 | bytes 1572864 | tf_op jit(solution)/shard_map/rows_kernel/pallas_call | solution.py:336
  22.8 0.0 copy-start.8
  22.8 33.0 %all_to_all.20 = f32[256,1,384]{2,1,0:T(1,128)S(1)} all-to-all(f32[256,1,384]{2,1,0:T(1,128)S(1)} %bitcast.10), channel_id=1, replica_groups=mesh['wide'=64,'lane'=4,'core'=2] {'wide','lane'}, dimensions={0} | all-to-all | bytes 786432 | tf_op jit(solution)/shard_map/all_to_all | solution.py:396
  55.8 0.0 copy-start.4
  55.8 1.6 %columns_kernel.1 = f32[768,128]{1,0:T(8,128)S(1)} custom-call(f32[768,128]{1,0:T(8,128)S(1)} %bitcast.8, f32[256,256]{1,0:T(8,128)S(1)} %get-tuple-element.13.source, bf16[2,256,512]{2,1,0:T(8,128)(2,1)S(1)} %copy-done, f32[2,256,128]{2,1,0:T(8,128)S(1)} %copy-done.10, bf16[2,256,640]{2,1,0:T(8,128)(2,1)S(1)} %copy-done.8, bf16[2,256,256]{2,1,0:T(8,128)(2,1)S(1)} %copy-done.9), custom_call_target="tpu_custom_call" | custom-call | flops 1073741824 | bytes 2752512 | tf_op jit(solution)/shard_map/columns_kernel/pallas_call | solution.py:336
  57.4 0.0 copy-start.1
  57.4 0.0 copy-start.2
  57.4 0.0 copy-start.3
  57.5 24.1 %all_to_all.21 = f32[256,1,384]{2,1,0:T(1,128)S(1)} all-to-all(f32[256,1,384]{2,1,0:T(1,128)S(1)} %bitcast.9), channel_id=1, replica_groups=mesh['wide'=64,'lane'=4,'core'=2] {'wide','lane'}, dimensions={0} | all-to-all | bytes 786432 | tf_op jit(solution)/shard_map/all_to_all | solution.py:396
  81.6 1.9 %rows_back_kernel.1 = f32[8,32,256]{2,1,0:T(8,128)S(1)} custom-call(s32[3]{0:T(128)S(1)} %pad_add_fusion.place, f32[768,128]{1,0:T(8,128)S(1)} %bitcast.7, bf16[512,256]{1,0:T(8,128)(2,1)S(1)} %get-tuple-element.14.places, f32[128,256]{1,0:T(8,128)S(1)} %get-tuple-element.15.beyond, bf16[2,256,512]{2,1,0:T(8,128)(2,1)S(1)} %copy-done, ...), custom_call_target="tpu_custom_call" | custom-call | flops 536870912 | bytes 2490368 | tf_op jit(solution)/shard_map/rows_back_kernel/pallas_call | solution.py:336
  83.5 0.0 copy-start.5
  83.5 0.0 copy-start.6
  83.5 16.4 %all_to_all.22.terms = f32[8,32,256]{2,1,0:T(8,128)S(1)} all-to-all(f32[8,32,256]{2,1,0:T(8,128)S(1)} %rows_back_kernel.1), channel_id=1, replica_groups=mesh['wide'=64,'lane'=4,'core'=2] {'lane','core'}, dimensions={0} | all-to-all | bytes 524288 | tf_op jit(solution)/shard_map/all_to_all | solution.py:403
  99.9 1.2 %finish_kernel.1 = (f32[2,32,256]{2,1,0:T(8,128)}, f32[2,32,256]{2,1,0:T(8,128)}) custom-call(s32[3]{0:T(128)S(1)} %pad_add_fusion.place, f32[8,32,256]{2,1,0:T(8,128)S(1)} %all_to_all.22.terms, f32[2,32,256]{2,1,0:T(8,128)S(1)} %copy-done.5, f32[2,32,256]{2,1,0:T(8,128)S(1)} %copy-done.6), custom_call_target="tpu_custom_call" | custom-call | flops 524288 | bytes 1048576 | tf_op jit(solution)/shard_map/finish_kernel/pallas_call | solution.py:379
  (17 shorter events, 0.0 us)
Async XLA Ops:
  0.6 20.7 %copy-start.12 = (bf16[2,256,128]{2,1,0:T(8,128)(2,1)S(1)}, bf16[2,256,128]{2,1,0:T(8,128)(2,1)}, u32[]{:S(2)}) copy-start(bf16[2,256,128]{2,1,0:T(8,128)(2,1)} %constant.33.clone.mix) | copy-start | bytes 393220
  2.3 10.3 %copy-start.13 = (s32[64,2]{0,1:T(2,128)S(1)}, s32[64,2]{0,1:T(2,128)}, u32[]{:S(2)}) copy-start(s32[64,2]{0,1:T(2,128)} %param.17) | copy-start | bytes 1540
  2.3 19.1 %copy-start = (bf16[2,256,512]{2,1,0:T(8,128)(2,1)S(1)}, bf16[2,256,512]{2,1,0:T(8,128)(2,1)}, u32[]{:S(2)}) copy-start(bf16[2,256,512]{2,1,0:T(8,128)(2,1)} %constant.35.clone.circles) | copy-start | bytes 1572868
  2.3 19.0 %all-to-all-start = ((f32[8,32,256]{2,1,0:T(8,128)}), f32[8,32,256]{2,1,0:T(8,128)S(1)}, u32[]{:S(2)}, u32[]{:S(2)}) async-start(f32[8,32,256]{2,1,0:T(8,128)} %deal_kernel.1), calls=%async_computation | async-start | bytes 524288 | tf_op jit(solution)/shard_map/all_to_all | solution.py:398
  12.6 0.8 copy-start.7
  12.6 8.7 %copy-start.11 = (f32[2,2,64,256]{3,2,1,0:T(8,128)S(1)}, f32[2,2,64,256]{3,2,1,0:T(8,128)}, u32[]{:S(2)}) copy-start(f32[2,2,64,256]{3,2,1,0:T(8,128)} %constant.34.clone.turn) | copy-start | bytes 786436
  21.3 34.5 %copy-start.9 = (bf16[2,256,256]{2,1,0:T(8,128)(2,1)S(1)}, bf16[2,256,256]{2,1,0:T(8,128)(2,1)}, u32[]{:S(2)}) copy-start(bf16[2,256,256]{2,1,0:T(8,128)(2,1)} %constant.38.clone.deal) | copy-start | bytes 786436
  21.3 34.4 %copy-start.10 = (f32[2,256,128]{2,1,0:T(8,128)S(1)}, f32[2,256,128]{2,1,0:T(8,128)}, u32[]{:S(2)}) copy-start(f32[2,256,128]{2,1,0:T(8,128)} %constant.36.clone.turn) | copy-start | bytes 786436
  22.8 33.0 %copy-start.8 = (bf16[2,256,640]{2,1,0:T(8,128)(2,1)S(1)}, bf16[2,256,640]{2,1,0:T(8,128)(2,1)}, u32[]{:S(2)}) copy-start(bf16[2,256,640]{2,1,0:T(8,128)(2,1)} %constant.37.clone.gather) | copy-start | bytes 1966084
  55.8 25.8 %copy-start.4 = (f32[2,2,32,256]{3,2,1,0:T(8,128)S(1)}, f32[2,2,32,256]{3,2,1,0:T(8,128)}, u32[]{:S(2)}) copy-start(f32[2,2,32,256]{3,2,1,0:T(8,128)} %constant.39.clone.main_turn) | copy-start | bytes 393220
  57.4 24.1 %copy-start.1 = (bf16[2,128,512]{2,1,0:T(8,128)(2,1)S(1)}, bf16[2,128,512]{2,1,0:T(8,128)(2,1)}, u32[]{:S(2)}) copy-start(bf16[2,128,512]{2,1,0:T(8,128)(2,1)} %constant.42.clone.zone_mix) | copy-start | bytes 786436
  57.4 24.1 %copy-start.2 = (bf16[2,256,256]{2,1,0:T(8,128)(2,1)S(1)}, bf16[2,256,256]{2,1,0:T(8,128)(2,1)}, u32[]{:S(2)}) copy-start(bf16[2,256,256]{2,1,0:T(8,128)(2,1)} %constant.41.clone.main_mix) | copy-start | bytes 786436
  57.4 24.1 %copy-start.3 = (f32[2,128,256]{2,1,0:T(8,128)S(1)}, f32[2,128,256]{2,1,0:T(8,128)}, u32[]{:S(2)}) copy-start(f32[2,128,256]{2,1,0:T(8,128)} %constant.40.clone.zone_turn) | copy-start | bytes 786436
  83.5 16.4 %copy-start.5 = (f32[2,32,256]{2,1,0:T(8,128)S(1)}, f32[2,32,256]{2,1,0:T(8,128)}, u32[]{:S(2)}) copy-start(f32[2,32,256]{2,1,0:T(8,128)} %eta.3) | copy-start | bytes 196612
  83.5 16.4 %copy-start.6 = (f32[2,32,256]{2,1,0:T(8,128)S(1)}, f32[2,32,256]{2,1,0:T(8,128)}, u32[]{:S(2)}) copy-start(f32[2,32,256]{2,1,0:T(8,128)} %phi.3) | copy-start | bytes 196612

commit v13 on v10

--- a/solution.py
+++ b/solution.py
@@ -210,10 +210,11 @@
     cosine = turn[0, core]
     sine = turn[1, core]
     parts = [[], []]
+    fields = [jnp.concatenate(tile, 0) for tile in tiles]
+    slopes = dot3((mix[0, :128], mix[1, :128]), split(jnp.concatenate(fields[:4], 1)))
+    lift = dot3((mix[0, 128:], mix[1, 128:]), split(fields[4]))
     for f in range(5):
-        rows = split(jnp.concatenate(tiles[f], 0))
-        kind = slice(0, 128) if f < 4 else slice(128, 256)
-        both = dot3((mix[0, kind], mix[1, kind]), rows)
+        both = slopes[:, 256 * f : 256 * f + 256] if f < 4 else lift
         first = both[:64]
         second = both[64:]
         turned = (first * cosine + second * sine).reshape(4, 2, 8, 256)

time: 102 us -> 102 us (level)
  no operation moved by 1% of the time
where the time goes in v13:
time: 102 us; the launch traced here: 101 us
  blocking collectives  73.5 us (72%)
  starting transfers between devices  10.3 us (10%)
  Pallas kernels  9.46 us (9%)
  waiting for transfers between devices  6.32 us (6%)
    all_to_all x2, blocking collectives, turn(): return swap(words.reshape(256, 1, 384), ('wide', 'lane')).reshape(768, 128)  57.1 us
    all_to_all x1, blocking collectives, local(): terms = swap(stage_rows_back(place, rows, places, beyond), ('lane', 'core'))  16.4 us
    all_to_all x1, starting transfers between devices, local(): modes = swap(stage_deal(eta_modes, phi_modes), ('lane', 'core'))  10.3 us
    pallas_call x6, Pallas kernels, call(): pl.pallas_call(kernel, out_shape=[jax.ShapeDtypeStruct(s, t) for s, t in...  9.46 us
    all_to_all x1, waiting for transfers between devices, local(): modes = swap(stage_deal(eta_modes, phi_modes), ('lane', 'core'))  6.32 us
  transfers between devices with their start and end apart: 1, of which 1 were waited for; matrix products, arithmetic and copies ran while one was open for 0% of the time, Pallas kernels for 2%

profile of v13, /device:TPU:1, one launch (start us, length us, event | category | flops | bytes accessed | tf_op | source)
XLA Modules:
  0.0 101.1 jit_solution(1837529061243478530)
XLA Ops:
  0.6 0.0 copy-start.12
  0.6 1.6 %deal_kernel.1 = f32[8,32,256]{2,1,0:T(8,128)} custom-call(f32[2,32,256]{2,1,0:T(8,128)} %eta.3, f32[2,32,256]{2,1,0:T(8,128)} %phi.3), custom_call_target="tpu_custom_call" | custom-call | flops 8589934592 | bytes 393216 | tf_op jit(solution)/shard_map/deal_kernel/pallas_call | solution.py:331
  2.3 10.3 %all-to-all-start = ((f32[8,32,256]{2,1,0:T(8,128)}), f32[8,32,256]{2,1,0:T(8,128)S(1)}, u32[]{:S(2)}, u32[]{:S(2)}) async-start(f32[8,32,256]{2,1,0:T(8,128)} %deal_kernel.1), calls=%async_computation | async-start | bytes 524288 | tf_op jit(solution)/shard_map/all_to_all | solution.py:383
  12.6 0.1 copy.17.offsets
  12.7 0.1 pad_add_fusion.place
  12.8 0.6 copy-done.7
  13.3 1.6 %source_kernel.1 = (f32[256,256]{1,0:T(8,128)S(1)}, bf16[512,256]{1,0:T(8,128)(2,1)S(1)}, f32[128,256]{1,0:T(8,128)S(1)}) custom-call(s32[3]{0:T(128)S(1)} %pad_add_fusion.place, s32[64,2]{1,0:T(8,128)S(1)} %copy.17.offsets, f32[64,128]{1,0:T(8,128)S(1)} %copy-done.7), custom_call_target="tpu_custom_call" | custom-call | flops 67108864 | bytes 950272 | tf_op jit(solution)/shard_map/source_kernel/pallas_call | solution.py:331
  15.0 6.3 %all-to-all-done.modes = f32[8,32,256]{2,1,0:T(8,128)S(1)} async-done(((f32[8,32,256]{2,1,0:T(8,128)}), f32[8,32,256]{2,1,0:T(8,128)S(1)}, u32[]{:S(2)}, u32[]{:S(2)}) %all-to-all-start) | async-done | bytes 262176 | tf_op jit(solution)/shard_map/all_to_all | solution.py:383
  21.3 0.0 copy-start.9
  21.3 0.0 copy-start.10
  21.4 1.4 %rows_kernel.1 = f32[768,128]{1,0:T(8,128)S(1)} custom-call(s32[3]{0:T(128)S(1)} %pad_add_fusion.place, f32[8,32,256]{2,1,0:T(8,128)S(1)} %all-to-all-done.modes, bf16[2,256,128]{2,1,0:T(8,128)(2,1)S(1)} %copy-done.12, f32[2,2,64,256]{3,2,1,0:T(8,128)S(1)} %copy-done.11, bf16[2,256,512]{2,1,0:T(8,128)(2,1)S(1)} %copy-done), custom_call_target="tpu_custom_call" | custom-call | flops 1073741824 | bytes 1572864 | tf_op jit(solution)/shard_map/rows_kernel/pallas_call | solution.py:331
  22.8 0.0 copy-start.8
  22.8 33.0 %all_to_all.20 = f32[256,1,384]{2,1,0:T(1,128)S(1)} all-to-all(f32[256,1,384]{2,1,0:T(1,128)S(1)} %bitcast.10), channel_id=1, replica_groups=mesh['wide'=64,'lane'=4,'core'=2] {'wide','lane'}, dimensions={0} | all-to-all | bytes 786432 | tf_op jit(solution)/shard_map/all_to_all | solution.py:381
  55.8 0.0 copy-start.4
  55.8 1.6 %columns_kernel.1 = f32[768,128]{1,0:T(8,128)S(1)} custom-call(f32[768,128]{1,0:T(8,128)S(1)} %bitcast.8, f32[256,256]{1,0:T(8,128)S(1)} %get-tuple-element.13.source, bf16[2,256,512]{2,1,0:T(8,128)(2,1)S(1)} %copy-done, f32[2,256,128]{2,1,0:T(8,128)S(1)} %copy-done.10, bf16[2,256,640]{2,1,0:T(8,128)(2,1)S(1)} %copy-done.8, bf16[2,256,256]{2,1,0:T(8,128)(2,1)S(1)} %copy-done.9), custom_call_target="tpu_custom_call" | custom-call | flops 1073741824 | bytes 2752512 | tf_op jit(solution)/shard_map/columns_kernel/pallas_call | solution.py:331
  57.4 0.0 copy-start.1
  57.4 0.0 copy-start.2
  57.4 0.0 copy-start.3
  57.5 24.1 %all_to_all.21 = f32[256,1,384]{2,1,0:T(1,128)S(1)} all-to-all(f32[256,1,384]{2,1,0:T(1,128)S(1)} %bitcast.9), channel_id=1, replica_groups=mesh['wide'=64,'lane'=4,'core'=2] {'wide','lane'}, dimensions={0} | all-to-all | bytes 786432 | tf_op jit(solution)/shard_map/all_to_all | solution.py:381
  81.6 1.9 %rows_back_kernel.1 = f32[8,32,256]{2,1,0:T(8,128)S(1)} custom-call(s32[3]{0:T(128)S(1)} %pad_add_fusion.place, f32[768,128]{1,0:T(8,128)S(1)} %bitcast.7, bf16[512,256]{1,0:T(8,128)(2,1)S(1)} %get-tuple-element.14.places, f32[128,256]{1,0:T(8,128)S(1)} %get-tuple-element.15.beyond, bf16[2,256,512]{2,1,0:T(8,128)(2,1)S(1)} %copy-done, ...), custom_call_target="tpu_custom_call" | custom-call | flops 536870912 | bytes 2490368 | tf_op jit(solution)/shard_map/rows_back_kernel/pallas_call | solution.py:331
  83.5 0.0 copy-start.5
  83.5 0.0 copy-start.6
  83.5 16.4 %all_to_all.22.terms = f32[8,32,256]{2,1,0:T(8,128)S(1)} all-to-all(f32[8,32,256]{2,1,0:T(8,128)S(1)} %rows_back_kernel.1), channel_id=1, replica_groups=mesh['wide'=64,'lane'=4,'core'=2] {'lane','core'}, dimensions={0} | all-to-all | bytes 524288 | tf_op jit(solution)/shard_map/all_to_all | solution.py:388
  99.9 1.2 %finish_kernel.1 = (f32[2,32,256]{2,1,0:T(8,128)}, f32[2,32,256]{2,1,0:T(8,128)}) custom-call(s32[3]{0:T(128)S(1)} %pad_add_fusion.place, f32[8,32,256]{2,1,0:T(8,128)S(1)} %all_to_all.22.terms, f32[2,32,256]{2,1,0:T(8,128)S(1)} %copy-done.5, f32[2,32,256]{2,1,0:T(8,128)S(1)} %copy-done.6), custom_call_target="tpu_custom_call" | custom-call | bytes 524288 | tf_op jit(solution)/shard_map/finish_kernel/pallas_call | solution.py:331
  (17 shorter events, 0.0 us)
Async XLA Ops:
  0.6 20.7 %copy-start.12 = (bf16[2,256,128]{2,1,0:T(8,128)(2,1)S(1)}, bf16[2,256,128]{2,1,0:T(8,128)(2,1)}, u32[]{:S(2)}) copy-start(bf16[2,256,128]{2,1,0:T(8,128)(2,1)} %constant.33.clone.mix) | copy-start | bytes 393220
  2.3 10.3 %copy-start.13 = (s32[64,2]{0,1:T(2,128)S(1)}, s32[64,2]{0,1:T(2,128)}, u32[]{:S(2)}) copy-start(s32[64,2]{0,1:T(2,128)} %param.17) | copy-start | bytes 1540
  2.3 19.1 %copy-start = (bf16[2,256,512]{2,1,0:T(8,128)(2,1)S(1)}, bf16[2,256,512]{2,1,0:T(8,128)(2,1)}, u32[]{:S(2)}) copy-start(bf16[2,256,512]{2,1,0:T(8,128)(2,1)} %constant.35.clone.circles) | copy-start | bytes 1572868
  2.3 19.0 %all-to-all-start = ((f32[8,32,256]{2,1,0:T(8,128)}), f32[8,32,256]{2,1,0:T(8,128)S(1)}, u32[]{:S(2)}, u32[]{:S(2)}) async-start(f32[8,32,256]{2,1,0:T(8,128)} %deal_kernel.1), calls=%async_computation | async-start | bytes 524288 | tf_op jit(solution)/shard_map/all_to_all | solution.py:383
  12.6 0.8 copy-start.7
  12.6 8.7 %copy-start.11 = (f32[2,2,64,256]{3,2,1,0:T(8,128)S(1)}, f32[2,2,64,256]{3,2,1,0:T(8,128)}, u32[]{:S(2)}) copy-start(f32[2,2,64,256]{3,2,1,0:T(8,128)} %constant.34.clone.turn) | copy-start | bytes 786436
  21.3 34.5 %copy-start.9 = (bf16[2,256,256]{2,1,0:T(8,128)(2,1)S(1)}, bf16[2,256,256]{2,1,0:T(8,128)(2,1)}, u32[]{:S(2)}) copy-start(bf16[2,256,256]{2,1,0:T(8,128)(2,1)} %constant.38.clone.deal) | copy-start | bytes 786436
  21.3 34.4 %copy-start.10 = (f32[2,256,128]{2,1,0:T(8,128)S(1)}, f32[2,256,128]{2,1,0:T(8,128)}, u32[]{:S(2)}) copy-start(f32[2,256,128]{2,1,0:T(8,128)} %constant.36.clone.turn) | copy-start | bytes 786436
  22.8 33.0 %copy-start.8 = (bf16[2,256,640]{2,1,0:T(8,128)(2,1)S(1)}, bf16[2,256,640]{2,1,0:T(8,128)(2,1)}, u32[]{:S(2)}) copy-start(bf16[2,256,640]{2,1,0:T(8,128)(2,1)} %constant.37.clone.gather) | copy-start | bytes 1966084
  55.8 25.8 %copy-start.4 = (f32[2,2,32,256]{3,2,1,0:T(8,128)S(1)}, f32[2,2,32,256]{3,2,1,0:T(8,128)}, u32[]{:S(2)}) copy-start(f32[2,2,32,256]{3,2,1,0:T(8,128)} %constant.39.clone.main_turn) | copy-start | bytes 393220
  57.4 24.1 %copy-start.1 = (bf16[2,128,512]{2,1,0:T(8,128)(2,1)S(1)}, bf16[2,128,512]{2,1,0:T(8,128)(2,1)}, u32[]{:S(2)}) copy-start(bf16[2,128,512]{2,1,0:T(8,128)(2,1)} %constant.42.clone.zone_mix) | copy-start | bytes 786436
  57.4 24.1 %copy-start.2 = (bf16[2,256,256]{2,1,0:T(8,128)(2,1)S(1)}, bf16[2,256,256]{2,1,0:T(8,128)(2,1)}, u32[]{:S(2)}) copy-start(bf16[2,256,256]{2,1,0:T(8,128)(2,1)} %constant.41.clone.main_mix) | copy-start | bytes 786436
  57.4 24.1 %copy-start.3 = (f32[2,128,256]{2,1,0:T(8,128)S(1)}, f32[2,128,256]{2,1,0:T(8,128)}, u32[]{:S(2)}) copy-start(f32[2,128,256]{2,1,0:T(8,128)} %constant.40.clone.zone_turn) | copy-start | bytes 786436
  83.5 16.4 %copy-start.5 = (f32[2,32,256]{2,1,0:T(8,128)S(1)}, f32[2,32,256]{2,1,0:T(8,128)}, u32[]{:S(2)}) copy-start(f32[2,32,256]{2,1,0:T(8,128)} %eta.3) | copy-start | bytes 196612
  83.5 16.4 %copy-start.6 = (f32[2,32,256]{2,1,0:T(8,128)S(1)}, f32[2,32,256]{2,1,0:T(8,128)}, u32[]{:S(2)}) copy-start(f32[2,32,256]{2,1,0:T(8,128)} %phi.3) | copy-start | bytes 196612

commit v14 on v13

--- a/solution.py
+++ b/solution.py
@@ -236,8 +236,10 @@
     words = split(
         jnp.concatenate([terms[pl.ds(q, 256, stride=3), :] for q in range(3)], 1)
     )
-    with_cos = dot3((circles[0, :, :256], circles[1, :, :256]), words)
-    with_sin = dot3((circles[0, :, 256:], circles[1, :, 256:]), words)
+    stacked = [jnp.concatenate([circles[k, :, :256], circles[k, :, 256:]], 0) for k in range(2)]
+    both = dot3(stacked, words)
+    with_cos = both[:256]
+    with_sin = both[256:]
     real = with_cos[:, :128] - with_sin[:, 128:256]
     imag = with_sin[:, :128] + with_cos[:, 128:256]
     lane = iota((256, 128), 1)

time: 102 us -> 102 us (level)
  no operation moved by 1% of the time
where the time goes in v14:
time: 102 us; the launch traced here: 101 us
  blocking collectives  73.5 us (72%)
  starting transfers between devices  10.3 us (10%)
  Pallas kernels  9.45 us (9%)
  waiting for transfers between devices  6.32 us (6%)
    all_to_all x2, blocking collectives, turn(): return swap(words.reshape(256, 1, 384), ('wide', 'lane')).reshape(768, 128)  57 us
    all_to_all x1, blocking collectives, local(): terms = swap(stage_rows_back(place, rows, places, beyond), ('lane', 'core'))  16.4 us
    all_to_all x1, starting transfers between devices, local(): modes = swap(stage_deal(eta_modes, phi_modes), ('lane', 'core'))  10.3 us
    pallas_call x6, Pallas kernels, call(): pl.pallas_call(kernel, out_shape=[jax.ShapeDtypeStruct(s, t) for s, t in...  9.45 us
    all_to_all x1, waiting for transfers between devices, local(): modes = swap(stage_deal(eta_modes, phi_modes), ('lane', 'core'))  6.32 us
  transfers between devices with their start and end apart: 1, of which 1 were waited for; matrix products, arithmetic and copies ran while one was open for 0% of the time, Pallas kernels for 2%

profile of v14, /device:TPU:1, one launch (start us, length us, event | category | flops | bytes accessed | tf_op | source)
XLA Modules:
  0.0 101.1 jit_solution(10099452237320689043)
XLA Ops:
  0.6 0.0 copy-start.12
  0.6 1.6 %deal_kernel.1 = f32[8,32,256]{2,1,0:T(8,128)} custom-call(f32[2,32,256]{2,1,0:T(8,128)} %eta.3, f32[2,32,256]{2,1,0:T(8,128)} %phi.3), custom_call_target="tpu_custom_call" | custom-call | flops 8589934592 | bytes 393216 | tf_op jit(solution)/shard_map/deal_kernel/pallas_call | solution.py:333
  2.3 10.3 %all-to-all-start = ((f32[8,32,256]{2,1,0:T(8,128)}), f32[8,32,256]{2,1,0:T(8,128)S(1)}, u32[]{:S(2)}, u32[]{:S(2)}) async-start(f32[8,32,256]{2,1,0:T(8,128)} %deal_kernel.1), calls=%async_computation | async-start | bytes 524288 | tf_op jit(solution)/shard_map/all_to_all | solution.py:385
  12.6 0.1 copy.17.offsets
  12.7 0.1 pad_add_fusion.place
  12.8 0.6 copy-done.7
  13.3 1.6 %source_kernel.1 = (f32[256,256]{1,0:T(8,128)S(1)}, bf16[512,256]{1,0:T(8,128)(2,1)S(1)}, f32[128,256]{1,0:T(8,128)S(1)}) custom-call(s32[3]{0:T(128)S(1)} %pad_add_fusion.place, s32[64,2]{1,0:T(8,128)S(1)} %copy.17.offsets, f32[64,128]{1,0:T(8,128)S(1)} %copy-done.7), custom_call_target="tpu_custom_call" | custom-call | flops 67108864 | bytes 950272 | tf_op jit(solution)/shard_map/source_kernel/pallas_call | solution.py:333
  15.0 6.3 %all-to-all-done.modes = f32[8,32,256]{2,1,0:T(8,128)S(1)} async-done(((f32[8,32,256]{2,1,0:T(8,128)}), f32[8,32,256]{2,1,0:T(8,128)S(1)}, u32[]{:S(2)}, u32[]{:S(2)}) %all-to-all-start) | async-done | bytes 262176 | tf_op jit(solution)/shard_map/all_to_all | solution.py:385
  21.3 0.0 copy-start.9
  21.3 0.0 copy-start.10
  21.4 1.4 %rows_kernel.1 = f32[768,128]{1,0:T(8,128)S(1)} custom-call(s32[3]{0:T(128)S(1)} %pad_add_fusion.place, f32[8,32,256]{2,1,0:T(8,128)S(1)} %all-to-all-done.modes, bf16[2,256,128]{2,1,0:T(8,128)(2,1)S(1)} %copy-done.12, f32[2,2,64,256]{3,2,1,0:T(8,128)S(1)} %copy-done.11, bf16[2,256,512]{2,1,0:T(8,128)(2,1)S(1)} %copy-done), custom_call_target="tpu_custom_call" | custom-call | flops 1073741824 | bytes 1572864 | tf_op jit(solution)/shard_map/rows_kernel/pallas_call | solution.py:333
  22.8 0.0 copy-start.8
  22.8 33.0 %all_to_all.20 = f32[256,1,384]{2,1,0:T(1,128)S(1)} all-to-all(f32[256,1,384]{2,1,0:T(1,128)S(1)} %bitcast.10), channel_id=1, replica_groups=mesh['wide'=64,'lane'=4,'core'=2] {'wide','lane'}, dimensions={0} | all-to-all | bytes 786432 | tf_op jit(solution)/shard_map/all_to_all | solution.py:383
  55.8 0.0 copy-start.4
  55.8 1.6 %columns_kernel.1 = f32[768,128]{1,0:T(8,128)S(1)} custom-call(f32[768,128]{1,0:T(8,128)S(1)} %bitcast.8, f32[256,256]{1,0:T(8,128)S(1)} %get-tuple-element.13.source, bf16[2,256,512]{2,1,0:T(8,128)(2,1)S(1)} %copy-done, f32[2,256,128]{2,1,0:T(8,128)S(1)} %copy-done.10, bf16[2,256,640]{2,1,0:T(8,128)(2,1)S(1)} %copy-done.8, bf16[2,256,256]{2,1,0:T(8,128)(2,1)S(1)} %copy-done.9), custom_call_target="tpu_custom_call" | custom-call | flops 1073741824 | bytes 2752512 | tf_op jit(solution)/shard_map/columns_kernel/pallas_call | solution.py:333
  57.4 0.0 copy-start.1
  57.4 0.0 copy-start.2
  57.4 0.0 copy-start.3
  57.5 24.1 %all_to_all.21 = f32[256,1,384]{2,1,0:T(1,128)S(1)} all-to-all(f32[256,1,384]{2,1,0:T(1,128)S(1)} %bitcast.9), channel_id=1, replica_groups=mesh['wide'=64,'lane'=4,'core'=2] {'wide','lane'}, dimensions={0} | all-to-all | bytes 786432 | tf_op jit(solution)/shard_map/all_to_all | solution.py:383
  81.5 1.9 %rows_back_kernel.1 = f32[8,32,256]{2,1,0:T(8,128)S(1)} custom-call(s32[3]{0:T(128)S(1)} %pad_add_fusion.place, f32[768,128]{1,0:T(8,128)S(1)} %bitcast.7, bf16[512,256]{1,0:T(8,128)(2,1)S(1)} %get-tuple-element.14.places, f32[128,256]{1,0:T(8,128)S(1)} %get-tuple-element.15.beyond, bf16[2,256,512]{2,1,0:T(8,128)(2,1)S(1)} %copy-done, ...), custom_call_target="tpu_custom_call" | custom-call | flops 536870912 | bytes 2490368 | tf_op jit(solution)/shard_map/rows_back_kernel/pallas_call | solution.py:333
  83.4 0.0 copy-start.5
  83.5 0.0 copy-start.6
  83.5 16.4 %all_to_all.22.terms = f32[8,32,256]{2,1,0:T(8,128)S(1)} all-to-all(f32[8,32,256]{2,1,0:T(8,128)S(1)} %rows_back_kernel.1), channel_id=1, replica_groups=mesh['wide'=64,'lane'=4,'core'=2] {'lane','core'}, dimensions={0} | all-to-all | bytes 524288 | tf_op jit(solution)/shard_map/all_to_all | solution.py:390
  99.9 1.2 %finish_kernel.1 = (f32[2,32,256]{2,1,0:T(8,128)}, f32[2,32,256]{2,1,0:T(8,128)}) custom-call(s32[3]{0:T(128)S(1)} %pad_add_fusion.place, f32[8,32,256]{2,1,0:T(8,128)S(1)} %all_to_all.22.terms, f32[2,32,256]{2,1,0:T(8,128)S(1)} %copy-done.5, f32[2,32,256]{2,1,0:T(8,128)S(1)} %copy-done.6), custom_call_target="tpu_custom_call" | custom-call | bytes 524288 | tf_op jit(solution)/shard_map/finish_kernel/pallas_call | solution.py:333
  (17 shorter events, 0.0 us)
Async XLA Ops:
  0.6 20.7 %copy-start.12 = (bf16[2,256,128]{2,1,0:T(8,128)(2,1)S(1)}, bf16[2,256,128]{2,1,0:T(8,128)(2,1)}, u32[]{:S(2)}) copy-start(bf16[2,256,128]{2,1,0:T(8,128)(2,1)} %constant.33.clone.mix) | copy-start | bytes 393220
  2.3 10.3 %copy-start.13 = (s32[64,2]{0,1:T(2,128)S(1)}, s32[64,2]{0,1:T(2,128)}, u32[]{:S(2)}) copy-start(s32[64,2]{0,1:T(2,128)} %param.17) | copy-start | bytes 1540
  2.3 19.1 %copy-start = (bf16[2,256,512]{2,1,0:T(8,128)(2,1)S(1)}, bf16[2,256,512]{2,1,0:T(8,128)(2,1)}, u32[]{:S(2)}) copy-start(bf16[2,256,512]{2,1,0:T(8,128)(2,1)} %constant.35.clone.circles) | copy-start | bytes 1572868
  2.3 19.0 %all-to-all-start = ((f32[8,32,256]{2,1,0:T(8,128)}), f32[8,32,256]{2,1,0:T(8,128)S(1)}, u32[]{:S(2)}, u32[]{:S(2)}) async-start(f32[8,32,256]{2,1,0:T(8,128)} %deal_kernel.1), calls=%async_computation | async-start | bytes 524288 | tf_op jit(solution)/shard_map/all_to_all | solution.py:385
  12.6 0.8 copy-start.7
  12.6 8.7 %copy-start.11 = (f32[2,2,64,256]{3,2,1,0:T(8,128)S(1)}, f32[2,2,64,256]{3,2,1,0:T(8,128)}, u32[]{:S(2)}) copy-start(f32[2,2,64,256]{3,2,1,0:T(8,128)} %constant.34.clone.turn) | copy-start | bytes 786436
  21.3 34.5 %copy-start.9 = (bf16[2,256,256]{2,1,0:T(8,128)(2,1)S(1)}, bf16[2,256,256]{2,1,0:T(8,128)(2,1)}, u32[]{:S(2)}) copy-start(bf16[2,256,256]{2,1,0:T(8,128)(2,1)} %constant.38.clone.deal) | copy-start | bytes 786436
  21.3 34.4 %copy-start.10 = (f32[2,256,128]{2,1,0:T(8,128)S(1)}, f32[2,256,128]{2,1,0:T(8,128)}, u32[]{:S(2)}) copy-start(f32[2,256,128]{2,1,0:T(8,128)} %constant.36.clone.turn) | copy-start | bytes 786436
  22.8 33.0 %copy-start.8 = (bf16[2,256,640]{2,1,0:T(8,128)(2,1)S(1)}, bf16[2,256,640]{2,1,0:T(8,128)(2,1)}, u32[]{:S(2)}) copy-start(bf16[2,256,640]{2,1,0:T(8,128)(2,1)} %constant.37.clone.gather) | copy-start | bytes 1966084
  55.8 25.7 %copy-start.4 = (f32[2,2,32,256]{3,2,1,0:T(8,128)S(1)}, f32[2,2,32,256]{3,2,1,0:T(8,128)}, u32[]{:S(2)}) copy-start(f32[2,2,32,256]{3,2,1,0:T(8,128)} %constant.39.clone.main_turn) | copy-start | bytes 393220
  57.4 24.1 %copy-start.1 = (bf16[2,128,512]{2,1,0:T(8,128)(2,1)S(1)}, bf16[2,128,512]{2,1,0:T(8,128)(2,1)}, u32[]{:S(2)}) copy-start(bf16[2,128,512]{2,1,0:T(8,128)(2,1)} %constant.42.clone.zone_mix) | copy-start | bytes 786436
  57.4 24.1 %copy-start.2 = (bf16[2,256,256]{2,1,0:T(8,128)(2,1)S(1)}, bf16[2,256,256]{2,1,0:T(8,128)(2,1)}, u32[]{:S(2)}) copy-start(bf16[2,256,256]{2,1,0:T(8,128)(2,1)} %constant.41.clone.main_mix) | copy-start | bytes 786436
  57.4 24.1 %copy-start.3 = (f32[2,128,256]{2,1,0:T(8,128)S(1)}, f32[2,128,256]{2,1,0:T(8,128)}, u32[]{:S(2)}) copy-start(f32[2,128,256]{2,1,0:T(8,128)} %constant.40.clone.zone_turn) | copy-start | bytes 786436
  83.4 16.5 %copy-start.5 = (f32[2,32,256]{2,1,0:T(8,128)S(1)}, f32[2,32,256]{2,1,0:T(8,128)}, u32[]{:S(2)}) copy-start(f32[2,32,256]{2,1,0:T(8,128)} %eta.3) | copy-start | bytes 196612
  83.5 16.5 %copy-start.6 = (f32[2,32,256]{2,1,0:T(8,128)S(1)}, f32[2,32,256]{2,1,0:T(8,128)}, u32[]{:S(2)}) copy-start(f32[2,32,256]{2,1,0:T(8,128)} %phi.3) | copy-start | bytes 196612

commit v15 on v12

--- a/solution.py
+++ b/solution.py
@@ -210,10 +210,11 @@
     cosine = turn[0, core]
     sine = turn[1, core]
     parts = [[], []]
+    fields = [jnp.concatenate(tile, 0) for tile in tiles]
+    slopes = dot3((mix[0, :128], mix[1, :128]), split(jnp.concatenate(fields[:4], 1)))
+    lift = dot3((mix[0, 128:], mix[1, 128:]), split(fields[4]))
     for f in range(5):
-        rows = split(jnp.concatenate(tiles[f], 0))
-        kind = slice(0, 128) if f < 4 else slice(128, 256)
-        both = dot3((mix[0, kind], mix[1, kind]), rows)
+        both = slopes[:, 256 * f : 256 * f + 256] if f < 4 else lift
         first = both[:64]
         second = both[64:]
         turned = (first * cosine + second * sine).reshape(4, 2, 8, 256)

time: 102 us -> 102 us (level)
  no operation moved by 1% of the time
where the time goes in v15:
time: 102 us; the launch traced here: 101 us
  blocking collectives  73.5 us (72%)
  starting transfers between devices  10.3 us (10%)
  Pallas kernels  9.48 us (9%)
  waiting for transfers between devices  6.32 us (6%)
    all_to_all x2, blocking collectives, turn(): return swap(words.reshape(256, 1, 384), ('wide', 'lane')).reshape(768, 128)  57.1 us
    all_to_all x1, blocking collectives, local(): terms = swap(stage_rows_back(place, rows, places, beyond), ('lane', 'core'))  16.4 us
    all_to_all x1, starting transfers between devices, local(): modes = swap(stage_deal(eta_modes, phi_modes), ('lane', 'core'))  10.3 us
    pallas_call x5, Pallas kernels, call(): pl.pallas_call(kernel, out_shape=[jax.ShapeDtypeStruct(s, t) for s, t in...  8.23 us
    all_to_all x1, waiting for transfers between devices, local(): modes = swap(stage_deal(eta_modes, phi_modes), ('lane', 'core'))  6.32 us
  transfers between devices with their start and end apart: 1, of which 1 were waited for; matrix products, arithmetic and copies ran while one was open for 0% of the time, Pallas kernels for 2%

profile of v15, /device:TPU:1, one launch (start us, length us, event | category | flops | bytes accessed | tf_op | source)
XLA Modules:
  0.0 101.2 jit_solution(12409250033382834562)
XLA Ops:
  0.6 0.0 copy-start.12
  0.6 1.6 %deal_kernel.1 = f32[8,32,256]{2,1,0:T(8,128)} custom-call(f32[2,32,256]{2,1,0:T(8,128)} %eta.3, f32[2,32,256]{2,1,0:T(8,128)} %phi.3), custom_call_target="tpu_custom_call" | custom-call | flops 8589934592 | bytes 393216 | tf_op jit(solution)/shard_map/deal_kernel/pallas_call | solution.py:337
  2.3 10.3 %all-to-all-start = ((f32[8,32,256]{2,1,0:T(8,128)}), f32[8,32,256]{2,1,0:T(8,128)S(1)}, u32[]{:S(2)}, u32[]{:S(2)}) async-start(f32[8,32,256]{2,1,0:T(8,128)} %deal_kernel.1), calls=%async_computation | async-start | bytes 524288 | tf_op jit(solution)/shard_map/all_to_all | solution.py:399
  12.6 0.1 copy.17.offsets
  12.7 0.1 pad_add_fusion.place
  12.8 0.6 copy-done.7
  13.3 1.6 %source_kernel.1 = (f32[256,256]{1,0:T(8,128)S(1)}, bf16[512,256]{1,0:T(8,128)(2,1)S(1)}, f32[128,256]{1,0:T(8,128)S(1)}) custom-call(s32[3]{0:T(128)S(1)} %pad_add_fusion.place, s32[64,2]{1,0:T(8,128)S(1)} %copy.17.offsets, f32[64,128]{1,0:T(8,128)S(1)} %copy-done.7), custom_call_target="tpu_custom_call" | custom-call | flops 67108864 | bytes 950272 | tf_op jit(solution)/shard_map/source_kernel/pallas_call | solution.py:337
  15.0 6.3 %all-to-all-done.modes = f32[8,32,256]{2,1,0:T(8,128)S(1)} async-done(((f32[8,32,256]{2,1,0:T(8,128)}), f32[8,32,256]{2,1,0:T(8,128)S(1)}, u32[]{:S(2)}, u32[]{:S(2)}) %all-to-all-start) | async-done | bytes 262176 | tf_op jit(solution)/shard_map/all_to_all | solution.py:399
  21.3 0.0 copy-start.9
  21.3 0.0 copy-start.10
  21.4 1.4 %rows_kernel.1 = f32[768,128]{1,0:T(8,128)S(1)} custom-call(s32[3]{0:T(128)S(1)} %pad_add_fusion.place, f32[8,32,256]{2,1,0:T(8,128)S(1)} %all-to-all-done.modes, bf16[2,256,128]{2,1,0:T(8,128)(2,1)S(1)} %copy-done.12, f32[2,2,64,256]{3,2,1,0:T(8,128)S(1)} %copy-done.11, bf16[2,256,512]{2,1,0:T(8,128)(2,1)S(1)} %copy-done), custom_call_target="tpu_custom_call" | custom-call | flops 1073741824 | bytes 1572864 | tf_op jit(solution)/shard_map/rows_kernel/pallas_call | solution.py:337
  22.8 0.0 copy-start.8
  22.8 33.0 %all_to_all.20 = f32[256,1,384]{2,1,0:T(1,128)S(1)} all-to-all(f32[256,1,384]{2,1,0:T(1,128)S(1)} %bitcast.10), channel_id=1, replica_groups=mesh['wide'=64,'lane'=4,'core'=2] {'wide','lane'}, dimensions={0} | all-to-all | bytes 786432 | tf_op jit(solution)/shard_map/all_to_all | solution.py:397
  55.8 0.0 copy-start.4
  55.8 1.6 %columns_kernel.1 = f32[768,128]{1,0:T(8,128)S(1)} custom-call(f32[768,128]{1,0:T(8,128)S(1)} %bitcast.8, f32[256,256]{1,0:T(8,128)S(1)} %get-tuple-element.13.source, bf16[2,256,512]{2,1,0:T(8,128)(2,1)S(1)} %copy-done, f32[2,256,128]{2,1,0:T(8,128)S(1)} %copy-done.10, bf16[2,256,640]{2,1,0:T(8,128)(2,1)S(1)} %copy-done.8, bf16[2,256,256]{2,1,0:T(8,128)(2,1)S(1)} %copy-done.9), custom_call_target="tpu_custom_call" | custom-call | flops 1073741824 | bytes 2752512 | tf_op jit(solution)/shard_map/columns_kernel/pallas_call | solution.py:337
  57.4 0.0 copy-start.1
  57.4 0.0 copy-start.2
  57.4 0.0 copy-start.3
  57.5 24.1 %all_to_all.21 = f32[256,1,384]{2,1,0:T(1,128)S(1)} all-to-all(f32[256,1,384]{2,1,0:T(1,128)S(1)} %bitcast.9), channel_id=1, replica_groups=mesh['wide'=64,'lane'=4,'core'=2] {'wide','lane'}, dimensions={0} | all-to-all | bytes 786432 | tf_op jit(solution)/shard_map/all_to_all | solution.py:397
  81.6 1.9 %rows_back_kernel.1 = f32[8,32,256]{2,1,0:T(8,128)S(1)} custom-call(s32[3]{0:T(128)S(1)} %pad_add_fusion.place, f32[768,128]{1,0:T(8,128)S(1)} %bitcast.7, bf16[512,256]{1,0:T(8,128)(2,1)S(1)} %get-tuple-element.14.places, f32[128,256]{1,0:T(8,128)S(1)} %get-tuple-element.15.beyond, bf16[2,256,512]{2,1,0:T(8,128)(2,1)S(1)} %copy-done, ...), custom_call_target="tpu_custom_call" | custom-call | flops 536870912 | bytes 2490368 | tf_op jit(solution)/shard_map/rows_back_kernel/pallas_call | solution.py:337
  83.5 0.0 copy-start.5
  83.5 0.0 copy-start.6
  83.5 16.4 %all_to_all.22.terms = f32[8,32,256]{2,1,0:T(8,128)S(1)} all-to-all(f32[8,32,256]{2,1,0:T(8,128)S(1)} %rows_back_kernel.1), channel_id=1, replica_groups=mesh['wide'=64,'lane'=4,'core'=2] {'lane','core'}, dimensions={0} | all-to-all | bytes 524288 | tf_op jit(solution)/shard_map/all_to_all | solution.py:404
  99.9 1.2 %finish_kernel.1 = (f32[2,32,256]{2,1,0:T(8,128)}, f32[2,32,256]{2,1,0:T(8,128)}) custom-call(s32[3]{0:T(128)S(1)} %pad_add_fusion.place, f32[8,32,256]{2,1,0:T(8,128)S(1)} %all_to_all.22.terms, f32[2,32,256]{2,1,0:T(8,128)S(1)} %copy-done.5, f32[2,32,256]{2,1,0:T(8,128)S(1)} %copy-done.6), custom_call_target="tpu_custom_call" | custom-call | flops 524288 | bytes 1048576 | tf_op jit(solution)/shard_map/finish_kernel/pallas_call | solution.py:380
  (17 shorter events, 0.0 us)
Async XLA Ops:
  0.6 20.7 %copy-start.12 = (bf16[2,256,128]{2,1,0:T(8,128)(2,1)S(1)}, bf16[2,256,128]{2,1,0:T(8,128)(2,1)}, u32[]{:S(2)}) copy-start(bf16[2,256,128]{2,1,0:T(8,128)(2,1)} %constant.33.clone.mix) | copy-start | bytes 393220
  2.3 10.3 %copy-start.13 = (s32[64,2]{0,1:T(2,128)S(1)}, s32[64,2]{0,1:T(2,128)}, u32[]{:S(2)}) copy-start(s32[64,2]{0,1:T(2,128)} %param.17) | copy-start | bytes 1540
  2.3 19.1 %copy-start = (bf16[2,256,512]{2,1,0:T(8,128)(2,1)S(1)}, bf16[2,256,512]{2,1,0:T(8,128)(2,1)}, u32[]{:S(2)}) copy-start(bf16[2,256,512]{2,1,0:T(8,128)(2,1)} %constant.35.clone.circles) | copy-start | bytes 1572868
  2.3 19.0 %all-to-all-start = ((f32[8,32,256]{2,1,0:T(8,128)}), f32[8,32,256]{2,1,0:T(8,128)S(1)}, u32[]{:S(2)}, u32[]{:S(2)}) async-start(f32[8,32,256]{2,1,0:T(8,128)} %deal_kernel.1), calls=%async_computation | async-start | bytes 524288 | tf_op jit(solution)/shard_map/all_to_all | solution.py:399
  12.6 0.8 copy-start.7
  12.6 8.7 %copy-start.11 = (f32[2,2,64,256]{3,2,1,0:T(8,128)S(1)}, f32[2,2,64,256]{3,2,1,0:T(8,128)}, u32[]{:S(2)}) copy-start(f32[2,2,64,256]{3,2,1,0:T(8,128)} %constant.34.clone.turn) | copy-start | bytes 786436
  21.3 34.5 %copy-start.9 = (bf16[2,256,256]{2,1,0:T(8,128)(2,1)S(1)}, bf16[2,256,256]{2,1,0:T(8,128)(2,1)}, u32[]{:S(2)}) copy-start(bf16[2,256,256]{2,1,0:T(8,128)(2,1)} %constant.38.clone.deal) | copy-start | bytes 786436
  21.3 34.4 %copy-start.10 = (f32[2,256,128]{2,1,0:T(8,128)S(1)}, f32[2,256,128]{2,1,0:T(8,128)}, u32[]{:S(2)}) copy-start(f32[2,256,128]{2,1,0:T(8,128)} %constant.36.clone.turn) | copy-start | bytes 786436
  22.8 33.0 %copy-start.8 = (bf16[2,256,640]{2,1,0:T(8,128)(2,1)S(1)}, bf16[2,256,640]{2,1,0:T(8,128)(2,1)}, u32[]{:S(2)}) copy-start(bf16[2,256,640]{2,1,0:T(8,128)(2,1)} %constant.37.clone.gather) | copy-start | bytes 1966084
  55.8 25.8 %copy-start.4 = (f32[2,2,32,256]{3,2,1,0:T(8,128)S(1)}, f32[2,2,32,256]{3,2,1,0:T(8,128)}, u32[]{:S(2)}) copy-start(f32[2,2,32,256]{3,2,1,0:T(8,128)} %constant.39.clone.main_turn) | copy-start | bytes 393220
  57.4 24.1 %copy-start.1 = (bf16[2,128,512]{2,1,0:T(8,128)(2,1)S(1)}, bf16[2,128,512]{2,1,0:T(8,128)(2,1)}, u32[]{:S(2)}) copy-start(bf16[2,128,512]{2,1,0:T(8,128)(2,1)} %constant.42.clone.zone_mix) | copy-start | bytes 786436
  57.4 24.1 %copy-start.2 = (bf16[2,256,256]{2,1,0:T(8,128)(2,1)S(1)}, bf16[2,256,256]{2,1,0:T(8,128)(2,1)}, u32[]{:S(2)}) copy-start(bf16[2,256,256]{2,1,0:T(8,128)(2,1)} %constant.41.clone.main_mix) | copy-start | bytes 786436
  57.4 24.1 %copy-start.3 = (f32[2,128,256]{2,1,0:T(8,128)S(1)}, f32[2,128,256]{2,1,0:T(8,128)}, u32[]{:S(2)}) copy-start(f32[2,128,256]{2,1,0:T(8,128)} %constant.40.clone.zone_turn) | copy-start | bytes 786436
  83.5 16.4 %copy-start.5 = (f32[2,32,256]{2,1,0:T(8,128)S(1)}, f32[2,32,256]{2,1,0:T(8,128)}, u32[]{:S(2)}) copy-start(f32[2,32,256]{2,1,0:T(8,128)} %eta.3) | copy-start | bytes 196612
  83.5 16.4 %copy-start.6 = (f32[2,32,256]{2,1,0:T(8,128)S(1)}, f32[2,32,256]{2,1,0:T(8,128)}, u32[]{:S(2)}) copy-start(f32[2,32,256]{2,1,0:T(8,128)} %phi.3) | copy-start | bytes 196612
